TPU v7x, 256 devices: a whole 4x4x8 slice. The times are simulated.
256 devices in a mesh: wide: 32 (over z, y_lo, core), narrow: 8 (over y_hi, x).
Axes of the slice: x: 4, y: 4 (y_hi: 2, y_lo: 2; y = y_hi * 2 + y_lo), z: 8, core: 2. Of those that a mesh axis runs over, the one named last changes fastest.
Arguments:
- video: bfloat16 [128, 16, 64, 1024], P('wide', 'narrow'), may hold values from -15 to 15
- w_qkv: bfloat16 [1024, 3072], replicated, may hold values from -0.1875 to 0.1875
- w_out: bfloat16 [1024, 1024], replicated, may hold values from -0.1875 to 0.1875
- w_proj: bfloat16 [1024, 768], replicated, may hold values from -0.1875 to 0.1875
- captions: bfloat16 [4096, 768], P(('wide', 'narrow')), may hold values from -330 to 330
- positive: int32 [128], P('wide'), may hold values from 0 to 4095
Outputs:
- clip_grad: float32 [128, 768], P('wide')
- caption_grad: float32 [4096, 768], P(('wide', 'narrow'))
All inputs are finite; a program needn't handle non-finite values.
Results may differ from a plain program's by a relative error of at most 0.0085.
Values may be sent and summed in bfloat16 or wider, within the bound.
No kernel may reach another device: no remote copies, remote signals or barrier semaphores. Data moves between devices by JAX's collectives and lax.ppermute only.
A program may use at most 64 MiB of HBM per device.

v0:
```python
import jax
import jax.numpy as jnp
from jax import lax
from jax.sharding import PartitionSpec as P

HEADS = 16
FRAMES = 16
SPATIAL = 64


TEMP = 10.0
BIAS = -2.0
EPS = 1e-06


def passed_along(value, axis, steps):
    count = lax.axis_size(axis)
    pairs = [(source, (source + steps) % count) for source in range(count)]
    return lax.ppermute(value, axis, pairs)


def normalize(values):
    length = jnp.sqrt(jnp.sum(values * values, axis=-1, keepdims=True) + EPS)
    return (values / length, length)


def pair_terms(unit, positive, block_unit, global_ids):
    logits = TEMP * jnp.dot(unit, block_unit.T, precision=lax.Precision.HIGHEST) + BIAS
    sign = jnp.where(global_ids[None, :] == positive[:, None], 1.0, -1.0).astype(jnp.float32)
    weight = -sign * jax.nn.sigmoid(-sign * logits)
    grad_unit = TEMP * jnp.dot(weight, block_unit, precision=lax.Precision.HIGHEST)
    grad_block = TEMP * jnp.dot(weight.T, unit, precision=lax.Precision.HIGHEST)
    return (grad_unit, grad_block)


def per_device(video, w_qkv, w_out, w_proj, captions, positive):
    width = video.shape[3]
    head_size = width // HEADS
    scale = 1.0 / jnp.sqrt(jnp.float32(head_size))
    tokens = lax.all_to_all(video, "narrow", split_axis=2, concat_axis=1, tiled=True)
    items, frames, spots, _ = tokens.shape
    rows = tokens.reshape(items * frames * spots, width)
    qkv = jnp.dot(rows, w_qkv, preferred_element_type=jnp.float32).astype(jnp.bfloat16)
    qkv = qkv.reshape(items, frames, spots, 3, HEADS, head_size)
    scores = (
        jnp.einsum(
            "cfshd,cgshd->cshfg",
            qkv[:, :, :, 0],
            qkv[:, :, :, 1],
            preferred_element_type=jnp.float32,
        )
        * scale
    )
    top = jnp.max(scores, axis=-1, keepdims=True)
    expo = jnp.exp(scores - top)
    probs = (expo / jnp.sum(expo, axis=-1, keepdims=True)).astype(jnp.bfloat16)
    mixed = jnp.einsum(
        "cshfg,cgshd->cfshd", probs, qkv[:, :, :, 2], preferred_element_type=jnp.float32
    )
    mixed = mixed.astype(jnp.bfloat16).reshape(items * frames * spots, width)
    layer_out = rows.astype(jnp.float32) + jnp.dot(mixed, w_out, preferred_element_type=jnp.float32)
    partial_sums = jnp.sum(layer_out.reshape(items, frames * spots, width), axis=1)
    pooled = lax.psum(partial_sums, "narrow") / (FRAMES * SPATIAL)
    embed = jnp.dot(pooled, w_proj.astype(jnp.float32), precision=lax.Precision.HIGHEST)
    unit, length = normalize(embed)
    cap_unit, cap_len = normalize(captions.astype(jnp.float32))
    cap_rows = captions.shape[0]
    cycle_size = lax.axis_size("wide")
    column_size = lax.axis_size("narrow")
    rank_wide = lax.axis_index("wide")
    rank_narrow = lax.axis_index("narrow")
    offsets = jnp.arange(cap_rows, dtype=jnp.int32)

    def turn(step, state):
        held, totals, grad_unit = state
        anchor = (rank_wide - step) % cycle_size
        global_ids = (anchor * column_size + rank_narrow) * cap_rows + offsets
        part_unit, part_block = pair_terms(unit, positive, held, global_ids)
        held, totals = passed_along((held, totals + part_block), "wide", 1)
        return (held, totals, grad_unit + part_unit)

    start_state = (cap_unit, jnp.zeros_like(cap_unit), jnp.zeros_like(unit))
    _, grad_cap, grad_unit = lax.fori_loop(0, cycle_size, turn, start_state)
    grad_unit = lax.psum(grad_unit, "narrow")
    clip_grad = (grad_unit - unit * jnp.sum(unit * grad_unit, axis=-1, keepdims=True)) / length
    caption_grad = (
        grad_cap - cap_unit * jnp.sum(cap_unit * grad_cap, axis=-1, keepdims=True)
    ) / cap_len
    return (clip_grad, caption_grad)


def solution(mesh):
    in_specs = (
        P("wide", "narrow", None, None),
        P(),
        P(),
        P(),
        P(("wide", "narrow"), None),
        P("wide"),
    )
    out_specs = (P("wide", None), P(("wide", "narrow"), None))
    return jax.shard_map(
        per_device, mesh=mesh, in_specs=in_specs, out_specs=out_specs, check_vma=False
    )
```

profile of v0, /device:TPU:128, one launch (start us, length us, event | category | flops | bytes accessed | tf_op | source)
XLA Modules:
  0.0 361.0 jit_solution(5692398457457596926)
XLA Ops:
  3.8 6.9 %all-to-all-start = ((bf16[4,2,64,1024]{3,0,1,2:T(4,128)(2,1)}), bf16[4,2,64,1024]{3,0,1,2:T(4,128)(2,1)S(1)}, u32[]{:S(2)}, u32[]{:S(2)}) async-start(bf16[4,2,64,1024]{3,0,1,2:T(4,128)(2,1)} %copy.26), calls=%async_computation | async-start | bytes 2097152 | tf_op jit(solution)/shard_map/all_to_all | solution.py:40
  11.0 17.0 %all-to-all-done = bf16[4,2,64,1024]{3,0,1,2:T(4,128)(2,1)S(1)} async-done(((bf16[4,2,64,1024]{3,0,1,2:T(4,128)(2,1)}), bf16[4,2,64,1024]{3,0,1,2:T(4,128)(2,1)S(1)}, u32[]{:S(2)}, u32[]{:S(2)}) %all-to-all-start) | async-done | bytes 1048608 | tf_op jit(solution)/shard_map/all_to_all | solution.py:40
  29.5 7.6 %convolution_convert_fusion = bf16[512,3072]{1,0:T(8,128)(2,1)} fusion(bf16[512,1024]{1,0:T(8,128)(2,1)S(1)} %bitcast.45, bf16[1024,3072]{1,0:T(8,128)(2,1)} %param.9), kind=kOutput, calls=%fused_computation.15 | convolution fusion | flops 3222798336 | bytes 10485760 | tf_op jit(solution)/shard_map/dot_general | solution.py:43
  37.1 8.6 %reshape.41 = bf16[4,16,8,3,16,64]{5,4,3,2,1,0:T(8,128)(2,1)} reshape(bf16[512,3072]{1,0:T(8,128)(2,1)} %convolution_convert_fusion) | data formatting | bytes 6291456 | tf_op jit(solution)/shard_map/reshape | solution.py:44
  45.7 5.6 %fusion.25 = (bf16[4,16,8,1,16,64]{5,4,3,2,1,0:T(8,128)(2,1)S(1)}, bf16[4,16,8,1,16,64]{5,4,3,2,1,0:T(8,128)(2,1)S(1)}, bf16[4,16,8,1,16,64]{5,4,3,2,1,0:T(8,128)(2,1)S(1)}) fusion(bf16[4,16,8,3,16,64]{5,4,3,2,1,0:T(8,128)(2,1)} %reshape.41), kind=kLoop, calls=%fused_computation.46 | loop fusion | bytes 6291456 | tf_op jit(solution)/shard_map/slice | solution.py:58
  53.8 17.7 %fusion.26 = (f32[4,8,16,16]{3,2,1,0:T(8,128)S(1)}, f32[4,8,16,16,16]{3,4,2,1,0:T(8,128)S(1)}) fusion(f32[4,8,16,16,16]{3,4,2,1,0:T(8,128)S(1)} %fusion.16), kind=kOutput, calls=%fused_computation.47 | output fusion | flops 524303 | bytes 1081344 | tf_op jit(solution)/shard_map/sub | solution.py:55
  81.0 38.0 %psum.14 = f32[4,1024]{1,0:T(4,128)S(1)} all-reduce(f32[4,1024]{1,0:T(4,128)S(1)} %bitcast_reduce_fusion), channel_id=1, replica_groups=mesh['wide'=32,'narrow'=8] {'narrow'}, use_global_device_ids=true, to_apply=%region_4.0 | all-reduce | flops 4096 | bytes 32768 | tf_op jit(solution)/shard_map/psum | solution.py:63
  121.3 201.3 %while.20 = (s32[]{:T(128)}, f32[16,768]{1,0:T(8,128)S(1)}, f32[16,768]{1,0:T(8,128)S(1)}, f32[4,768]{1,0:T(4,128)S(1)}, s32[]{:T(128)}, /*index=5*/s32[]{:T(128...) while((s32[]{:T(128)}, f32[16,768]{1,0:T(8,128)S(1)}, ...), condition=%wide.region_7.8_spmd.clone, body=%wide.region_6.7_spmd.clone.sunk | while | flops 1803938 | bytes 738576 | solution.py:83
  128.5 5.4 %collective-permute-done.1 = f32[16,768]{1,0:T(8,128)S(1)} collective-permute-done((f32[16,768]{1,0:T(8,128)S(1)}, f32[16,768]{1,0:T(8,128)S(1)}, u32[]{:S(2)}, u32[]{:S(2)}) %collective-permute-start.1) | collective-permute-done | bytes 49184 | tf_op jit(solution)/shard_map/while/body/eval_jaxpr/ppermute | solution.py:19
  134.8 5.4 %collective-permute-done.1 = f32[16,768]{1,0:T(8,128)S(1)} collective-permute-done((f32[16,768]{1,0:T(8,128)S(1)}, f32[16,768]{1,0:T(8,128)S(1)}, u32[]{:S(2)}, u32[]{:S(2)}) %collective-permute-start.1) | collective-permute-done | bytes 49184 | tf_op jit(solution)/shard_map/while/body/eval_jaxpr/ppermute | solution.py:19
  141.1 5.4 %collective-permute-done.1 = f32[16,768]{1,0:T(8,128)S(1)} collective-permute-done((f32[16,768]{1,0:T(8,128)S(1)}, f32[16,768]{1,0:T(8,128)S(1)}, u32[]{:S(2)}, u32[]{:S(2)}) %collective-permute-start.1) | collective-permute-done | bytes 49184 | tf_op jit(solution)/shard_map/while/body/eval_jaxpr/ppermute | solution.py:19
  147.4 5.4 %collective-permute-done.1 = f32[16,768]{1,0:T(8,128)S(1)} collective-permute-done((f32[16,768]{1,0:T(8,128)S(1)}, f32[16,768]{1,0:T(8,128)S(1)}, u32[]{:S(2)}, u32[]{:S(2)}) %collective-permute-start.1) | collective-permute-done | bytes 49184 | tf_op jit(solution)/shard_map/while/body/eval_jaxpr/ppermute | solution.py:19
  153.6 5.4 %collective-permute-done.1 = f32[16,768]{1,0:T(8,128)S(1)} collective-permute-done((f32[16,768]{1,0:T(8,128)S(1)}, f32[16,768]{1,0:T(8,128)S(1)}, u32[]{:S(2)}, u32[]{:S(2)}) %collective-permute-start.1) | collective-permute-done | bytes 49184 | tf_op jit(solution)/shard_map/while/body/eval_jaxpr/ppermute | solution.py:19
  159.9 5.4 %collective-permute-done.1 = f32[16,768]{1,0:T(8,128)S(1)} collective-permute-done((f32[16,768]{1,0:T(8,128)S(1)}, f32[16,768]{1,0:T(8,128)S(1)}, u32[]{:S(2)}, u32[]{:S(2)}) %collective-permute-start.1) | collective-permute-done | bytes 49184 | tf_op jit(solution)/shard_map/while/body/eval_jaxpr/ppermute | solution.py:19
  166.2 5.4 %collective-permute-done.1 = f32[16,768]{1,0:T(8,128)S(1)} collective-permute-done((f32[16,768]{1,0:T(8,128)S(1)}, f32[16,768]{1,0:T(8,128)S(1)}, u32[]{:S(2)}, u32[]{:S(2)}) %collective-permute-start.1) | collective-permute-done | bytes 49184 | tf_op jit(solution)/shard_map/while/body/eval_jaxpr/ppermute | solution.py:19
  172.5 5.4 %collective-permute-done.1 = f32[16,768]{1,0:T(8,128)S(1)} collective-permute-done((f32[16,768]{1,0:T(8,128)S(1)}, f32[16,768]{1,0:T(8,128)S(1)}, u32[]{:S(2)}, u32[]{:S(2)}) %collective-permute-start.1) | collective-permute-done | bytes 49184 | tf_op jit(solution)/shard_map/while/body/eval_jaxpr/ppermute | solution.py:19
  178.8 5.4 %collective-permute-done.1 = f32[16,768]{1,0:T(8,128)S(1)} collective-permute-done((f32[16,768]{1,0:T(8,128)S(1)}, f32[16,768]{1,0:T(8,128)S(1)}, u32[]{:S(2)}, u32[]{:S(2)}) %collective-permute-start.1) | collective-permute-done | bytes 49184 | tf_op jit(solution)/shard_map/while/body/eval_jaxpr/ppermute | solution.py:19
  185.1 5.4 %collective-permute-done.1 = f32[16,768]{1,0:T(8,128)S(1)} collective-permute-done((f32[16,768]{1,0:T(8,128)S(1)}, f32[16,768]{1,0:T(8,128)S(1)}, u32[]{:S(2)}, u32[]{:S(2)}) %collective-permute-start.1) | collective-permute-done | bytes 49184 | tf_op jit(solution)/shard_map/while/body/eval_jaxpr/ppermute | solution.py:19
  191.4 5.4 %collective-permute-done.1 = f32[16,768]{1,0:T(8,128)S(1)} collective-permute-done((f32[16,768]{1,0:T(8,128)S(1)}, f32[16,768]{1,0:T(8,128)S(1)}, u32[]{:S(2)}, u32[]{:S(2)}) %collective-permute-start.1) | collective-permute-done | bytes 49184 | tf_op jit(solution)/shard_map/while/body/eval_jaxpr/ppermute | solution.py:19
  197.7 5.4 %collective-permute-done.1 = f32[16,768]{1,0:T(8,128)S(1)} collective-permute-done((f32[16,768]{1,0:T(8,128)S(1)}, f32[16,768]{1,0:T(8,128)S(1)}, u32[]{:S(2)}, u32[]{:S(2)}) %collective-permute-start.1) | collective-permute-done | bytes 49184 | tf_op jit(solution)/shard_map/while/body/eval_jaxpr/ppermute | solution.py:19
  204.0 5.4 %collective-permute-done.1 = f32[16,768]{1,0:T(8,128)S(1)} collective-permute-done((f32[16,768]{1,0:T(8,128)S(1)}, f32[16,768]{1,0:T(8,128)S(1)}, u32[]{:S(2)}, u32[]{:S(2)}) %collective-permute-start.1) | collective-permute-done | bytes 49184 | tf_op jit(solution)/shard_map/while/body/eval_jaxpr/ppermute | solution.py:19
  210.2 5.4 %collective-permute-done.1 = f32[16,768]{1,0:T(8,128)S(1)} collective-permute-done((f32[16,768]{1,0:T(8,128)S(1)}, f32[16,768]{1,0:T(8,128)S(1)}, u32[]{:S(2)}, u32[]{:S(2)}) %collective-permute-start.1) | collective-permute-done | bytes 49184 | tf_op jit(solution)/shard_map/while/body/eval_jaxpr/ppermute | solution.py:19
  216.5 5.4 %collective-permute-done.1 = f32[16,768]{1,0:T(8,128)S(1)} collective-permute-done((f32[16,768]{1,0:T(8,128)S(1)}, f32[16,768]{1,0:T(8,128)S(1)}, u32[]{:S(2)}, u32[]{:S(2)}) %collective-permute-start.1) | collective-permute-done | bytes 49184 | tf_op jit(solution)/shard_map/while/body/eval_jaxpr/ppermute | solution.py:19
  222.8 5.4 %collective-permute-done.1 = f32[16,768]{1,0:T(8,128)S(1)} collective-permute-done((f32[16,768]{1,0:T(8,128)S(1)}, f32[16,768]{1,0:T(8,128)S(1)}, u32[]{:S(2)}, u32[]{:S(2)}) %collective-permute-start.1) | collective-permute-done | bytes 49184 | tf_op jit(solution)/shard_map/while/body/eval_jaxpr/ppermute | solution.py:19
  229.1 5.4 %collective-permute-done.1 = f32[16,768]{1,0:T(8,128)S(1)} collective-permute-done((f32[16,768]{1,0:T(8,128)S(1)}, f32[16,768]{1,0:T(8,128)S(1)}, u32[]{:S(2)}, u32[]{:S(2)}) %collective-permute-start.1) | collective-permute-done | bytes 49184 | tf_op jit(solution)/shard_map/while/body/eval_jaxpr/ppermute | solution.py:19
  235.4 5.4 %collective-permute-done.1 = f32[16,768]{1,0:T(8,128)S(1)} collective-permute-done((f32[16,768]{1,0:T(8,128)S(1)}, f32[16,768]{1,0:T(8,128)S(1)}, u32[]{:S(2)}, u32[]{:S(2)}) %collective-permute-start.1) | collective-permute-done | bytes 49184 | tf_op jit(solution)/shard_map/while/body/eval_jaxpr/ppermute | solution.py:19
  241.7 5.4 %collective-permute-done.1 = f32[16,768]{1,0:T(8,128)S(1)} collective-permute-done((f32[16,768]{1,0:T(8,128)S(1)}, f32[16,768]{1,0:T(8,128)S(1)}, u32[]{:S(2)}, u32[]{:S(2)}) %collective-permute-start.1) | collective-permute-done | bytes 49184 | tf_op jit(solution)/shard_map/while/body/eval_jaxpr/ppermute | solution.py:19
  248.0 5.4 %collective-permute-done.1 = f32[16,768]{1,0:T(8,128)S(1)} collective-permute-done((f32[16,768]{1,0:T(8,128)S(1)}, f32[16,768]{1,0:T(8,128)S(1)}, u32[]{:S(2)}, u32[]{:S(2)}) %collective-permute-start.1) | collective-permute-done | bytes 49184 | tf_op jit(solution)/shard_map/while/body/eval_jaxpr/ppermute | solution.py:19
  254.3 5.4 %collective-permute-done.1 = f32[16,768]{1,0:T(8,128)S(1)} collective-permute-done((f32[16,768]{1,0:T(8,128)S(1)}, f32[16,768]{1,0:T(8,128)S(1)}, u32[]{:S(2)}, u32[]{:S(2)}) %collective-permute-start.1) | collective-permute-done | bytes 49184 | tf_op jit(solution)/shard_map/while/body/eval_jaxpr/ppermute | solution.py:19
  260.6 5.4 %collective-permute-done.1 = f32[16,768]{1,0:T(8,128)S(1)} collective-permute-done((f32[16,768]{1,0:T(8,128)S(1)}, f32[16,768]{1,0:T(8,128)S(1)}, u32[]{:S(2)}, u32[]{:S(2)}) %collective-permute-start.1) | collective-permute-done | bytes 49184 | tf_op jit(solution)/shard_map/while/body/eval_jaxpr/ppermute | solution.py:19
  273.1 5.4 %collective-permute-done.1 = f32[16,768]{1,0:T(8,128)S(1)} collective-permute-done((f32[16,768]{1,0:T(8,128)S(1)}, f32[16,768]{1,0:T(8,128)S(1)}, u32[]{:S(2)}, u32[]{:S(2)}) %collective-permute-start.1) | collective-permute-done | bytes 49184 | tf_op jit(solution)/shard_map/while/body/eval_jaxpr/ppermute | solution.py:19
  323.5 36.7 %psum.15 = f32[4,768]{1,0:T(4,128)S(1)} all-reduce(f32[4,768]{1,0:T(4,128)S(1)} %get-tuple-element.224), channel_id=1, replica_groups=mesh['wide'=32,'narrow'=8] {'narrow'}, use_global_device_ids=true, to_apply=%region_8.9 | all-reduce | flops 3072 | bytes 24576 | tf_op jit(solution)/shard_map/psum | solution.py:84
  (292 shorter events, 94.7 us)
Async XLA Ops:
  3.8 24.1 %all-to-all-start = ((bf16[4,2,64,1024]{3,0,1,2:T(4,128)(2,1)}), bf16[4,2,64,1024]{3,0,1,2:T(4,128)(2,1)S(1)}, u32[]{:S(2)}, u32[]{:S(2)}) async-start(bf16[4,2,64,1024]{3,0,1,2:T(4,128)(2,1)} %copy.26), calls=%async_computation | async-start | bytes 2097152 | tf_op jit(solution)/shard_map/all_to_all | solution.py:40
  121.3 6.3 %collective-permute-start = (f32[16,768]{1,0:T(8,128)S(1)}, f32[16,768]{1,0:T(8,128)S(1)}, u32[]{:S(2)}, u32[]{:S(2)}) collective-permute-start(f32[16,768]{1,0:T(8,128)S(1)} %copy.50), channel_id=1, source_target_pairs={{0,8},{8,16},{16,24},{24,32},{32,40},{40,48},{48,56},{56,64},{64,7... | collective-permute-start | bytes 147464 | tf_op jit(solution)/shard_map/while/body/eval_jaxpr/ppermute | solution.py:19
  127.6 6.3 %collective-permute-start = (f32[16,768]{1,0:T(8,128)S(1)}, f32[16,768]{1,0:T(8,128)S(1)}, u32[]{:S(2)}, u32[]{:S(2)}) collective-permute-start(f32[16,768]{1,0:T(8,128)S(1)} %copy.50), channel_id=1, source_target_pairs={{0,8},{8,16},{16,24},{24,32},{32,40},{40,48},{48,56},{56,64},{64,7... | collective-permute-start | bytes 147464 | tf_op jit(solution)/shard_map/while/body/eval_jaxpr/ppermute | solution.py:19
  133.9 6.3 %collective-permute-start = (f32[16,768]{1,0:T(8,128)S(1)}, f32[16,768]{1,0:T(8,128)S(1)}, u32[]{:S(2)}, u32[]{:S(2)}) collective-permute-start(f32[16,768]{1,0:T(8,128)S(1)} %copy.50), channel_id=1, source_target_pairs={{0,8},{8,16},{16,24},{24,32},{32,40},{40,48},{48,56},{56,64},{64,7... | collective-permute-start | bytes 147464 | tf_op jit(solution)/shard_map/while/body/eval_jaxpr/ppermute | solution.py:19
  140.2 6.3 %collective-permute-start = (f32[16,768]{1,0:T(8,128)S(1)}, f32[16,768]{1,0:T(8,128)S(1)}, u32[]{:S(2)}, u32[]{:S(2)}) collective-permute-start(f32[16,768]{1,0:T(8,128)S(1)} %copy.50), channel_id=1, source_target_pairs={{0,8},{8,16},{16,24},{24,32},{32,40},{40,48},{48,56},{56,64},{64,7... | collective-permute-start | bytes 147464 | tf_op jit(solution)/shard_map/while/body/eval_jaxpr/ppermute | solution.py:19
  146.5 6.3 %collective-permute-start = (f32[16,768]{1,0:T(8,128)S(1)}, f32[16,768]{1,0:T(8,128)S(1)}, u32[]{:S(2)}, u32[]{:S(2)}) collective-permute-start(f32[16,768]{1,0:T(8,128)S(1)} %copy.50), channel_id=1, source_target_pairs={{0,8},{8,16},{16,24},{24,32},{32,40},{40,48},{48,56},{56,64},{64,7... | collective-permute-start | bytes 147464 | tf_op jit(solution)/shard_map/while/body/eval_jaxpr/ppermute | solution.py:19
  152.8 6.3 %collective-permute-start = (f32[16,768]{1,0:T(8,128)S(1)}, f32[16,768]{1,0:T(8,128)S(1)}, u32[]{:S(2)}, u32[]{:S(2)}) collective-permute-start(f32[16,768]{1,0:T(8,128)S(1)} %copy.50), channel_id=1, source_target_pairs={{0,8},{8,16},{16,24},{24,32},{32,40},{40,48},{48,56},{56,64},{64,7... | collective-permute-start | bytes 147464 | tf_op jit(solution)/shard_map/while/body/eval_jaxpr/ppermute | solution.py:19
  159.1 6.3 %collective-permute-start = (f32[16,768]{1,0:T(8,128)S(1)}, f32[16,768]{1,0:T(8,128)S(1)}, u32[]{:S(2)}, u32[]{:S(2)}) collective-permute-start(f32[16,768]{1,0:T(8,128)S(1)} %copy.50), channel_id=1, source_target_pairs={{0,8},{8,16},{16,24},{24,32},{32,40},{40,48},{48,56},{56,64},{64,7... | collective-permute-start | bytes 147464 | tf_op jit(solution)/shard_map/while/body/eval_jaxpr/ppermute | solution.py:19
  165.4 6.3 %collective-permute-start = (f32[16,768]{1,0:T(8,128)S(1)}, f32[16,768]{1,0:T(8,128)S(1)}, u32[]{:S(2)}, u32[]{:S(2)}) collective-permute-start(f32[16,768]{1,0:T(8,128)S(1)} %copy.50), channel_id=1, source_target_pairs={{0,8},{8,16},{16,24},{24,32},{32,40},{40,48},{48,56},{56,64},{64,7... | collective-permute-start | bytes 147464 | tf_op jit(solution)/shard_map/while/body/eval_jaxpr/ppermute | solution.py:19
  171.7 6.3 %collective-permute-start = (f32[16,768]{1,0:T(8,128)S(1)}, f32[16,768]{1,0:T(8,128)S(1)}, u32[]{:S(2)}, u32[]{:S(2)}) collective-permute-start(f32[16,768]{1,0:T(8,128)S(1)} %copy.50), channel_id=1, source_target_pairs={{0,8},{8,16},{16,24},{24,32},{32,40},{40,48},{48,56},{56,64},{64,7... | collective-permute-start | bytes 147464 | tf_op jit(solution)/shard_map/while/body/eval_jaxpr/ppermute | solution.py:19
  177.9 6.3 %collective-permute-start = (f32[16,768]{1,0:T(8,128)S(1)}, f32[16,768]{1,0:T(8,128)S(1)}, u32[]{:S(2)}, u32[]{:S(2)}) collective-permute-start(f32[16,768]{1,0:T(8,128)S(1)} %copy.50), channel_id=1, source_target_pairs={{0,8},{8,16},{16,24},{24,32},{32,40},{40,48},{48,56},{56,64},{64,7... | collective-permute-start | bytes 147464 | tf_op jit(solution)/shard_map/while/body/eval_jaxpr/ppermute | solution.py:19
  184.2 6.3 %collective-permute-start = (f32[16,768]{1,0:T(8,128)S(1)}, f32[16,768]{1,0:T(8,128)S(1)}, u32[]{:S(2)}, u32[]{:S(2)}) collective-permute-start(f32[16,768]{1,0:T(8,128)S(1)} %copy.50), channel_id=1, source_target_pairs={{0,8},{8,16},{16,24},{24,32},{32,40},{40,48},{48,56},{56,64},{64,7... | collective-permute-start | bytes 147464 | tf_op jit(solution)/shard_map/while/body/eval_jaxpr/ppermute | solution.py:19
  190.5 6.3 %collective-permute-start = (f32[16,768]{1,0:T(8,128)S(1)}, f32[16,768]{1,0:T(8,128)S(1)}, u32[]{:S(2)}, u32[]{:S(2)}) collective-permute-start(f32[16,768]{1,0:T(8,128)S(1)} %copy.50), channel_id=1, source_target_pairs={{0,8},{8,16},{16,24},{24,32},{32,40},{40,48},{48,56},{56,64},{64,7... | collective-permute-start | bytes 147464 | tf_op jit(solution)/shard_map/while/body/eval_jaxpr/ppermute | solution.py:19
  196.8 6.3 %collective-permute-start = (f32[16,768]{1,0:T(8,128)S(1)}, f32[16,768]{1,0:T(8,128)S(1)}, u32[]{:S(2)}, u32[]{:S(2)}) collective-permute-start(f32[16,768]{1,0:T(8,128)S(1)} %copy.50), channel_id=1, source_target_pairs={{0,8},{8,16},{16,24},{24,32},{32,40},{40,48},{48,56},{56,64},{64,7... | collective-permute-start | bytes 147464 | tf_op jit(solution)/shard_map/while/body/eval_jaxpr/ppermute | solution.py:19
  203.1 6.3 %collective-permute-start = (f32[16,768]{1,0:T(8,128)S(1)}, f32[16,768]{1,0:T(8,128)S(1)}, u32[]{:S(2)}, u32[]{:S(2)}) collective-permute-start(f32[16,768]{1,0:T(8,128)S(1)} %copy.50), channel_id=1, source_target_pairs={{0,8},{8,16},{16,24},{24,32},{32,40},{40,48},{48,56},{56,64},{64,7... | collective-permute-start | bytes 147464 | tf_op jit(solution)/shard_map/while/body/eval_jaxpr/ppermute | solution.py:19
  209.4 6.3 %collective-permute-start = (f32[16,768]{1,0:T(8,128)S(1)}, f32[16,768]{1,0:T(8,128)S(1)}, u32[]{:S(2)}, u32[]{:S(2)}) collective-permute-start(f32[16,768]{1,0:T(8,128)S(1)} %copy.50), channel_id=1, source_target_pairs={{0,8},{8,16},{16,24},{24,32},{32,40},{40,48},{48,56},{56,64},{64,7... | collective-permute-start | bytes 147464 | tf_op jit(solution)/shard_map/while/body/eval_jaxpr/ppermute | solution.py:19
  215.7 6.3 %collective-permute-start = (f32[16,768]{1,0:T(8,128)S(1)}, f32[16,768]{1,0:T(8,128)S(1)}, u32[]{:S(2)}, u32[]{:S(2)}) collective-permute-start(f32[16,768]{1,0:T(8,128)S(1)} %copy.50), channel_id=1, source_target_pairs={{0,8},{8,16},{16,24},{24,32},{32,40},{40,48},{48,56},{56,64},{64,7... | collective-permute-start | bytes 147464 | tf_op jit(solution)/shard_map/while/body/eval_jaxpr/ppermute | solution.py:19
  222.0 6.3 %collective-permute-start = (f32[16,768]{1,0:T(8,128)S(1)}, f32[16,768]{1,0:T(8,128)S(1)}, u32[]{:S(2)}, u32[]{:S(2)}) collective-permute-start(f32[16,768]{1,0:T(8,128)S(1)} %copy.50), channel_id=1, source_target_pairs={{0,8},{8,16},{16,24},{24,32},{32,40},{40,48},{48,56},{56,64},{64,7... | collective-permute-start | bytes 147464 | tf_op jit(solution)/shard_map/while/body/eval_jaxpr/ppermute | solution.py:19
  228.3 6.3 %collective-permute-start = (f32[16,768]{1,0:T(8,128)S(1)}, f32[16,768]{1,0:T(8,128)S(1)}, u32[]{:S(2)}, u32[]{:S(2)}) collective-permute-start(f32[16,768]{1,0:T(8,128)S(1)} %copy.50), channel_id=1, source_target_pairs={{0,8},{8,16},{16,24},{24,32},{32,40},{40,48},{48,56},{56,64},{64,7... | collective-permute-start | bytes 147464 | tf_op jit(solution)/shard_map/while/body/eval_jaxpr/ppermute | solution.py:19
  234.5 6.3 %collective-permute-start = (f32[16,768]{1,0:T(8,128)S(1)}, f32[16,768]{1,0:T(8,128)S(1)}, u32[]{:S(2)}, u32[]{:S(2)}) collective-permute-start(f32[16,768]{1,0:T(8,128)S(1)} %copy.50), channel_id=1, source_target_pairs={{0,8},{8,16},{16,24},{24,32},{32,40},{40,48},{48,56},{56,64},{64,7... | collective-permute-start | bytes 147464 | tf_op jit(solution)/shard_map/while/body/eval_jaxpr/ppermute | solution.py:19
  240.8 6.3 %collective-permute-start = (f32[16,768]{1,0:T(8,128)S(1)}, f32[16,768]{1,0:T(8,128)S(1)}, u32[]{:S(2)}, u32[]{:S(2)}) collective-permute-start(f32[16,768]{1,0:T(8,128)S(1)} %copy.50), channel_id=1, source_target_pairs={{0,8},{8,16},{16,24},{24,32},{32,40},{40,48},{48,56},{56,64},{64,7... | collective-permute-start | bytes 147464 | tf_op jit(solution)/shard_map/while/body/eval_jaxpr/ppermute | solution.py:19
  247.1 6.3 %collective-permute-start = (f32[16,768]{1,0:T(8,128)S(1)}, f32[16,768]{1,0:T(8,128)S(1)}, u32[]{:S(2)}, u32[]{:S(2)}) collective-permute-start(f32[16,768]{1,0:T(8,128)S(1)} %copy.50), channel_id=1, source_target_pairs={{0,8},{8,16},{16,24},{24,32},{32,40},{40,48},{48,56},{56,64},{64,7... | collective-permute-start | bytes 147464 | tf_op jit(solution)/shard_map/while/body/eval_jaxpr/ppermute | solution.py:19
  253.4 6.3 %collective-permute-start = (f32[16,768]{1,0:T(8,128)S(1)}, f32[16,768]{1,0:T(8,128)S(1)}, u32[]{:S(2)}, u32[]{:S(2)}) collective-permute-start(f32[16,768]{1,0:T(8,128)S(1)} %copy.50), channel_id=1, source_target_pairs={{0,8},{8,16},{16,24},{24,32},{32,40},{40,48},{48,56},{56,64},{64,7... | collective-permute-start | bytes 147464 | tf_op jit(solution)/shard_map/while/body/eval_jaxpr/ppermute | solution.py:19
  259.7 6.3 %collective-permute-start = (f32[16,768]{1,0:T(8,128)S(1)}, f32[16,768]{1,0:T(8,128)S(1)}, u32[]{:S(2)}, u32[]{:S(2)}) collective-permute-start(f32[16,768]{1,0:T(8,128)S(1)} %copy.50), channel_id=1, source_target_pairs={{0,8},{8,16},{16,24},{24,32},{32,40},{40,48},{48,56},{56,64},{64,7... | collective-permute-start | bytes 147464 | tf_op jit(solution)/shard_map/while/body/eval_jaxpr/ppermute | solution.py:19
  266.0 6.3 %collective-permute-start = (f32[16,768]{1,0:T(8,128)S(1)}, f32[16,768]{1,0:T(8,128)S(1)}, u32[]{:S(2)}, u32[]{:S(2)}) collective-permute-start(f32[16,768]{1,0:T(8,128)S(1)} %copy.50), channel_id=1, source_target_pairs={{0,8},{8,16},{16,24},{24,32},{32,40},{40,48},{48,56},{56,64},{64,7... | collective-permute-start | bytes 147464 | tf_op jit(solution)/shard_map/while/body/eval_jaxpr/ppermute | solution.py:19
  272.3 6.3 %collective-permute-start = (f32[16,768]{1,0:T(8,128)S(1)}, f32[16,768]{1,0:T(8,128)S(1)}, u32[]{:S(2)}, u32[]{:S(2)}) collective-permute-start(f32[16,768]{1,0:T(8,128)S(1)} %copy.50), channel_id=1, source_target_pairs={{0,8},{8,16},{16,24},{24,32},{32,40},{40,48},{48,56},{56,64},{64,7... | collective-permute-start | bytes 147464 | tf_op jit(solution)/shard_map/while/body/eval_jaxpr/ppermute | solution.py:19
  278.6 6.3 %collective-permute-start = (f32[16,768]{1,0:T(8,128)S(1)}, f32[16,768]{1,0:T(8,128)S(1)}, u32[]{:S(2)}, u32[]{:S(2)}) collective-permute-start(f32[16,768]{1,0:T(8,128)S(1)} %copy.50), channel_id=1, source_target_pairs={{0,8},{8,16},{16,24},{24,32},{32,40},{40,48},{48,56},{56,64},{64,7... | collective-permute-start | bytes 147464 | tf_op jit(solution)/shard_map/while/body/eval_jaxpr/ppermute | solution.py:19
  284.9 6.3 %collective-permute-start = (f32[16,768]{1,0:T(8,128)S(1)}, f32[16,768]{1,0:T(8,128)S(1)}, u32[]{:S(2)}, u32[]{:S(2)}) collective-permute-start(f32[16,768]{1,0:T(8,128)S(1)} %copy.50), channel_id=1, source_target_pairs={{0,8},{8,16},{16,24},{24,32},{32,40},{40,48},{48,56},{56,64},{64,7... | collective-permute-start | bytes 147464 | tf_op jit(solution)/shard_map/while/body/eval_jaxpr/ppermute | solution.py:19
  291.1 6.3 %collective-permute-start = (f32[16,768]{1,0:T(8,128)S(1)}, f32[16,768]{1,0:T(8,128)S(1)}, u32[]{:S(2)}, u32[]{:S(2)}) collective-permute-start(f32[16,768]{1,0:T(8,128)S(1)} %copy.50), channel_id=1, source_target_pairs={{0,8},{8,16},{16,24},{24,32},{32,40},{40,48},{48,56},{56,64},{64,7... | collective-permute-start | bytes 147464 | tf_op jit(solution)/shard_map/while/body/eval_jaxpr/ppermute | solution.py:19
  297.4 6.3 %collective-permute-start = (f32[16,768]{1,0:T(8,128)S(1)}, f32[16,768]{1,0:T(8,128)S(1)}, u32[]{:S(2)}, u32[]{:S(2)}) collective-permute-start(f32[16,768]{1,0:T(8,128)S(1)} %copy.50), channel_id=1, source_target_pairs={{0,8},{8,16},{16,24},{24,32},{32,40},{40,48},{48,56},{56,64},{64,7... | collective-permute-start | bytes 147464 | tf_op jit(solution)/shard_map/while/body/eval_jaxpr/ppermute | solution.py:19
  303.7 6.3 %collective-permute-start = (f32[16,768]{1,0:T(8,128)S(1)}, f32[16,768]{1,0:T(8,128)S(1)}, u32[]{:S(2)}, u32[]{:S(2)}) collective-permute-start(f32[16,768]{1,0:T(8,128)S(1)} %copy.50), channel_id=1, source_target_pairs={{0,8},{8,16},{16,24},{24,32},{32,40},{40,48},{48,56},{56,64},{64,7... | collective-permute-start | bytes 147464 | tf_op jit(solution)/shard_map/while/body/eval_jaxpr/ppermute | solution.py:19
  310.0 6.3 %collective-permute-start = (f32[16,768]{1,0:T(8,128)S(1)}, f32[16,768]{1,0:T(8,128)S(1)}, u32[]{:S(2)}, u32[]{:S(2)}) collective-permute-start(f32[16,768]{1,0:T(8,128)S(1)} %copy.50), channel_id=1, source_target_pairs={{0,8},{8,16},{16,24},{24,32},{32,40},{40,48},{48,56},{56,64},{64,7... | collective-permute-start | bytes 147464 | tf_op jit(solution)/shard_map/while/body/eval_jaxpr/ppermute | solution.py:19
  (37 other events, 320.5 us)
where the time goes:
time: 362 us; the launch traced here: 361 us
  waiting for transfers between devices  190 us (52%)
  blocking collectives  74.6 us (21%)
  matrix products  35.8 us (10%)
  local copies, waits for them, and re-layouts  24.2 us (7%)
  other arithmetic  19.9 us (5%)
  starting transfers between devices  13 us (4%)
    ppermute x64, waiting for transfers between devices, passed_along(): return lax.ppermute(value, axis, pairs)  173 us
    psum x1, blocking collectives, per_device(): pooled = lax.psum(partial_sums, 'narrow') / (FRAMES * SPATIAL)  38 us
    psum x1, blocking collectives, per_device(): grad_unit = lax.psum(grad_unit, 'narrow')  36.7 us
    sub x1, other arithmetic, per_device(): expo = jnp.exp(scores - top)  17.7 us
    all_to_all x1, waiting for transfers between devices, per_device(): lax.all_to_all(video, 'narrow', split_axis=2, concat_axis=1, tiled=True)  17 us
    dot_general x32, matrix products, pair_terms(): grad_block = TEMP * jnp.dot(weight.T, unit, precision=lax.Precision.HIGHEST)  8.72 us
    reshape x1, local copies, waits for them, and re-layouts, per_device(): qkv = qkv.reshape(items, frames, spots, 3, HEADS, head_size)  8.59 us
    dot_general x1, matrix products, per_device(): jnp.dot(rows, w_qkv, preferred_element_type=jnp.float32)  7.61 us
  transfers between devices with their start and end apart: 65, of which 33 were waited for; matrix products, arithmetic and copies ran while one was open for 5% of the time, Pallas kernels for 0%

commit v1 on v0

v1 whole, which is shorter than its diff:
```python
import jax
import jax.numpy as jnp
from jax import lax
from jax.experimental import pallas as pl
from jax.experimental.pallas import tpu as pltpu
from jax.sharding import PartitionSpec as P

D = 1024
E = 768
HEADS = 16
HEAD = D // HEADS
FRAMES = 16
SPATIAL = 64
TOKENS = FRAMES * SPATIAL
LANES = 128
GROUP = 4
WIDTH = GROUP * HEAD
BLOCKS = 4
ROWS = FRAMES * 8

TEMP = 10.0
BIAS = -2.0
EPS = 1e-06
LOG2E = 1.4426950408889634

F32 = jnp.float32
BF16 = jnp.bfloat16


def dot(a, b):
    return jnp.dot(a, b, preferred_element_type=F32)


def dot_t(a, b):
    return lax.dot_general(a, b, (((1,), (1,)), ((), ())), preferred_element_type=F32)


def parts_of(value, count):
    terms = []
    for _ in range(count):
        term = value.astype(BF16)
        terms.append(term)
        value = value - term.astype(F32)
    return terms


def temporal_kernel(x_ref, wqkv_hbm, wout_hbm, wproj_hbm, out_ref, wqkv, wout, wproj, weights, sems):
    copies = []
    for j in range(HEADS // GROUP):
        for k in range(2):
            cols = pl.ds(k * D + j * WIDTH, WIDTH)
            copies.append(pltpu.make_async_copy(wqkv_hbm.at[:, cols], wqkv.at[:, cols], sems.at[len(copies)]))
    cols = pl.ds(2 * D, D)
    copies.append(pltpu.make_async_copy(wqkv_hbm.at[:, cols], wqkv.at[:, cols], sems.at[len(copies)]))
    copies.append(pltpu.make_async_copy(wout_hbm, wout, sems.at[len(copies)]))
    copies.append(pltpu.make_async_copy(wproj_hbm, wproj, sems.at[len(copies)]))
    for copy in copies:
        copy.start()
    x = jnp.concatenate([x_ref[:, 16 * b : 16 * b + 16, :].reshape(ROWS, D) for b in range(BLOCKS)], axis=0)
    lane = lax.broadcasted_iota(jnp.int32, (ROWS, WIDTH), 1) // HEAD
    same = lax.broadcasted_iota(jnp.int32, (8, ROWS), 0) == lax.broadcasted_iota(jnp.int32, (8, ROWS), 1) % 8
    ones = jnp.ones((8, ROWS), BF16)
    for j in range(HEADS // GROUP):
        copies[2 * j].wait()
        query = dot(x, wqkv[:, j * WIDTH : (j + 1) * WIDTH]).astype(BF16)
        copies[2 * j + 1].wait()
        keys = dot(x, wqkv[:, D + j * WIDTH : D + (j + 1) * WIDTH]).astype(BF16)
        for b in range(BLOCKS):
            q = query[b * ROWS : (b + 1) * ROWS]
            k = keys[b * ROWS : (b + 1) * ROWS]
            split = jnp.concatenate([jnp.where(lane == h, k, jnp.zeros_like(k)) for h in range(GROUP)], axis=0)
            scores = dot_t(split, q).reshape(GROUP, FRAMES, 8, ROWS)
            top = jnp.max(scores, axis=1, keepdims=True)
            expo = jnp.exp2((scores - top) * (HEAD**-0.5 * LOG2E))
            total = jnp.sum(expo, axis=1, keepdims=True)
            probs = expo * jnp.where(same, 1.0 / total, 0.0)
            row = dot_t(ones, probs.astype(BF16).reshape(GROUP * ROWS, ROWS))
            for h in range(GROUP):
                weights[j * GROUP + h : j * GROUP + h + 1, b * ROWS : (b + 1) * ROWS] = row[:1, h * ROWS : (h + 1) * ROWS]
    left = parts_of(weights[...], 2) + [jnp.ones((HEADS, BLOCKS * ROWS), BF16)]
    sums = dot(jnp.concatenate(left, axis=0), x)
    heads = sums[:HEADS] + sums[HEADS : 2 * HEADS]
    rows = sums[2 * HEADS : 2 * HEADS + 1]
    copies[-3].wait()
    values = dot(jnp.concatenate(parts_of(heads, 2), axis=0), wqkv[:, 2 * D :])
    values = values[:HEADS] + values[HEADS:]
    own = lax.broadcasted_iota(jnp.int32, (HEADS, D), 0) == lax.broadcasted_iota(jnp.int32, (HEADS, D), 1) // HEAD
    mixed = jnp.sum(jnp.where(own, values, 0.0), axis=0, keepdims=True)
    copies[-2].wait()
    mixed = jnp.concatenate([jnp.broadcast_to(part, (8, D)) for part in parts_of(mixed, 2)], axis=0)
    layer = dot(mixed, wout[...])
    pooled = (rows + layer[:1] + layer[8:9]) * (1.0 / TOKENS)
    copies[-1].wait()
    pooled = jnp.concatenate([jnp.broadcast_to(part, (8, D)) for part in parts_of(pooled, 3)], axis=0)
    embed = dot(pooled, wproj[...])
    embed = embed[:8] + embed[8:16] + embed[16:24]
    for j in range(E // LANES):
        out_ref[:, j, :] = embed[:, j * LANES : (j + 1) * LANES]
    out_ref[:, E // LANES :, :] = jnp.zeros((8, 8 - E // LANES, LANES), F32)


def temporal(x, w_qkv, w_out, w_proj):
    anywhere = pl.BlockSpec(memory_space=pl.ANY)
    return pl.pallas_call(
        temporal_kernel,
        out_shape=jax.ShapeDtypeStruct((8, 8, LANES), F32),
        in_specs=[pl.BlockSpec(memory_space=pltpu.VMEM), anywhere, anywhere, anywhere],
        out_specs=pl.BlockSpec(memory_space=pltpu.VMEM),
        scratch_shapes=[
            pltpu.VMEM((D, 3 * D), BF16),
            pltpu.VMEM((D, D), BF16),
            pltpu.VMEM((D, E), BF16),
            pltpu.VMEM((HEADS, BLOCKS * ROWS), F32),
            pltpu.SemaphoreType.DMA((11,)),
        ],
        compiler_params=pltpu.CompilerParams(vmem_limit_bytes=40 << 20),
        cost_estimate=pl.CostEstimate(flops=3 << 30, bytes_accessed=11 << 20, transcendentals=0),
        name="temporal",
    )(x, w_qkv, w_out, w_proj)


def unit_kernel(parts_ref, positive_ref, unit_ref, length_ref, send_ref):
    for j in range(E // LANES):
        for c in range(4):
            unit_ref[c : c + 1, j * LANES : (j + 1) * LANES] = parts_ref[2 * c, j : j + 1, :] + parts_ref[2 * c + 1, j : j + 1, :]
    embed = unit_ref[...]
    length = jnp.sqrt(jnp.sum(embed * embed, axis=-1, keepdims=True) + EPS)
    unit = embed / length
    unit_ref[...] = unit
    length_ref[...] = jnp.broadcast_to(length, length_ref.shape)
    send_ref[:, :, :E] = jnp.broadcast_to(unit[None], (send_ref.shape[0], 4, E))
    send_ref[:, :, E:] = jnp.broadcast_to(positive_ref[...][None], (send_ref.shape[0], 4, LANES))


def make_units(parts, positive, copies):
    return pl.pallas_call(
        unit_kernel,
        out_shape=(
            jax.ShapeDtypeStruct((4, E), F32),
            jax.ShapeDtypeStruct((4, LANES), F32),
            jax.ShapeDtypeStruct((copies, 4, E + LANES), F32),
        ),
        name="units",
    )(parts, positive)


def row_lengths(cap):
    squares = cap.astype(F32)
    squares = squares * squares
    ones = jnp.ones((8, E), BF16)
    total = sum(dot_t(ones, part) for part in parts_of(squares, 2))
    return 1.0 / jnp.sqrt(total[:1] + EPS)


def slope(logits, hit):
    sign = jnp.where(hit, 1.0, -1.0)
    return -sign / (1.0 + jnp.exp(sign * logits))


def clip_kernel(unit_ref, cap_ref, ids_ref, positive_ref, out_ref):
    cap = cap_ref[...]
    scale = row_lengths(cap)
    logits = dot_t(jnp.concatenate(parts_of(unit_ref[...], 3), axis=0), cap)
    logits = (logits[:4] + logits[4:8] + logits[8:12]) * (TEMP * scale) + BIAS
    weight = slope(logits, ids_ref[...] == positive_ref[:, :1])
    grad = dot(jnp.concatenate(parts_of(weight * (TEMP * scale), 3), axis=0), cap)
    out_ref[...] = grad[:4] + grad[4:8] + grad[8:12]


def clip_part(unit, caps, ids, positive):
    return pl.pallas_call(
        clip_kernel,
        out_shape=jax.ShapeDtypeStruct((4, E), F32),
        compiler_params=pltpu.CompilerParams(vmem_limit_bytes=24 << 20),
        cost_estimate=pl.CostEstimate(flops=100 << 20, bytes_accessed=1 << 20, transcendentals=0),
        name="clip_part",
    )(unit, caps, ids, positive)


def caption_kernel(units_ref, other_ref, cap_ref, ids_ref, out_ref):
    cap = cap_ref[...].astype(F32)
    length = jnp.sqrt(jnp.sum(cap * cap, axis=-1, keepdims=True) + EPS)
    cap_unit = cap / length
    grad = jnp.zeros(cap.shape, F32)
    for ref in (units_ref, other_ref):
        rows = jnp.concatenate([ref[g] for g in range(ref.shape[0])], axis=0)
        unit = rows[:, :E]
        positive = rows[:, E:].T[:1]
        logits = TEMP * lax.dot_general(
            cap_unit, unit, (((1,), (1,)), ((), ())), precision=lax.Precision.HIGHEST, preferred_element_type=F32
        ) + BIAS
        weight = slope(logits, ids_ref[:, : rows.shape[0]] == positive)
        grad += TEMP * jnp.dot(weight, unit, precision=lax.Precision.HIGHEST, preferred_element_type=F32)
    out_ref[...] = (grad - cap_unit * jnp.sum(cap_unit * grad, axis=-1, keepdims=True)) / length


def caption_grads(units, other, captions, ids):
    return pl.pallas_call(
        caption_kernel,
        out_shape=jax.ShapeDtypeStruct(captions.shape, F32),
        compiler_params=pltpu.CompilerParams(vmem_limit_bytes=24 << 20),
        name="caption_grad",
    )(units, other, captions, ids)


def swapped(value, axis, bit):
    return lax.ppermute(value, axis, [(i, i ^ bit) for i in range(lax.axis_size(axis))])


def per_device(video, w_qkv, w_out, w_proj, captions, positive):
    wide = lax.axis_size("wide")
    narrow = lax.axis_size("narrow")
    rank_wide = lax.axis_index("wide")
    rank_narrow = lax.axis_index("narrow")
    cap_rows = captions.shape[0]
    chips = wide // 2
    same_core = [[2 * g + core for g in range(chips)] for core in range(2)]

    send = video.reshape(4, 2, 8, 8, D).transpose(0, 2, 1, 3, 4).reshape(8, 64, D)
    tokens = lax.all_to_all(send, "narrow", 0, 0, tiled=True)

    near = lax.all_to_all(
        jnp.broadcast_to(captions[None], (chips, cap_rows, E)), "wide", 0, 0, axis_index_groups=same_core, tiled=True
    )
    caps = jnp.concatenate([near, swapped(near, "wide", 1)], axis=0).reshape(wide * cap_rows, E)
    core = rank_wide % 2
    source = jnp.arange(wide, dtype=jnp.int32)
    source = jnp.where(source < chips, 2 * source + core, 2 * (source - chips) + 1 - core)
    cap_ids = (source[:, None] * narrow + rank_narrow) * cap_rows + jnp.arange(cap_rows, dtype=jnp.int32)[None]
    cap_ids = cap_ids.reshape(1, wide * cap_rows).astype(F32)
    own_ids = (rank_wide * narrow + rank_narrow) * cap_rows + jnp.arange(cap_rows, dtype=jnp.int32)
    own_ids = jnp.broadcast_to(own_ids.astype(F32)[:, None], (cap_rows, LANES))
    positive = jnp.broadcast_to(positive.astype(F32)[:, None], (4, LANES))

    parts = lax.all_to_all(temporal(tokens, w_qkv, w_out, w_proj), "narrow", 0, 0, tiled=True)
    unit, length, outgoing = make_units(parts, positive, chips)
    units = lax.all_to_all(outgoing, "wide", 0, 0, axis_index_groups=same_core, tiled=True)
    other = swapped(units, "wide", 1)
    caption_grad = caption_grads(units, other, captions, own_ids)

    grad_unit = clip_part(unit, caps, cap_ids, positive)
    for bit in (1, 2, 4):
        grad_unit = grad_unit + swapped(grad_unit, "narrow", bit)
    clip_grad = (grad_unit - unit * jnp.sum(unit * grad_unit, axis=-1, keepdims=True)) / length[:, :1]
    return (clip_grad, caption_grad)


def solution(mesh):
    in_specs = (
        P("wide", "narrow", None, None),
        P(),
        P(),
        P(),
        P(("wide", "narrow"), None),
        P("wide"),
    )
    out_specs = (P("wide", None), P(("wide", "narrow"), None))
    return jax.shard_map(
        per_device, mesh=mesh, in_specs=in_specs, out_specs=out_specs, check_vma=False
    )
```

time: 362 us -> 106 us (0.29)
  the two profiles are of different devices: /device:TPU:128 before, /device:TPU:8 now
where the time goes in v1:
time: 106 us
  waiting for transfers between devices  45.8 us (43%)
  starting transfers between devices  28.3 us (27%)
  Pallas kernels  18.9 us (18%)
  local copies, waits for them, and re-layouts  9.82 us (9%)
  other arithmetic  1.97 us (2%)
    all_to_all x1, waiting for transfers between devices, per_device(): tokens = lax.all_to_all(send, 'narrow', 0, 0, tiled=True)  15.4 us
    pallas_call x1, Pallas kernels, temporal(): pl.pallas_call(temporal_kernel, out_shape=jax.ShapeDtypeStruct((8, 8, LAN...  14.3 us
    ppermute x5, waiting for transfers between devices, swapped(): lax.ppermute(value, axis, [(i, i ^ bit) for i in range(lax.axis_size(axis...  12.1 us
    all_to_all x1, waiting for transfers between devices, per_device(): lax.all_to_all(jnp.broadcast_to(captions[None], (chips, cap_rows, E)), 'w...  10.7 us
    all_to_all x1, starting transfers between devices, per_device(): lax.all_to_all(jnp.broadcast_to(captions[None], (chips, cap_rows, E)), 'w...  9.94 us
    all_to_all x1, waiting for transfers between devices, per_device(): lax.all_to_all(temporal(tokens, w_qkv, w_out, w_proj), 'narrow', 0, 0, ti...  7.66 us
    all_to_all x1, starting transfers between devices, per_device(): lax.all_to_all(outgoing, 'wide', 0, 0, axis_index_groups=same_core, tiled...  6.96 us
    all_to_all x1, starting transfers between devices, per_device(): tokens = lax.all_to_all(send, 'narrow', 0, 0, tiled=True)  6.03 us
  transfers between devices with their start and end apart: 9, of which 6 were waited for; matrix products, arithmetic and copies ran while one was open for 5% of the time, Pallas kernels for 16%

profile of v1, /device:TPU:8, one launch (start us, length us, event | category | flops | bytes accessed | tf_op | source)
XLA Modules:
  0.0 105.5 jit_solution(4439242714787213234)
XLA Ops:
  0.6 1.5 %broadcast_in_dim.7 = bf16[16,16,768]{2,1,0:T(8,128)(2,1)} broadcast(bf16[16,768]{1,0:T(8,128)(2,1)} %cap_ref.1), dimensions={1,2} | broadcast | bytes 417792 | tf_op jit(solution)/shard_map/broadcast_in_dim | solution.py:223
  2.2 9.9 %all-to-all-start.2 = ((bf16[16,16,768]{2,1,0:T(8,128)(2,1)}), bf16[16,16,768]{2,1,0:T(8,128)(2,1)S(1)}, u32[]{:S(2)}, u32[]{:S(2)}) async-start(bf16[16,16,768]{2,1,0:T(8,128)(2,1)} %broadcast_in_dim.7), calls=%async_computation.2 | async-start | bytes 786432 | tf_op jit(solution)/shard_map/all_to_all | solution.py:222
  12.1 2.5 %copy.9 = bf16[4,2,8,8,1024]{4,3,1,2,0:T(8,128)(2,1)} copy(bf16[4,2,8,8,1024]{4,3,2,1,0:T(8,128)(2,1)} %bitcast.7) | data formatting | bytes 2097152 | tf_op jit(solution)/shard_map/reshape | solution.py:219
  14.6 10.7 %all-to-all-done.2 = bf16[16,16,768]{2,1,0:T(8,128)(2,1)S(1)} async-done(((bf16[16,16,768]{2,1,0:T(8,128)(2,1)}), bf16[16,16,768]{2,1,0:T(8,128)(2,1)S(1)}, u32[]{:S(2)}, u32[]{:S(2)}) %all-to-all-start.2) | async-done | bytes 393248 | tf_op jit(solution)/shard_map/all_to_all | solution.py:222
  25.2 6.0 %all-to-all-start = ((bf16[8,64,1024]{2,1,0:T(8,128)(2,1)}), bf16[8,64,1024]{2,1,0:T(8,128)(2,1)S(1)}, u32[]{:S(2)}, u32[]{:S(2)}) async-start(bf16[8,64,1024]{2,1,0:T(8,128)(2,1)} %bitcast.6), calls=%async_computation | async-start | bytes 2097152 | tf_op jit(solution)/shard_map/all_to_all | solution.py:220
  31.2 0.1 collective-permute-start
  31.4 15.4 %all-to-all-done.x_ref = bf16[8,64,1024]{2,1,0:T(8,128)(2,1)S(1)} async-done(((bf16[8,64,1024]{2,1,0:T(8,128)(2,1)}), bf16[8,64,1024]{2,1,0:T(8,128)(2,1)S(1)}, u32[]{:S(2)}, u32[]{:S(2)}) %all-to-all-start) | async-done | bytes 1048608 | tf_op jit(solution)/shard_map/all_to_all | solution.py:220
  46.7 2.8 %copy-done.4 = bf16[1024,3072]{1,0:T(8,128)(2,1)S(1)} copy-done((bf16[1024,3072]{1,0:T(8,128)(2,1)S(1)}, bf16[1024,3072]{1,0:T(8,128)(2,1)}, u32[]{:S(2)}) %copy-start.4) | copy-done | bytes 6291480
  49.5 1.4 %copy-done.6 = bf16[1024,768]{1,0:T(8,128)(2,1)S(1)} copy-done((bf16[1024,768]{1,0:T(8,128)(2,1)S(1)}, bf16[1024,768]{1,0:T(8,128)(2,1)}, u32[]{:S(2)}) %copy-start.6) | copy-done | bytes 1572888
  50.9 14.3 %temporal.1 = f32[8,8,128]{2,1,0:T(8,128)} custom-call(bf16[8,64,1024]{2,1,0:T(8,128)(2,1)S(1)} %all-to-all-done.x_ref, bf16[1024,3072]{1,0:T(8,128)(2,1)S(1)} %copy-done.4, bf16[1024,1024]{1,0:T(8,128)(2,1)S(1)} %copy-done.5, bf16[1024,768]{1,0:T(8,128)(2,1)S(1)} %copy-done.6), custom_call_target="tpu_custom_call" | custom-call | flops 3221225472 | bytes 11534336 | tf_op jit(solution)/shard_map/temporal/pallas_call | solution.py:104
  65.2 3.4 %all-to-all-start.1 = ((f32[8,8,128]{2,1,0:T(8,128)}), f32[8,8,128]{2,1,0:T(8,128)S(1)}, u32[]{:S(2)}, u32[]{:S(2)}) async-start(f32[8,8,128]{2,1,0:T(8,128)} %temporal.1), calls=%async_computation.1 | async-start | bytes 65536 | tf_op jit(solution)/shard_map/all_to_all | solution.py:235
  68.6 7.7 %all-to-all-done.1.parts_ref = f32[8,8,128]{2,1,0:T(8,128)S(1)} async-done(((f32[8,8,128]{2,1,0:T(8,128)}), f32[8,8,128]{2,1,0:T(8,128)S(1)}, u32[]{:S(2)}, u32[]{:S(2)}) %all-to-all-start.1) | async-done | bytes 32800 | tf_op jit(solution)/shard_map/all_to_all | solution.py:235
  76.3 0.6 broadcast_in_dim.6.positive_ref
  76.9 1.6 %units.1 = (f32[4,768]{1,0:T(4,128)}, f32[4,128]{1,0:T(4,128)}, f32[16,4,896]{2,1,0:T(4,128)}) custom-call(f32[8,8,128]{2,1,0:T(8,128)} %copy-done.7, f32[4,128]{1,0:T(4,128)} %broadcast_in_dim.6.positive_ref), custom_call_target="tpu_custom_call" | custom-call | tf_op jit(solution)/shard_map/units/pallas_call | solution.py:136
  78.5 7.0 %all-to-all-start.3 = ((f32[16,4,896]{2,1,0:T(4,128)}), f32[16,4,896]{2,1,0:T(4,128)S(1)}, u32[]{:S(2)}, u32[]{:S(2)}) async-start(f32[16,4,896]{2,1,0:T(4,128)} %get-tuple-element.7), calls=%async_computation.3 | async-start | bytes 458752 | tf_op jit(solution)/shard_map/all_to_all | solution.py:237
  85.5 0.1 add_convert_fusion
  85.5 0.1 convert_element_type.17.ids_ref
  85.6 1.1 %pad_maximum_fusion = bf16[32,16,768]{2,1,0:T(8,128)(2,1)S(1)} fusion(bf16[16,16,768]{2,1,0:T(8,128)(2,1)} %collective-permute-done, bf16[16,16,768]{2,1,0:T(8,128)(2,1)S(1)} %all-to-all-done.2), kind=kLoop, calls=%fused_computation | loop fusion | flops 393216 | bytes 1572864 | tf_op jit(solution)/shard_map/concatenate | solution.py:225
  86.7 0.7 copy-done
  87.4 1.0 clip_part.1
  88.4 0.7 collective-permute-start.1
  89.1 3.1 %collective-permute-done.1 = f32[4,768]{1,0:T(4,128)S(1)} collective-permute-done((f32[4,768]{1,0:T(4,128)S(1)}, f32[4,768]{1,0:T(4,128)S(1)}, u32[]{:S(2)}, u32[]{:S(2)}) %collective-permute-start.1) | collective-permute-done | bytes 12320 | tf_op jit(solution)/shard_map/ppermute | solution.py:207
  92.2 1.2 %collective-permute-start.2 = (f32[4,768]{1,0:T(4,128)S(1)}, f32[4,768]{1,0:T(4,128)S(1)}, u32[]{:S(2)}, u32[]{:S(2)}) collective-permute-start(f32[4,768]{1,0:T(4,128)S(1)} %add.94), channel_id=1, source_target_pairs={{0,2},{1,3},{2,0},{3,1},{4,6},{5,7},{6,4},{7,5},{8,10},{9,11},{10,... | collective-permute-start | bytes 36872 | tf_op jit(solution)/shard_map/ppermute | solution.py:207
  93.3 4.0 %collective-permute-done.2 = f32[4,768]{1,0:T(4,128)S(1)} collective-permute-done((f32[4,768]{1,0:T(4,128)S(1)}, f32[4,768]{1,0:T(4,128)S(1)}, u32[]{:S(2)}, u32[]{:S(2)}) %collective-permute-start.2) | collective-permute-done | bytes 12320 | tf_op jit(solution)/shard_map/ppermute | solution.py:207
  97.4 0.0 collective-permute-start.3
  97.4 0.1 slice_reduce_fusion
  97.5 0.1 collective-permute-start.4
  97.6 5.0 %collective-permute-done.3 = f32[4,768]{1,0:T(4,128)S(1)} collective-permute-done((f32[4,768]{1,0:T(4,128)S(1)}, f32[4,768]{1,0:T(4,128)S(1)}, u32[]{:S(2)}, u32[]{:S(2)}) %collective-permute-start.3) | collective-permute-done | bytes 12320 | tf_op jit(solution)/shard_map/ppermute | solution.py:207
  102.6 0.1 multiply_reduce_fusion
  102.7 0.7 subtract_divide_fusion
  103.4 0.1 broadcast_in_dim.8.ids_ref
  103.5 2.1 %caption_grad.1 = f32[16,768]{1,0:T(8,128)} custom-call(f32[16,4,896]{2,1,0:T(4,128)S(1)} %all-to-all-done.3.units_ref, f32[16,4,896]{2,1,0:T(4,128)S(1)} %collective-permute-done.4.other_ref, bf16[16,768]{1,0:T(8,128)(2,1)S(1)} %copy-done.2, f32[16,128]{1,0:T(8,128)S(1)} %broadcast_in_dim.8.ids_ref), custom_call_target="tpu_custom_call" | custom-call | tf_op jit(solution)/shard_map/caption_grad/pallas_call | solution.py:198
  (25 shorter events, 0.1 us)
Async XLA Ops:
  2.2 23.0 %all-to-all-start.2 = ((bf16[16,16,768]{2,1,0:T(8,128)(2,1)}), bf16[16,16,768]{2,1,0:T(8,128)(2,1)S(1)}, u32[]{:S(2)}, u32[]{:S(2)}) async-start(bf16[16,16,768]{2,1,0:T(8,128)(2,1)} %broadcast_in_dim.7), calls=%async_computation.2 | async-start | bytes 786432 | tf_op jit(solution)/shard_map/all_to_all | solution.py:222
  12.1 34.6 %copy-start.5 = (bf16[1024,1024]{1,0:T(8,128)(2,1)S(1)}, bf16[1024,1024]{1,0:T(8,128)(2,1)}, u32[]{:S(2)}) copy-start(bf16[1024,1024]{1,0:T(8,128)(2,1)} %wout_hbm.1) | copy-start | bytes 6291460
  25.2 21.5 %all-to-all-start = ((bf16[8,64,1024]{2,1,0:T(8,128)(2,1)}), bf16[8,64,1024]{2,1,0:T(8,128)(2,1)S(1)}, u32[]{:S(2)}, u32[]{:S(2)}) async-start(bf16[8,64,1024]{2,1,0:T(8,128)(2,1)} %bitcast.6), calls=%async_computation | async-start | bytes 2097152 | tf_op jit(solution)/shard_map/all_to_all | solution.py:220
  31.2 37.4 %copy-start.9 = (s32[4]{0:T(128)S(1)}, s32[4]{0:T(128)}, u32[]{:S(2)}) copy-start(s32[4]{0:T(128)} %param.11) | copy-start | bytes 52
  31.2 54.4 %collective-permute-start = (bf16[16,16,768]{2,1,0:T(8,128)(2,1)S(1)}, bf16[16,16,768]{2,1,0:T(8,128)(2,1)}, u32[]{:S(2)}, u32[]{:S(2)}) collective-permute-start(bf16[16,16,768]{2,1,0:T(8,128)(2,1)S(1)} %all-to-all-done.2), channel_id=1, source_target_pairs={{0,8},{8,0},{16,24},{24,16},{32,40},{40,32},{48,56},{56,48},{64,72... | collective-permute-start | bytes 1179656 | tf_op jit(solution)/shard_map/ppermute | solution.py:207
  46.7 2.8 %copy-start.4 = (bf16[1024,3072]{1,0:T(8,128)(2,1)S(1)}, bf16[1024,3072]{1,0:T(8,128)(2,1)}, u32[]{:S(2)}) copy-start(bf16[1024,3072]{1,0:T(8,128)(2,1)} %wqkv_hbm.1) | copy-start | bytes 18874372
  49.5 1.4 %copy-start.6 = (bf16[1024,768]{1,0:T(8,128)(2,1)S(1)}, bf16[1024,768]{1,0:T(8,128)(2,1)}, u32[]{:S(2)}) copy-start(bf16[1024,768]{1,0:T(8,128)(2,1)} %wproj_hbm.1) | copy-start | bytes 4718596
  65.2 38.2 %copy-start.2 = (bf16[16,768]{1,0:T(8,128)(2,1)S(1)}, bf16[16,768]{1,0:T(8,128)(2,1)}, u32[]{:S(2)}) copy-start(bf16[16,768]{1,0:T(8,128)(2,1)} %cap_ref.1) | copy-start | bytes 73732
  65.2 11.1 %all-to-all-start.1 = ((f32[8,8,128]{2,1,0:T(8,128)}), f32[8,8,128]{2,1,0:T(8,128)S(1)}, u32[]{:S(2)}, u32[]{:S(2)}) async-start(f32[8,8,128]{2,1,0:T(8,128)} %temporal.1), calls=%async_computation.1 | async-start | bytes 65536 | tf_op jit(solution)/shard_map/all_to_all | solution.py:235
  76.3 0.7 copy-start.7
  76.9 9.8 %copy-start.3 = (f32[4,128]{1,0:T(4,128)S(1)}, f32[4,128]{1,0:T(4,128)}, u32[]{:S(2)}) copy-start(f32[4,128]{1,0:T(4,128)} %broadcast_in_dim.6.positive_ref) | copy-start | bytes 6148
  78.5 18.9 %copy-start.8 = (f32[4,128]{1,0:T(4,128)S(1)}, f32[4,128]{1,0:T(4,128)}, u32[]{:S(2)}) copy-start(f32[4,128]{1,0:T(4,128)} %get-tuple-element.6) | copy-start | bytes 6148
  78.5 24.1 %copy-start.1 = (f32[4,768]{1,0:T(4,128)S(1)}, f32[4,768]{1,0:T(4,128)}, u32[]{:S(2)}) copy-start(f32[4,768]{1,0:T(4,128)} %get-tuple-element.5.unit_ref) | copy-start | bytes 36868
  78.5 19.0 %all-to-all-start.3 = ((f32[16,4,896]{2,1,0:T(4,128)}), f32[16,4,896]{2,1,0:T(4,128)S(1)}, u32[]{:S(2)}, u32[]{:S(2)}) async-start(f32[16,4,896]{2,1,0:T(4,128)} %get-tuple-element.7), calls=%async_computation.3 | async-start | bytes 458752 | tf_op jit(solution)/shard_map/all_to_all | solution.py:237
  86.7 0.7 copy-start
  88.4 3.8 %collective-permute-start.1 = (f32[4,768]{1,0:T(4,128)S(1)}, f32[4,768]{1,0:T(4,128)S(1)}, u32[]{:S(2)}, u32[]{:S(2)}) collective-permute-start(f32[4,768]{1,0:T(4,128)S(1)} %clip_part.1), channel_id=1, source_target_pairs={{0,1},{1,0},{2,3},{3,2},{4,5},{5,4},{6,7},{7,6},{8,9},{9,8},{10,11... | collective-permute-start | bytes 36872 | tf_op jit(solution)/shard_map/ppermute | solution.py:207
  92.2 5.2 %collective-permute-start.2 = (f32[4,768]{1,0:T(4,128)S(1)}, f32[4,768]{1,0:T(4,128)S(1)}, u32[]{:S(2)}, u32[]{:S(2)}) collective-permute-start(f32[4,768]{1,0:T(4,128)S(1)} %add.94), channel_id=1, source_target_pairs={{0,2},{1,3},{2,0},{3,1},{4,6},{5,7},{6,4},{7,5},{8,10},{9,11},{10,... | collective-permute-start | bytes 36872 | tf_op jit(solution)/shard_map/ppermute | solution.py:207
  97.4 5.2 %collective-permute-start.3 = (f32[4,768]{1,0:T(4,128)S(1)}, f32[4,768]{1,0:T(4,128)S(1)}, u32[]{:S(2)}, u32[]{:S(2)}) collective-permute-start(f32[4,768]{1,0:T(4,128)S(1)} %add.95), channel_id=1, source_target_pairs={{0,4},{1,5},{2,6},{3,7},{4,0},{5,1},{6,2},{7,3},{8,12},{9,13},{10,... | collective-permute-start | bytes 36872 | tf_op jit(solution)/shard_map/ppermute | solution.py:207
  97.5 5.9 %collective-permute-start.4 = (f32[16,4,896]{2,1,0:T(4,128)S(1)}, f32[16,4,896]{2,1,0:T(4,128)S(1)}, u32[]{:S(2)}, u32[]{:S(2)}) collective-permute-start(f32[16,4,896]{2,1,0:T(4,128)S(1)} %all-to-all-done.3.units_ref), channel_id=1, source_target_pairs={{0,8},{8,0},{16,24},{24,16},{32,40},{40,32},{48,56},{56,48},{64,72... | collective-permute-start | bytes 688136 | tf_op jit(solution)/shard_map/ppermute | solution.py:207

commit v2 on v1

v2 whole, which is shorter than its diff:
```python
import jax
import jax.numpy as jnp
from jax import lax
from jax.experimental import pallas as pl
from jax.experimental.pallas import tpu as pltpu
from jax.sharding import PartitionSpec as P

D = 1024
E = 768
HEADS = 16
HEAD = D // HEADS
FRAMES = 16
SPATIAL = 64
TOKENS = FRAMES * SPATIAL
LANES = 128
GROUP = 4
WIDTH = GROUP * HEAD
BLOCKS = 4
ROWS = FRAMES * 8

TEMP = 10.0
BIAS = -2.0
EPS = 1e-06
LOG2E = 1.4426950408889634

ANYWHERE = pl.BlockSpec(memory_space=pl.ANY)
IN_VMEM = pl.BlockSpec(memory_space=pltpu.VMEM)

F32 = jnp.float32
BF16 = jnp.bfloat16


def dot(a, b):
    return jnp.dot(a, b, preferred_element_type=F32)


def dot_t(a, b):
    return lax.dot_general(a, b, (((1,), (1,)), ((), ())), preferred_element_type=F32)


def parts_of(value, count):
    terms = []
    for _ in range(count):
        term = value.astype(BF16)
        terms.append(term)
        value = value - term.astype(F32)
    return terms


def temporal_kernel(x_ref, wqkv_hbm, wout_hbm, wproj_hbm, out_ref, wqkv, wout, wproj, sems):
    copies = []

    def bring(source, target, columns):
        copy = pltpu.make_async_copy(source.at[:, columns], target.at[:, columns], sems.at[len(copies)])
        copy.start()
        copies.append(copy)

    for start, width in ((0, WIDTH), (WIDTH, D - WIDTH)):
        bring(wqkv_hbm, wqkv, pl.ds(start, width))
        bring(wqkv_hbm, wqkv, pl.ds(D + start, width))
    bring(wqkv_hbm, wqkv, pl.ds(2 * D, D))
    bring(wout_hbm, wout, pl.ds(0, D))
    bring(wproj_hbm, wproj, pl.ds(0, E))

    x = jnp.concatenate([x_ref[:, 16 * b : 16 * b + 16, :].reshape(ROWS, D) for b in range(BLOCKS)], axis=0)
    lane = lax.broadcasted_iota(jnp.int32, (ROWS, WIDTH), 1) // HEAD
    same = lax.broadcasted_iota(jnp.int32, (8, GROUP * ROWS), 0) == lax.broadcasted_iota(jnp.int32, (8, GROUP * ROWS), 1) % 8
    owner = lax.broadcasted_iota(jnp.int32, (GROUP * ROWS, LANES), 0) // ROWS
    column = lax.broadcasted_iota(jnp.int32, (GROUP * ROWS, LANES), 1)
    weights = jnp.zeros((BLOCKS * ROWS, LANES), F32)
    def project(j):
        query = dot(x, wqkv[:, j * WIDTH : (j + 1) * WIDTH]).astype(BF16)
        keys = dot(x, wqkv[:, D + j * WIDTH : D + (j + 1) * WIDTH]).astype(BF16)
        return query, keys

    def attend(query, keys, b):
        q = query[b * ROWS : (b + 1) * ROWS]
        k = keys[b * ROWS : (b + 1) * ROWS]
        split = jnp.concatenate([jnp.where(lane == h, q, jnp.zeros_like(q)) for h in range(GROUP)], axis=0)
        scores = dot_t(k, split).reshape(FRAMES, 8, GROUP * ROWS)
        top = jnp.max(scores, axis=0, keepdims=True)
        expo = jnp.exp2((scores - top) * (HEAD**-0.5 * LOG2E))
        total = jnp.sum(expo, axis=0, keepdims=True)
        return (expo * jnp.where(same, 1.0 / total, 0.0)).astype(BF16).reshape(ROWS, GROUP * ROWS)

    def place(j):
        return jnp.where(owner + j * GROUP == column, 1.0, 0.0).astype(BF16)

    copies[0].wait()
    copies[1].wait()
    ready = project(0)
    copies[2].wait()
    copies[3].wait()
    for j in range(HEADS // GROUP):
        current = ready
        if j + 1 < HEADS // GROUP:
            ready = project(j + 1)
        probs = [attend(*current, b) for b in range(BLOCKS)]
        weights += dot(jnp.concatenate(probs, axis=0), place(j))
    left = parts_of(weights.T[:HEADS], 2) + [jnp.ones((HEADS, BLOCKS * ROWS), BF16)]
    sums = dot(jnp.concatenate(left, axis=0), x)
    heads = sums[:HEADS] + sums[HEADS : 2 * HEADS]
    rows = sums[2 * HEADS : 2 * HEADS + 1]
    copies[-3].wait()
    values = dot(jnp.concatenate(parts_of(heads, 2), axis=0), wqkv[:, 2 * D :])
    values = values[:HEADS] + values[HEADS:]
    own = lax.broadcasted_iota(jnp.int32, (HEADS, D), 0) == lax.broadcasted_iota(jnp.int32, (HEADS, D), 1) // HEAD
    mixed = jnp.sum(jnp.where(own, values, 0.0), axis=0, keepdims=True)
    copies[-2].wait()
    mixed = jnp.concatenate([jnp.broadcast_to(part, (8, D)) for part in parts_of(mixed, 2)], axis=0)
    layer = dot(mixed, wout[...])
    pooled = (rows + layer[:1] + layer[8:9]) * (1.0 / TOKENS)
    copies[-1].wait()
    pooled = jnp.concatenate([jnp.broadcast_to(part, (8, D)) for part in parts_of(pooled, 3)], axis=0)
    embed = dot(pooled, wproj[...])
    embed = embed[:8] + embed[8:16] + embed[16:24]
    for j in range(E // LANES):
        out_ref[:, j, :] = embed[:, j * LANES : (j + 1) * LANES]
    out_ref[:, E // LANES :, :] = jnp.zeros((8, 8 - E // LANES, LANES), F32)


def temporal(x, w_qkv, w_out, w_proj):
    return pl.pallas_call(
        temporal_kernel,
        out_shape=jax.ShapeDtypeStruct((8, 8, LANES), F32),
        in_specs=[IN_VMEM, ANYWHERE, ANYWHERE, ANYWHERE],
        out_specs=IN_VMEM,
        scratch_shapes=[
            pltpu.VMEM((D, 3 * D), BF16),
            pltpu.VMEM((D, D), BF16),
            pltpu.VMEM((D, E), BF16),
            pltpu.SemaphoreType.DMA((16,)),
        ],
        compiler_params=pltpu.CompilerParams(vmem_limit_bytes=30 << 20),
        cost_estimate=pl.CostEstimate(flops=3 << 30, bytes_accessed=11 << 20, transcendentals=0),
        name="temporal",
    )(
        pltpu.with_memory_space_constraint(x, pltpu.VMEM),
        *(pltpu.with_memory_space_constraint(w, pltpu.HBM) for w in (w_qkv, w_out, w_proj)),
    )


def scale_kernel(*refs):
    out_ref = refs[-1]
    ones = jnp.ones((8, E), BF16)
    rows = refs[0].shape[0]
    for k, ref in enumerate(refs[:-1]):
        squares = ref[...].astype(F32)
        squares = squares * squares
        total = sum(dot_t(ones, part) for part in parts_of(squares, 2))
        out_ref[:, k * rows : (k + 1) * rows] = TEMP / jnp.sqrt(total + EPS)


def caption_scales(pieces):
    return pl.pallas_call(
        scale_kernel,
        out_shape=jax.ShapeDtypeStruct((8, 4 * pieces[0].shape[0]), F32),
        in_specs=[IN_VMEM] * 4,
        out_specs=IN_VMEM,
        compiler_params=pltpu.CompilerParams(vmem_limit_bytes=24 << 20),
        cost_estimate=pl.CostEstimate(flops=20 << 20, bytes_accessed=1 << 20, transcendentals=0),
        name="caption_scales",
    )(*pieces)


def slope(logits, hit):
    sign = jnp.where(hit, 1.0, -1.0)
    return -sign / (1.0 + jnp.exp(sign * logits))


def clip_kernel(parts_ref, *refs):
    pieces, (scale_ref, ids_ref, positive_ref, unit_ref, length_ref, grad_ref) = refs[:4], refs[4:]
    embed = jnp.concatenate(
        [
            jnp.concatenate([parts_ref[2 * c, j : j + 1, :] + parts_ref[2 * c + 1, j : j + 1, :] for j in range(E // LANES)], axis=1)
            for c in range(4)
        ],
        axis=0,
    )
    length = jnp.sqrt(jnp.sum(embed * embed, axis=-1, keepdims=True) + EPS)
    unit = embed / length
    unit_ref[:, :E] = unit
    unit_ref[:, E:] = positive_ref[...]
    length_ref[...] = jnp.broadcast_to(length, length_ref.shape)
    terms = jnp.concatenate(parts_of(unit, 3), axis=0)
    caps = [ref[...] for ref in pieces]
    scale = scale_ref[:1]
    logits = jnp.concatenate([dot_t(terms, cap) for cap in caps], axis=1)
    logits = (logits[:4] + logits[4:8] + logits[8:12]) * scale + BIAS
    weight = slope(logits, ids_ref[...] == positive_ref[:, :1])
    grad = dot(jnp.concatenate(parts_of(weight * scale, 3), axis=0), jnp.concatenate(caps, axis=0))
    grad_ref[...] = grad[:4] + grad[4:8] + grad[8:12]


def clip_part(parts, pieces, scales, ids, positive):
    return pl.pallas_call(
        clip_kernel,
        out_shape=(
            jax.ShapeDtypeStruct((4, E + LANES), F32),
            jax.ShapeDtypeStruct((4, LANES), F32),
            jax.ShapeDtypeStruct((4, E), F32),
        ),
        compiler_params=pltpu.CompilerParams(vmem_limit_bytes=24 << 20),
        cost_estimate=pl.CostEstimate(flops=100 << 20, bytes_accessed=1 << 20, transcendentals=0),
        name="clip_part",
    )(parts, *pieces, scales, ids, positive)


def caption_sum(cap_unit, rows, ids):
    unit = rows[:, :E]
    positive = rows[:, E:].T[:1]
    logits = lax.dot_general(
        cap_unit, unit, (((1,), (1,)), ((), ())), precision=lax.Precision.HIGHEST, preferred_element_type=F32
    )
    weight = slope(TEMP * logits + BIAS, ids[:, : rows.shape[0]] == positive)
    return TEMP * jnp.dot(weight, unit, precision=lax.Precision.HIGHEST, preferred_element_type=F32)


def stacked(ref):
    return jnp.concatenate([ref[g] for g in range(ref.shape[0])], axis=0)


def near_kernel(units_ref, cap_ref, ids_ref, out_ref):
    cap = cap_ref[...].astype(F32)
    length = jnp.sqrt(jnp.sum(cap * cap, axis=-1, keepdims=True) + EPS)
    out_ref[...] = caption_sum(cap / length, stacked(units_ref), ids_ref[...])


def far_kernel(units_ref, part_ref, cap_ref, ids_ref, out_ref):
    cap = cap_ref[...].astype(F32)
    length = jnp.sqrt(jnp.sum(cap * cap, axis=-1, keepdims=True) + EPS)
    cap_unit = cap / length
    grad = part_ref[...] + caption_sum(cap_unit, stacked(units_ref), ids_ref[...])
    out_ref[...] = (grad - cap_unit * jnp.sum(cap_unit * grad, axis=-1, keepdims=True)) / length


def swapped(value, axis, bit):
    return lax.ppermute(value, axis, [(i, i ^ bit) for i in range(lax.axis_size(axis))])


def per_device(video, w_qkv, w_out, w_proj, captions, positive):
    wide = lax.axis_size("wide")
    narrow = lax.axis_size("narrow")
    rank_wide = lax.axis_index("wide")
    rank_narrow = lax.axis_index("narrow")
    cap_rows = captions.shape[0]
    chips = wide // 2
    same_core = [[2 * g + core for g in range(chips)] for core in range(2)]

    send = video.reshape(4, 2, 8, 8, D).transpose(0, 2, 1, 3, 4).reshape(8, 64, D)
    tokens = lax.all_to_all(send, "narrow", 0, 0, tiled=True)

    near = jnp.concatenate([captions, swapped(captions, "wide", 16)], axis=0)
    near = jnp.concatenate([near] + [swapped(near, "wide", bit) for bit in (4, 8, 12)], axis=0)
    source = jnp.stack([rank_wide, rank_wide ^ 16])
    source = jnp.concatenate([source ^ bit for bit in (0, 4, 8, 12)])
    pieces = [near] + [swapped(near, "wide", bit) for bit in (1, 2, 3)]
    source = jnp.concatenate([source ^ bit for bit in range(4)])
    cap_ids = (source[:, None] * narrow + rank_narrow) * cap_rows + jnp.arange(cap_rows, dtype=jnp.int32)[None]
    cap_ids = cap_ids.reshape(1, wide * cap_rows).astype(F32)
    own_ids = (rank_wide * narrow + rank_narrow) * cap_rows + jnp.arange(cap_rows, dtype=jnp.int32)
    own_ids = jnp.broadcast_to(own_ids.astype(F32)[:, None], (cap_rows, LANES))
    positive = jnp.broadcast_to(positive.astype(F32)[:, None], (4, LANES))

    parts = lax.all_to_all(temporal(tokens, w_qkv, w_out, w_proj), "narrow", 0, 0, tiled=True)
    unit, length, grad_unit = clip_part(parts, pieces, caption_scales(pieces), cap_ids, positive)
    outgoing = jnp.broadcast_to(unit[None], (chips, *unit.shape))
    units = lax.all_to_all(outgoing, "wide", 0, 0, axis_index_groups=same_core, tiled=True)
    other = swapped(units, "wide", 1)
    small = pltpu.CompilerParams(vmem_limit_bytes=24 << 20)
    shape = jax.ShapeDtypeStruct(captions.shape, F32)
    part = pl.pallas_call(near_kernel, out_shape=shape, compiler_params=small, name="caption_near")(units, captions, own_ids)
    caption_grad = pl.pallas_call(far_kernel, out_shape=shape, compiler_params=small, name="caption_far")(
        other, part, captions, own_ids
    )
    for bit in (1, 2, 4):
        grad_unit = grad_unit + swapped(grad_unit, "narrow", bit)
    unit = unit[:, :E]
    clip_grad = (grad_unit - unit * jnp.sum(unit * grad_unit, axis=-1, keepdims=True)) / length[:, :1]
    return (clip_grad, caption_grad)


def solution(mesh):
    in_specs = (
        P("wide", "narrow", None, None),
        P(),
        P(),
        P(),
        P(("wide", "narrow"), None),
        P("wide"),
    )
    out_specs = (P("wide", None), P(("wide", "narrow"), None))
    return jax.shard_map(
        per_device, mesh=mesh, in_specs=in_specs, out_specs=out_specs, check_vma=False
    )
```

time: 106 us -> 79.4 us (0.75)
  waiting for transfers between devices: 45.8 us -> 25.9 us
  starting transfers between devices: 28.3 us -> 36.2 us
  Pallas kernels: 18.9 us -> 11.7 us
  local copies, waits for them, and re-layouts: 9.82 us -> 3.57 us
    all_to_all x1, waiting for transfers between devices: 15.4 us -> 0.01 us  [per_device(): tokens = lax.all_to_all(send, 'narrow', 0, 0, tiled=True)]
    ppermute x5 -> x11, starting transfers between devices: 2.05 us -> 15.8 us  [swapped(): lax.ppermute(value, axis, [(i, i ^ bit) for i in range(lax.axis_size(axis...]
    all_to_all x1 -> x0, waiting for transfers between devices: 10.7 us -> none  [per_device(): lax.all_to_all(jnp.broadcast_to(captions[None], (chips, cap_rows, E)), 'w...]
    all_to_all x1 -> x0, starting transfers between devices: 9.94 us -> none  [per_device(): lax.all_to_all(jnp.broadcast_to(captions[None], (chips, cap_rows, E)), 'w...]
    ppermute x5 -> x11, waiting for transfers between devices: 12.1 us -> 18.8 us  [swapped(): lax.ppermute(value, axis, [(i, i ^ bit) for i in range(lax.axis_size(axis...]
    pallas_call x1, Pallas kernels: 14.3 us -> 8.4 us  [temporal(): pl.pallas_call(temporal_kernel, out_shape=jax.ShapeDtypeStruct((8, 8, LAN...]
    unnamed x20 -> x7, local copies, waits for them, and re-layouts: 4.92 us -> 0.02 us
    all_to_all x1, starting transfers between devices: 3.35 us -> 7.14 us  [per_device(): lax.all_to_all(temporal(tokens, w_qkv, w_out, w_proj), 'narrow', 0, 0, ti...]
  transfers between devices with their start and end apart: 9 -> 14, of which waited for: 6 -> 7; matrix products, arithmetic and copies ran while one was open for 5% -> 2% of each run, Pallas kernels for 16% -> 12%
where the time goes in v2:
time: 79.4 us; the launch traced here: 79 us
  starting transfers between devices  36.2 us (46%)
  waiting for transfers between devices  25.9 us (33%)
  Pallas kernels  11.7 us (15%)
  local copies, waits for them, and re-layouts  3.57 us (4%)
  other arithmetic  0.98 us (1%)
    ppermute x11, waiting for transfers between devices, swapped(): lax.ppermute(value, axis, [(i, i ^ bit) for i in range(lax.axis_size(axis...  18.8 us
    ppermute x11, starting transfers between devices, swapped(): lax.ppermute(value, axis, [(i, i ^ bit) for i in range(lax.axis_size(axis...  15.8 us
    pallas_call x1, Pallas kernels, temporal(): pl.pallas_call(temporal_kernel, out_shape=jax.ShapeDtypeStruct((8, 8, LAN...  8.4 us
    all_to_all x1, starting transfers between devices, per_device(): lax.all_to_all(outgoing, 'wide', 0, 0, axis_index_groups=same_core, tiled...  7.24 us
    all_to_all x1, starting transfers between devices, per_device(): lax.all_to_all(temporal(tokens, w_qkv, w_out, w_proj), 'narrow', 0, 0, ti...  7.14 us
    all_to_all x1, waiting for transfers between devices, per_device(): lax.all_to_all(temporal(tokens, w_qkv, w_out, w_proj), 'narrow', 0, 0, ti...  7.04 us
    all_to_all x1, starting transfers between devices, per_device(): tokens = lax.all_to_all(send, 'narrow', 0, 0, tiled=True)  6.03 us
    reshape x1, local copies, waits for them, and re-layouts, per_device(): video.reshape(4, 2, 8, 8, D).transpose(0, 2, 1, 3, 4).reshape(8, 64, D)  2.32 us
  transfers between devices with their start and end apart: 14, of which 7 were waited for; matrix products, arithmetic and copies ran while one was open for 2% of the time, Pallas kernels for 12%

profile of v2, /device:TPU:8, one launch (start us, length us, event | category | flops | bytes accessed | tf_op | source)
XLA Modules:
  0.0 79.0 jit_solution(15724924208925677985)
XLA Ops:
  0.6 2.3 %copy.9 = bf16[4,2,8,8,1024]{4,3,1,2,0:T(8,128)(2,1)} copy(bf16[4,2,8,8,1024]{4,3,2,1,0:T(8,128)(2,1)} %bitcast.6) | data formatting | bytes 2097152 | tf_op jit(solution)/shard_map/reshape | solution.py:250
  3.0 6.0 %all-to-all-start = ((bf16[8,64,1024]{2,1,0:T(8,128)(2,1)}), bf16[8,64,1024]{2,1,0:T(8,128)(2,1)S(1)}, u32[]{:S(2)}, u32[]{:S(2)}) async-start(bf16[8,64,1024]{2,1,0:T(8,128)(2,1)} %bitcast.2), calls=%async_computation | async-start | bytes 2097152 | tf_op jit(solution)/shard_map/all_to_all | solution.py:251
  9.0 7.3 %collective-permute-start = (bf16[16,768]{1,0:T(8,128)(2,1)S(1)}, bf16[16,768]{1,0:T(8,128)(2,1)S(1)}, u32[]{:S(2)}, u32[]{:S(2)}) collective-permute-start(bf16[16,768]{1,0:T(8,128)(2,1)S(1)} %copy-done), channel_id=1, source_target_pairs={{0,128},{8,136},{16,144},{24,152},{32,160},{40,168},{48,176},{56,1... | collective-permute-start | bytes 73736 | tf_op jit(solution)/shard_map/ppermute | solution.py:238
  16.4 0.1 concatenate.40
  16.5 1.5 %collective-permute-done = bf16[16,768]{1,0:T(8,128)(2,1)S(1)} collective-permute-done((bf16[16,768]{1,0:T(8,128)(2,1)S(1)}, bf16[16,768]{1,0:T(8,128)(2,1)S(1)}, u32[]{:S(2)}, u32[]{:S(2)}) %collective-permute-start) | collective-permute-done | bytes 24608 | tf_op jit(solution)/shard_map/ppermute | solution.py:238
  18.1 1.0 %collective-permute-start.1 = (bf16[32,768]{1,0:T(8,128)(2,1)S(1)}, bf16[32,768]{1,0:T(8,128)(2,1)S(1)}, u32[]{:S(2)}, u32[]{:S(2)}) collective-permute-start(bf16[32,768]{1,0:T(8,128)(2,1)S(1)} %get-tuple-element.12), channel_id=1, source_target_pairs={{0,32},{8,40},{16,48},{24,56},{32,0},{40,8},{48,16},{56,24},{64,96... | collective-permute-start | bytes 147464 | tf_op jit(solution)/shard_map/ppermute | solution.py:238
  19.1 2.9 %collective-permute-start.2 = (bf16[32,768]{1,0:T(8,128)(2,1)S(1)}, bf16[32,768]{1,0:T(8,128)(2,1)S(1)}, u32[]{:S(2)}, u32[]{:S(2)}) collective-permute-start(bf16[32,768]{1,0:T(8,128)(2,1)S(1)} %get-tuple-element.12), channel_id=1, source_target_pairs={{0,64},{8,72},{16,80},{24,88},{32,96},{40,104},{48,112},{56,120},{... | collective-permute-start | bytes 147464 | tf_op jit(solution)/shard_map/ppermute | solution.py:238
  22.0 0.5 collective-permute-start.3
  22.5 2.7 %collective-permute-done.2 = bf16[32,768]{1,0:T(8,128)(2,1)S(1)} collective-permute-done((bf16[32,768]{1,0:T(8,128)(2,1)S(1)}, bf16[32,768]{1,0:T(8,128)(2,1)S(1)}, u32[]{:S(2)}, u32[]{:S(2)}) %collective-permute-start.2) | collective-permute-done | bytes 49184 | tf_op jit(solution)/shard_map/ppermute | solution.py:238
  25.2 2.7 %collective-permute-done.3 = bf16[32,768]{1,0:T(8,128)(2,1)S(1)} collective-permute-done((bf16[32,768]{1,0:T(8,128)(2,1)S(1)}, bf16[32,768]{1,0:T(8,128)(2,1)S(1)}, u32[]{:S(2)}, u32[]{:S(2)}) %collective-permute-start.3) | collective-permute-done | bytes 49184 | tf_op jit(solution)/shard_map/ppermute | solution.py:238
  27.9 1.4 %collective-permute-start.5 = (bf16[128,768]{1,0:T(8,128)(2,1)S(1)}, bf16[128,768]{1,0:T(8,128)(2,1)S(1)}, u32[]{:S(2)}, u32[]{:S(2)}) collective-permute-start(bf16[128,768]{1,0:T(8,128)(2,1)S(1)} %constant_dynamic-update-slice_fusion.2.refs_0_), channel_id=1, source_target_pairs={{0,16},{8,24},{16,0},{24,8},{32,48},{40,56},{48,32},{56,40},{64,80... | collective-permute-start | bytes 589832 | tf_op jit(solution)/shard_map/ppermute | solution.py:238
  29.4 0.4 collective-permute-start.6
  29.8 8.4 %temporal.1 = f32[8,8,128]{2,1,0:T(8,128)} custom-call(bf16[8,64,1024]{2,1,0:T(8,128)(2,1)S(1)} %all-to-all-done.x_ref, bf16[1024,3072]{1,0:T(8,128)(2,1)} %wqkv_hbm.1, bf16[1024,1024]{1,0:T(8,128)(2,1)} %wout_hbm.1, bf16[1024,768]{1,0:T(8,128)(2,1)} %wproj_hbm.1), custom_call_target="tpu_custom_call" | custom-call | flops 3221225472 | bytes 11534336 | tf_op jit(solution)/shard_map/temporal/pallas_call | solution.py:123
  38.2 7.1 %all-to-all-start.1 = ((f32[8,8,128]{2,1,0:T(8,128)}), f32[8,8,128]{2,1,0:T(8,128)S(1)}, u32[]{:S(2)}, u32[]{:S(2)}) async-start(f32[8,8,128]{2,1,0:T(8,128)} %temporal.1), calls=%async_computation.1 | async-start | bytes 65536 | tf_op jit(solution)/shard_map/all_to_all | solution.py:265
  45.4 0.1 convert_element_type.16.refs_5_
  45.5 0.5 caption_scales.1.refs_4_
  46.1 7.0 %all-to-all-done.1.parts_ref = f32[8,8,128]{2,1,0:T(8,128)S(1)} async-done(((f32[8,8,128]{2,1,0:T(8,128)}), f32[8,8,128]{2,1,0:T(8,128)S(1)}, u32[]{:S(2)}, u32[]{:S(2)}) %all-to-all-start.1) | async-done | bytes 32800 | tf_op jit(solution)/shard_map/all_to_all | solution.py:265
  53.2 0.6 clip_part.1
  53.8 0.7 broadcast_in_dim.7
  54.5 7.2 %all-to-all-start.2 = ((f32[16,4,896]{2,1,0:T(4,128)}), f32[16,4,896]{2,1,0:T(4,128)S(1)}, u32[]{:S(2)}, u32[]{:S(2)}) async-start(f32[16,4,896]{2,1,0:T(4,128)} %broadcast_in_dim.7), calls=%async_computation.2 | async-start | bytes 458752 | tf_op jit(solution)/shard_map/all_to_all | solution.py:268
  61.8 0.7 collective-permute-start.7
  62.4 3.2 %collective-permute-done.7 = f32[4,768]{1,0:T(4,128)S(1)} collective-permute-done((f32[4,768]{1,0:T(4,128)S(1)}, f32[4,768]{1,0:T(4,128)S(1)}, u32[]{:S(2)}, u32[]{:S(2)}) %collective-permute-start.7) | collective-permute-done | bytes 12320 | tf_op jit(solution)/shard_map/ppermute | solution.py:238
  65.6 1.1 %collective-permute-start.8 = (f32[4,768]{1,0:T(4,128)S(1)}, f32[4,768]{1,0:T(4,128)S(1)}, u32[]{:S(2)}, u32[]{:S(2)}) collective-permute-start(f32[4,768]{1,0:T(4,128)S(1)} %add.60), channel_id=1, source_target_pairs={{0,2},{1,3},{2,0},{3,1},{4,6},{5,7},{6,4},{7,5},{8,10},{9,11},{10,... | collective-permute-start | bytes 36872 | tf_op jit(solution)/shard_map/ppermute | solution.py:238
  66.7 4.1 %collective-permute-done.8 = f32[4,768]{1,0:T(4,128)S(1)} collective-permute-done((f32[4,768]{1,0:T(4,128)S(1)}, f32[4,768]{1,0:T(4,128)S(1)}, u32[]{:S(2)}, u32[]{:S(2)}) %collective-permute-start.8) | collective-permute-done | bytes 12320 | tf_op jit(solution)/shard_map/ppermute | solution.py:238
  70.8 0.4 collective-permute-start.9
  71.3 0.1 slice_reduce_fusion
  71.4 0.1 collective-permute-start.10
  71.5 4.5 %collective-permute-done.9 = f32[4,768]{1,0:T(4,128)S(1)} collective-permute-done((f32[4,768]{1,0:T(4,128)S(1)}, f32[4,768]{1,0:T(4,128)S(1)}, u32[]{:S(2)}, u32[]{:S(2)}) %collective-permute-start.9) | collective-permute-done | bytes 12320 | tf_op jit(solution)/shard_map/ppermute | solution.py:238
  76.0 0.1 multiply_reduce_fusion
  76.1 0.7 subtract_divide_fusion
  76.9 0.7 caption_near.1.part_ref
  77.6 1.4 %caption_far.1 = f32[16,768]{1,0:T(8,128)} custom-call(f32[16,4,896]{2,1,0:T(4,128)S(1)} %collective-permute-done.10.units_ref, f32[16,768]{1,0:T(8,128)S(1)} %caption_near.1.part_ref, bf16[16,768]{1,0:T(8,128)(2,1)S(1)} %copy-done, f32[16,128]{1,0:T(8,128)S(1)} %broadcast_in_dim.8.ids_ref), custom_call_target="tpu_custom_call" | custom-call | tf_op jit(solution)/shard_map/caption_far/pallas_call | solution.py:273
  (29 shorter events, 0.4 us)
Async XLA Ops:
  0.6 8.4 %copy-start = (bf16[16,768]{1,0:T(8,128)(2,1)S(1)}, bf16[16,768]{1,0:T(8,128)(2,1)}, u32[]{:S(2)}) copy-start(bf16[16,768]{1,0:T(8,128)(2,1)} %cap_ref.3) | copy-start | bytes 73732
  3.0 26.8 %all-to-all-start = ((bf16[8,64,1024]{2,1,0:T(8,128)(2,1)}), bf16[8,64,1024]{2,1,0:T(8,128)(2,1)S(1)}, u32[]{:S(2)}, u32[]{:S(2)}) async-start(bf16[8,64,1024]{2,1,0:T(8,128)(2,1)} %bitcast.2), calls=%async_computation | async-start | bytes 2097152 | tf_op jit(solution)/shard_map/all_to_all | solution.py:251
  9.0 9.1 %collective-permute-start = (bf16[16,768]{1,0:T(8,128)(2,1)S(1)}, bf16[16,768]{1,0:T(8,128)(2,1)S(1)}, u32[]{:S(2)}, u32[]{:S(2)}) collective-permute-start(bf16[16,768]{1,0:T(8,128)(2,1)S(1)} %copy-done), channel_id=1, source_target_pairs={{0,128},{8,136},{16,144},{24,152},{32,160},{40,168},{48,176},{56,1... | collective-permute-start | bytes 73736 | tf_op jit(solution)/shard_map/ppermute | solution.py:238
  18.1 4.4 %collective-permute-start.1 = (bf16[32,768]{1,0:T(8,128)(2,1)S(1)}, bf16[32,768]{1,0:T(8,128)(2,1)S(1)}, u32[]{:S(2)}, u32[]{:S(2)}) collective-permute-start(bf16[32,768]{1,0:T(8,128)(2,1)S(1)} %get-tuple-element.12), channel_id=1, source_target_pairs={{0,32},{8,40},{16,48},{24,56},{32,0},{40,8},{48,16},{56,24},{64,96... | collective-permute-start | bytes 147464 | tf_op jit(solution)/shard_map/ppermute | solution.py:238
  19.1 6.0 %collective-permute-start.2 = (bf16[32,768]{1,0:T(8,128)(2,1)S(1)}, bf16[32,768]{1,0:T(8,128)(2,1)S(1)}, u32[]{:S(2)}, u32[]{:S(2)}) collective-permute-start(bf16[32,768]{1,0:T(8,128)(2,1)S(1)} %get-tuple-element.12), channel_id=1, source_target_pairs={{0,64},{8,72},{16,80},{24,88},{32,96},{40,104},{48,112},{56,120},{... | collective-permute-start | bytes 147464 | tf_op jit(solution)/shard_map/ppermute | solution.py:238
  22.0 5.9 %collective-permute-start.3 = (bf16[32,768]{1,0:T(8,128)(2,1)S(1)}, bf16[32,768]{1,0:T(8,128)(2,1)S(1)}, u32[]{:S(2)}, u32[]{:S(2)}) collective-permute-start(bf16[32,768]{1,0:T(8,128)(2,1)S(1)} %get-tuple-element.12), channel_id=1, source_target_pairs={{0,96},{8,104},{16,112},{24,120},{32,64},{40,72},{48,80},{56,88},{... | collective-permute-start | bytes 147464 | tf_op jit(solution)/shard_map/ppermute | solution.py:238
  27.9 17.6 %copy-start.1 = (s32[4]{0:T(128)S(1)}, s32[4]{0:T(128)}, u32[]{:S(2)}) copy-start(s32[4]{0:T(128)} %param.11) | copy-start | bytes 52
  27.9 17.6 %collective-permute-start.4 = (bf16[128,768]{1,0:T(8,128)(2,1)S(1)}, bf16[128,768]{1,0:T(8,128)(2,1)S(1)}, u32[]{:S(2)}, u32[]{:S(2)}) collective-permute-start(bf16[128,768]{1,0:T(8,128)(2,1)S(1)} %constant_dynamic-update-slice_fusion.2.refs_0_), channel_id=1, source_target_pairs={{0,8},{8,0},{16,24},{24,16},{32,40},{40,32},{48,56},{56,48},{64,72... | collective-permute-start | bytes 589832 | tf_op jit(solution)/shard_map/ppermute | solution.py:238
  27.9 17.6 %collective-permute-start.5 = (bf16[128,768]{1,0:T(8,128)(2,1)S(1)}, bf16[128,768]{1,0:T(8,128)(2,1)S(1)}, u32[]{:S(2)}, u32[]{:S(2)}) collective-permute-start(bf16[128,768]{1,0:T(8,128)(2,1)S(1)} %constant_dynamic-update-slice_fusion.2.refs_0_), channel_id=1, source_target_pairs={{0,16},{8,24},{16,0},{24,8},{32,48},{40,56},{48,32},{56,40},{64,80... | collective-permute-start | bytes 589832 | tf_op jit(solution)/shard_map/ppermute | solution.py:238
  29.4 16.2 %collective-permute-start.6 = (bf16[128,768]{1,0:T(8,128)(2,1)S(1)}, bf16[128,768]{1,0:T(8,128)(2,1)S(1)}, u32[]{:S(2)}, u32[]{:S(2)}) collective-permute-start(bf16[128,768]{1,0:T(8,128)(2,1)S(1)} %constant_dynamic-update-slice_fusion.2.refs_0_), channel_id=1, source_target_pairs={{0,24},{8,16},{16,8},{24,0},{32,56},{40,48},{48,40},{56,32},{64,88... | collective-permute-start | bytes 589832 | tf_op jit(solution)/shard_map/ppermute | solution.py:238
  38.2 14.9 %all-to-all-start.1 = ((f32[8,8,128]{2,1,0:T(8,128)}), f32[8,8,128]{2,1,0:T(8,128)S(1)}, u32[]{:S(2)}, u32[]{:S(2)}) async-start(f32[8,8,128]{2,1,0:T(8,128)} %temporal.1), calls=%async_computation.1 | async-start | bytes 65536 | tf_op jit(solution)/shard_map/all_to_all | solution.py:265
  54.5 16.8 %all-to-all-start.2 = ((f32[16,4,896]{2,1,0:T(4,128)}), f32[16,4,896]{2,1,0:T(4,128)S(1)}, u32[]{:S(2)}, u32[]{:S(2)}) async-start(f32[16,4,896]{2,1,0:T(4,128)} %broadcast_in_dim.7), calls=%async_computation.2 | async-start | bytes 458752 | tf_op jit(solution)/shard_map/all_to_all | solution.py:268
  61.8 3.8 %collective-permute-start.7 = (f32[4,768]{1,0:T(4,128)S(1)}, f32[4,768]{1,0:T(4,128)S(1)}, u32[]{:S(2)}, u32[]{:S(2)}) collective-permute-start(f32[4,768]{1,0:T(4,128)S(1)} %get-tuple-element.5), channel_id=1, source_target_pairs={{0,1},{1,0},{2,3},{3,2},{4,5},{5,4},{6,7},{7,6},{8,9},{9,8},{10,11... | collective-permute-start | bytes 36872 | tf_op jit(solution)/shard_map/ppermute | solution.py:238
  65.6 5.2 %collective-permute-start.8 = (f32[4,768]{1,0:T(4,128)S(1)}, f32[4,768]{1,0:T(4,128)S(1)}, u32[]{:S(2)}, u32[]{:S(2)}) collective-permute-start(f32[4,768]{1,0:T(4,128)S(1)} %add.60), channel_id=1, source_target_pairs={{0,2},{1,3},{2,0},{3,1},{4,6},{5,7},{6,4},{7,5},{8,10},{9,11},{10,... | collective-permute-start | bytes 36872 | tf_op jit(solution)/shard_map/ppermute | solution.py:238
  70.8 5.2 %collective-permute-start.9 = (f32[4,768]{1,0:T(4,128)S(1)}, f32[4,768]{1,0:T(4,128)S(1)}, u32[]{:S(2)}, u32[]{:S(2)}) collective-permute-start(f32[4,768]{1,0:T(4,128)S(1)} %add.61), channel_id=1, source_target_pairs={{0,4},{1,5},{2,6},{3,7},{4,0},{5,1},{6,2},{7,3},{8,12},{9,13},{10,... | collective-permute-start | bytes 36872 | tf_op jit(solution)/shard_map/ppermute | solution.py:238
  71.4 6.2 %collective-permute-start.10 = (f32[16,4,896]{2,1,0:T(4,128)S(1)}, f32[16,4,896]{2,1,0:T(4,128)S(1)}, u32[]{:S(2)}, u32[]{:S(2)}) collective-permute-start(f32[16,4,896]{2,1,0:T(4,128)S(1)} %all-to-all-done.2.units_ref), channel_id=1, source_target_pairs={{0,8},{8,0},{16,24},{24,16},{32,40},{40,32},{48,56},{56,48},{64,72... | collective-permute-start | bytes 688136 | tf_op jit(solution)/shard_map/ppermute | solution.py:238

commit v3 on v2

--- a/solution.py
+++ b/solution.py
@@ -1,3 +1,5 @@
+import functools
+
 import jax
 import jax.numpy as jnp
 from jax import lax
@@ -55,7 +57,7 @@
         copy.start()
         copies.append(copy)
 
-    for start, width in ((0, WIDTH), (WIDTH, D - WIDTH)):
+    for start, width in ((0, WIDTH), (WIDTH, WIDTH), (2 * WIDTH, 2 * WIDTH)):
         bring(wqkv_hbm, wqkv, pl.ds(start, width))
         bring(wqkv_hbm, wqkv, pl.ds(D + start, width))
     bring(wqkv_hbm, wqkv, pl.ds(2 * D, D))
@@ -89,10 +91,11 @@
     copies[0].wait()
     copies[1].wait()
     ready = project(0)
-    copies[2].wait()
-    copies[3].wait()
     for j in range(HEADS // GROUP):
         current = ready
+        if j < 2:
+            copies[2 * j + 2].wait()
+            copies[2 * j + 3].wait()
         if j + 1 < HEADS // GROUP:
             ready = project(j + 1)
         probs = [attend(*current, b) for b in range(BLOCKS)]
@@ -122,7 +125,7 @@
 def temporal(x, w_qkv, w_out, w_proj):
     return pl.pallas_call(
         temporal_kernel,
-        out_shape=jax.ShapeDtypeStruct((8, 8, LANES), F32),
+        out_shape=pltpu.HBM((8, 8, LANES), F32),
         in_specs=[IN_VMEM, ANYWHERE, ANYWHERE, ANYWHERE],
         out_specs=IN_VMEM,
         scratch_shapes=[
@@ -140,21 +143,56 @@
     )
 
 
-def scale_kernel(*refs):
-    out_ref = refs[-1]
+def slope(logits, hit):
+    sign = jnp.where(hit, 1.0, -1.0)
+    return -sign / (1.0 + jnp.exp(sign * logits))
+
+
+def caption_ids(shape, dimension, rows, gathered):
+    spot = lax.broadcasted_iota(jnp.int32, shape, dimension)
+    block = spot // rows
+    source = lax.axis_index("wide") * jnp.ones(shape, jnp.int32)
+    if gathered:
+        source = source ^ (block // 8) ^ (block // 2 % 4 * 4) ^ (block % 2 * 16)
+    return (source * lax.axis_size("narrow") + lax.axis_index("narrow")) * rows + spot % rows
+
+
+def inverse_lengths(cap):
     ones = jnp.ones((8, E), BF16)
+    squares = cap.astype(F32)
+    squares = squares * squares
+    total = sum(dot_t(ones, part) for part in parts_of(squares, 2))
+    return 1.0 / jnp.sqrt(total[:1] + EPS)
+
+
+def join_kernel(after_ref, *refs):
     rows = refs[0].shape[0]
     for k, ref in enumerate(refs[:-1]):
-        squares = ref[...].astype(F32)
-        squares = squares * squares
-        total = sum(dot_t(ones, part) for part in parts_of(squares, 2))
-        out_ref[:, k * rows : (k + 1) * rows] = TEMP / jnp.sqrt(total + EPS)
+        refs[-1][k * rows : (k + 1) * rows] = ref[...]
+
+
+def join(after, arrays):
+    rows, columns = arrays[0].shape
+    return pl.pallas_call(
+        join_kernel,
+        out_shape=jax.ShapeDtypeStruct((len(arrays) * rows, columns), arrays[0].dtype),
+        in_specs=[ANYWHERE] + [IN_VMEM] * len(arrays),
+        out_specs=IN_VMEM,
+        compiler_params=pltpu.CompilerParams(vmem_limit_bytes=16 << 20),
+        name="join",
+    )(pltpu.with_memory_space_constraint(after, pltpu.HBM), *arrays)
+
+
+def scale_kernel(*refs):
+    rows = refs[0].shape[0]
+    for k, ref in enumerate(refs[:-1]):
+        refs[-1][:, k * rows : (k + 1) * rows] = TEMP * inverse_lengths(ref[...])
 
 
 def caption_scales(pieces):
     return pl.pallas_call(
         scale_kernel,
-        out_shape=jax.ShapeDtypeStruct((8, 4 * pieces[0].shape[0]), F32),
+        out_shape=jax.ShapeDtypeStruct((1, 4 * pieces[0].shape[0]), F32),
         in_specs=[IN_VMEM] * 4,
         out_specs=IN_VMEM,
         compiler_params=pltpu.CompilerParams(vmem_limit_bytes=24 << 20),
@@ -163,13 +201,8 @@
     )(*pieces)
 
 
-def slope(logits, hit):
-    sign = jnp.where(hit, 1.0, -1.0)
-    return -sign / (1.0 + jnp.exp(sign * logits))
-
-
-def clip_kernel(parts_ref, *refs):
-    pieces, (scale_ref, ids_ref, positive_ref, unit_ref, length_ref, grad_ref) = refs[:4], refs[4:]
+def clip_kernel(rows, positive_ref, parts_ref, scale_ref, *refs):
+    pieces, (unit_ref, length_ref, grad_ref, send_ref) = refs[:4], refs[4:]
     embed = jnp.concatenate(
         [
             jnp.concatenate([parts_ref[2 * c, j : j + 1, :] + parts_ref[2 * c + 1, j : j + 1, :] for j in range(E // LANES)], axis=1)
@@ -179,40 +212,51 @@
     )
     length = jnp.sqrt(jnp.sum(embed * embed, axis=-1, keepdims=True) + EPS)
     unit = embed / length
+    clip = lax.broadcasted_iota(jnp.int32, (4, LANES), 0)
+    positive = jnp.zeros((4, LANES), jnp.int32)
+    for c in range(4):
+        positive = jnp.where(clip == c, positive_ref[c], positive)
     unit_ref[:, :E] = unit
-    unit_ref[:, E:] = positive_ref[...]
+    unit_ref[:, E:] = positive.astype(F32)
     length_ref[...] = jnp.broadcast_to(length, length_ref.shape)
+    for k in range(send_ref.shape[0]):
+        send_ref[k, :, :E] = unit
+        send_ref[k, :, E:] = positive.astype(F32)
     terms = jnp.concatenate(parts_of(unit, 3), axis=0)
     caps = [ref[...] for ref in pieces]
-    scale = scale_ref[:1]
+    scale = scale_ref[...]
     logits = jnp.concatenate([dot_t(terms, cap) for cap in caps], axis=1)
     logits = (logits[:4] + logits[4:8] + logits[8:12]) * scale + BIAS
-    weight = slope(logits, ids_ref[...] == positive_ref[:, :1])
+    weight = slope(logits, caption_ids(logits.shape, 1, rows, True) == positive[:, :1])
     grad = dot(jnp.concatenate(parts_of(weight * scale, 3), axis=0), jnp.concatenate(caps, axis=0))
     grad_ref[...] = grad[:4] + grad[4:8] + grad[8:12]
 
 
-def clip_part(parts, pieces, scales, ids, positive):
+def clip_part(positive, parts, scales, pieces, rows, copies):
     return pl.pallas_call(
-        clip_kernel,
+        functools.partial(clip_kernel, rows),
         out_shape=(
             jax.ShapeDtypeStruct((4, E + LANES), F32),
             jax.ShapeDtypeStruct((4, LANES), F32),
             jax.ShapeDtypeStruct((4, E), F32),
+            pltpu.HBM((copies, 4, E + LANES), F32),
         ),
+        in_specs=[pl.BlockSpec(memory_space=pltpu.SMEM)] + [IN_VMEM] * 6,
+        out_specs=(IN_VMEM,) * 4,
         compiler_params=pltpu.CompilerParams(vmem_limit_bytes=24 << 20),
         cost_estimate=pl.CostEstimate(flops=100 << 20, bytes_accessed=1 << 20, transcendentals=0),
         name="clip_part",
-    )(parts, *pieces, scales, ids, positive)
-
-
-def caption_sum(cap_unit, rows, ids):
+    )(positive, parts, scales, *pieces)
+
+
+def caption_sum(cap_unit, rows):
     unit = rows[:, :E]
     positive = rows[:, E:].T[:1]
     logits = lax.dot_general(
         cap_unit, unit, (((1,), (1,)), ((), ())), precision=lax.Precision.HIGHEST, preferred_element_type=F32
     )
-    weight = slope(TEMP * logits + BIAS, ids[:, : rows.shape[0]] == positive)
+    ids = caption_ids(logits.shape, 0, logits.shape[0], False).astype(F32)
+    weight = slope(TEMP * logits + BIAS, ids == positive)
     return TEMP * jnp.dot(weight, unit, precision=lax.Precision.HIGHEST, preferred_element_type=F32)
 
 
@@ -220,17 +264,17 @@
     return jnp.concatenate([ref[g] for g in range(ref.shape[0])], axis=0)
 
 
-def near_kernel(units_ref, cap_ref, ids_ref, out_ref):
+def near_kernel(units_ref, cap_ref, out_ref):
     cap = cap_ref[...].astype(F32)
     length = jnp.sqrt(jnp.sum(cap * cap, axis=-1, keepdims=True) + EPS)
-    out_ref[...] = caption_sum(cap / length, stacked(units_ref), ids_ref[...])
-
-
-def far_kernel(units_ref, part_ref, cap_ref, ids_ref, out_ref):
+    out_ref[...] = caption_sum(cap / length, stacked(units_ref))
+
+
+def far_kernel(units_ref, part_ref, cap_ref, out_ref):
     cap = cap_ref[...].astype(F32)
     length = jnp.sqrt(jnp.sum(cap * cap, axis=-1, keepdims=True) + EPS)
     cap_unit = cap / length
-    grad = part_ref[...] + caption_sum(cap_unit, stacked(units_ref), ids_ref[...])
+    grad = part_ref[...] + caption_sum(cap_unit, stacked(units_ref))
     out_ref[...] = (grad - cap_unit * jnp.sum(cap_unit * grad, axis=-1, keepdims=True)) / length
 
 
@@ -240,10 +284,6 @@
 
 def per_device(video, w_qkv, w_out, w_proj, captions, positive):
     wide = lax.axis_size("wide")
-    narrow = lax.axis_size("narrow")
-    rank_wide = lax.axis_index("wide")
-    rank_narrow = lax.axis_index("narrow")
-    cap_rows = captions.shape[0]
     chips = wide // 2
     same_core = [[2 * g + core for g in range(chips)] for core in range(2)]
 
@@ -251,30 +291,25 @@
     tokens = lax.all_to_all(send, "narrow", 0, 0, tiled=True)
 
     near = jnp.concatenate([captions, swapped(captions, "wide", 16)], axis=0)
-    near = jnp.concatenate([near] + [swapped(near, "wide", bit) for bit in (4, 8, 12)], axis=0)
-    source = jnp.stack([rank_wide, rank_wide ^ 16])
-    source = jnp.concatenate([source ^ bit for bit in (0, 4, 8, 12)])
+    layers = [near] + [swapped(near, "wide", bit) for bit in (4, 8, 12)]
+
+    parts = temporal(tokens, w_qkv, w_out, w_proj)
+    near = join(parts, layers)
     pieces = [near] + [swapped(near, "wide", bit) for bit in (1, 2, 3)]
-    source = jnp.concatenate([source ^ bit for bit in range(4)])
-    cap_ids = (source[:, None] * narrow + rank_narrow) * cap_rows + jnp.arange(cap_rows, dtype=jnp.int32)[None]
-    cap_ids = cap_ids.reshape(1, wide * cap_rows).astype(F32)
-    own_ids = (rank_wide * narrow + rank_narrow) * cap_rows + jnp.arange(cap_rows, dtype=jnp.int32)
-    own_ids = jnp.broadcast_to(own_ids.astype(F32)[:, None], (cap_rows, LANES))
-    positive = jnp.broadcast_to(positive.astype(F32)[:, None], (4, LANES))
-
-    parts = lax.all_to_all(temporal(tokens, w_qkv, w_out, w_proj), "narrow", 0, 0, tiled=True)
-    unit, length, grad_unit = clip_part(parts, pieces, caption_scales(pieces), cap_ids, positive)
-    outgoing = jnp.broadcast_to(unit[None], (chips, *unit.shape))
+    parts = lax.all_to_all(parts, "narrow", 0, 0, tiled=True)
+    unit, length, grad_unit, outgoing = clip_part(
+        positive, parts, caption_scales(pieces), pieces, captions.shape[0], chips
+    )
     units = lax.all_to_all(outgoing, "wide", 0, 0, axis_index_groups=same_core, tiled=True)
     other = swapped(units, "wide", 1)
     small = pltpu.CompilerParams(vmem_limit_bytes=24 << 20)
     shape = jax.ShapeDtypeStruct(captions.shape, F32)
-    part = pl.pallas_call(near_kernel, out_shape=shape, compiler_params=small, name="caption_near")(units, captions, own_ids)
-    caption_grad = pl.pallas_call(far_kernel, out_shape=shape, compiler_params=small, name="caption_far")(
-        other, part, captions, own_ids
-    )
-    for bit in (1, 2, 4):
-        grad_unit = grad_unit + swapped(grad_unit, "narrow", bit)
+    part = pl.pallas_call(near_kernel, out_shape=shape, compiler_params=small, name="caption_near")(units, captions)
+    caption_grad = pl.pallas_call(far_kernel, out_shape=shape, compiler_params=small, name="caption_far")(other, part, captions)
+
+    others = [swapped(grad_unit, "narrow", bit) for bit in (1, 2, 3)]
+    grad_unit = (grad_unit + others[0]) + (others[1] + others[2])
+    grad_unit = grad_unit + swapped(grad_unit, "narrow", 4)
     unit = unit[:, :E]
     clip_grad = (grad_unit - unit * jnp.sum(unit * grad_unit, axis=-1, keepdims=True)) / length[:, :1]
     return (clip_grad, caption_grad)

time: 79.4 us -> 74.6 us (0.940)
  waiting for transfers between devices: 25.9 us -> 19.4 us
  starting transfers between devices: 36.2 us -> 38.5 us
  local copies, waits for them, and re-layouts: 3.57 us -> 2.43 us
    all_to_all x1, waiting for transfers between devices: 7.04 us -> 1.24 us  [per_device(): parts = lax.all_to_all(parts, 'narrow', 0, 0, tiled=True)]
    ppermute x11 -> x12, waiting for transfers between devices: 18.8 us -> 13.9 us  [swapped(): lax.ppermute(value, axis, [(i, i ^ bit) for i in range(lax.axis_size(axis...]
    all_to_all x1, starting transfers between devices: 7.14 us -> 3.41 us  [per_device(): parts = lax.all_to_all(parts, 'narrow', 0, 0, tiled=True)]
    all_to_all x1, waiting for transfers between devices: 0.01 us -> 3.72 us  [per_device(): tokens = lax.all_to_all(send, 'narrow', 0, 0, tiled=True)]
    ppermute x11 -> x12, starting transfers between devices: 15.8 us -> 19.2 us  [swapped(): lax.ppermute(value, axis, [(i, i ^ bit) for i in range(lax.axis_size(axis...]
    all_to_all x1, starting transfers between devices: 7.24 us -> 9.82 us  [per_device(): lax.all_to_all(outgoing, 'wide', 0, 0, axis_index_groups=same_core, tiled...]
    broadcast_in_dim x3 -> x0, local copies, waits for them, and re-layouts: 0.87 us -> none  [the longest x1 0.73 us: per_device(): outgoing = jnp.broadcast_to(unit[None], (chips, *unit.shape))]
    pallas_call x3 -> x4, Pallas kernels: 9.56 us -> 10.2 us  [the longest x1 8.29 us: temporal(): pl.pallas_call(temporal_kernel, out_shape=pltpu.HBM((8, 8, LANES), F32),...]
  transfers between devices with their start and end apart: 14 -> 15, of which waited for: 7 -> 10; matrix products, arithmetic and copies ran while one was open for 2% -> 1% of each run, Pallas kernels for 12% -> 13%
where the time goes in v3:
time: 74.6 us; the launch traced here: 74.2 us
  starting transfers between devices  38.5 us (52%)
  waiting for transfers between devices  19.4 us (26%)
  Pallas kernels  12.4 us (17%)
  local copies, waits for them, and re-layouts  2.43 us (3%)
  other arithmetic  0.81 us (1%)
    ppermute x12, starting transfers between devices, swapped(): lax.ppermute(value, axis, [(i, i ^ bit) for i in range(lax.axis_size(axis...  19.2 us
    ppermute x12, waiting for transfers between devices, swapped(): lax.ppermute(value, axis, [(i, i ^ bit) for i in range(lax.axis_size(axis...  13.9 us
    all_to_all x1, starting transfers between devices, per_device(): lax.all_to_all(outgoing, 'wide', 0, 0, axis_index_groups=same_core, tiled...  9.82 us
    pallas_call x1, Pallas kernels, temporal(): pl.pallas_call(temporal_kernel, out_shape=pltpu.HBM((8, 8, LANES), F32),...  8.29 us
    all_to_all x1, starting transfers between devices, per_device(): tokens = lax.all_to_all(send, 'narrow', 0, 0, tiled=True)  6.03 us
    all_to_all x1, waiting for transfers between devices, per_device(): tokens = lax.all_to_all(send, 'narrow', 0, 0, tiled=True)  3.72 us
    all_to_all x1, starting transfers between devices, per_device(): parts = lax.all_to_all(parts, 'narrow', 0, 0, tiled=True)  3.41 us
    reshape x1, local copies, waits for them, and re-layouts, per_device(): video.reshape(4, 2, 8, 8, D).transpose(0, 2, 1, 3, 4).reshape(8, 64, D)  2.3 us
  transfers between devices with their start and end apart: 15, of which 10 were waited for; matrix products, arithmetic and copies ran while one was open for 1% of the time, Pallas kernels for 13%

profile of v3, /device:TPU:8, one launch (start us, length us, event | category | flops | bytes accessed | tf_op | source)
XLA Modules:
  0.0 74.2 jit_solution(2355044793327033712)
XLA Ops:
  0.6 2.3 %copy.9 = bf16[4,2,8,8,1024]{4,3,1,2,0:T(8,128)(2,1)} copy(bf16[4,2,8,8,1024]{4,3,2,1,0:T(8,128)(2,1)} %bitcast.4) | data formatting | bytes 2097152 | tf_op jit(solution)/shard_map/reshape | solution.py:290
  2.9 6.0 %all-to-all-start = ((bf16[8,64,1024]{2,1,0:T(8,128)(2,1)}), bf16[8,64,1024]{2,1,0:T(8,128)(2,1)S(1)}, u32[]{:S(2)}, u32[]{:S(2)}) async-start(bf16[8,64,1024]{2,1,0:T(8,128)(2,1)} %bitcast.2), calls=%async_computation | async-start | bytes 2097152 | tf_op jit(solution)/shard_map/all_to_all | solution.py:291
  9.0 7.3 %collective-permute-start = (bf16[16,768]{1,0:T(8,128)(2,1)S(1)}, bf16[16,768]{1,0:T(8,128)(2,1)S(1)}, u32[]{:S(2)}, u32[]{:S(2)}) collective-permute-start(bf16[16,768]{1,0:T(8,128)(2,1)S(1)} %copy-done), channel_id=1, source_target_pairs={{0,128},{8,136},{16,144},{24,152},{32,160},{40,168},{48,176},{56,1... | collective-permute-start | bytes 73736 | tf_op jit(solution)/shard_map/ppermute | solution.py:282
  16.3 1.8 %collective-permute-done = bf16[16,768]{1,0:T(8,128)(2,1)S(1)} collective-permute-done((bf16[16,768]{1,0:T(8,128)(2,1)S(1)}, bf16[16,768]{1,0:T(8,128)(2,1)S(1)}, u32[]{:S(2)}, u32[]{:S(2)}) %collective-permute-start) | collective-permute-done | bytes 24608 | tf_op jit(solution)/shard_map/ppermute | solution.py:282
  18.1 1.0 %collective-permute-start.1 = (bf16[32,768]{1,0:T(8,128)(2,1)S(1)}, bf16[32,768]{1,0:T(8,128)(2,1)S(1)}, u32[]{:S(2)}, u32[]{:S(2)}) collective-permute-start(bf16[32,768]{1,0:T(8,128)(2,1)S(1)} %constant_dynamic-update-slice_fusion.refs_0_), channel_id=1, source_target_pairs={{0,32},{8,40},{16,48},{24,56},{32,0},{40,8},{48,16},{56,24},{64,96... | collective-permute-start | bytes 147464 | tf_op jit(solution)/shard_map/ppermute | solution.py:282
  19.1 2.9 %collective-permute-start.2 = (bf16[32,768]{1,0:T(8,128)(2,1)S(1)}, bf16[32,768]{1,0:T(8,128)(2,1)S(1)}, u32[]{:S(2)}, u32[]{:S(2)}) collective-permute-start(bf16[32,768]{1,0:T(8,128)(2,1)S(1)} %constant_dynamic-update-slice_fusion.refs_0_), channel_id=1, source_target_pairs={{0,64},{8,72},{16,80},{24,88},{32,96},{40,104},{48,112},{56,120},{... | collective-permute-start | bytes 147464 | tf_op jit(solution)/shard_map/ppermute | solution.py:282
  22.0 0.5 collective-permute-start.3
  22.5 3.7 %all-to-all-done.x_ref = bf16[8,64,1024]{2,1,0:T(8,128)(2,1)S(1)} async-done(((bf16[8,64,1024]{2,1,0:T(8,128)(2,1)}), bf16[8,64,1024]{2,1,0:T(8,128)(2,1)S(1)}, u32[]{:S(2)}, u32[]{:S(2)}) %all-to-all-start) | async-done | bytes 1048608 | tf_op jit(solution)/shard_map/all_to_all | solution.py:291
  26.2 8.3 %temporal.1.after_ref = f32[8,8,128]{2,1,0:T(8,128)} custom-call(bf16[8,64,1024]{2,1,0:T(8,128)(2,1)S(1)} %all-to-all-done.x_ref, bf16[1024,3072]{1,0:T(8,128)(2,1)} %wqkv_hbm.1, bf16[1024,1024]{1,0:T(8,128)(2,1)} %wout_hbm.1, bf16[1024,768]{1,0:T(8,128)(2,1)} %wproj_hbm.1), custom_call_target="tpu_custom_call" | custom-call | flops 3221225472 | bytes 11534336 | tf_op jit(solution)/shard_map/temporal/pallas_call | solution.py:126
  34.6 1.4 %collective-permute-start.5 = (bf16[128,768]{1,0:T(8,128)(2,1)S(1)}, bf16[128,768]{1,0:T(8,128)(2,1)S(1)}, u32[]{:S(2)}, u32[]{:S(2)}) collective-permute-start(bf16[128,768]{1,0:T(8,128)(2,1)S(1)} %join.1.refs_0_), channel_id=1, source_target_pairs={{0,16},{8,24},{16,0},{24,8},{32,48},{40,56},{48,32},{56,40},{64,80... | collective-permute-start | bytes 589832 | tf_op jit(solution)/shard_map/ppermute | solution.py:282
  36.1 0.4 collective-permute-start.6
  36.5 3.4 %all-to-all-start.1 = ((f32[8,8,128]{2,1,0:T(8,128)}), f32[8,8,128]{2,1,0:T(8,128)S(1)}, u32[]{:S(2)}, u32[]{:S(2)}) async-start(f32[8,8,128]{2,1,0:T(8,128)} %temporal.1.after_ref), calls=%async_computation.1 | async-start | bytes 65536 | tf_op jit(solution)/shard_map/all_to_all | solution.py:299
  39.9 2.5 %collective-permute-done.5.refs_2_ = bf16[128,768]{1,0:T(8,128)(2,1)S(1)} collective-permute-done((bf16[128,768]{1,0:T(8,128)(2,1)S(1)}, bf16[128,768]{1,0:T(8,128)(2,1)S(1)}, u32[]{:S(2)}, u32[]{:S(2)}) %collective-permute-start.5) | collective-permute-done | bytes 196640 | tf_op jit(solution)/shard_map/ppermute | solution.py:282
  42.4 3.5 %collective-permute-done.6.refs_3_ = bf16[128,768]{1,0:T(8,128)(2,1)S(1)} collective-permute-done((bf16[128,768]{1,0:T(8,128)(2,1)S(1)}, bf16[128,768]{1,0:T(8,128)(2,1)S(1)}, u32[]{:S(2)}, u32[]{:S(2)}) %collective-permute-start.6) | collective-permute-done | bytes 196640 | tf_op jit(solution)/shard_map/ppermute | solution.py:282
  45.9 0.5 caption_scales.1.scale_ref
  46.4 1.2 %all-to-all-done.1.parts_ref = f32[8,8,128]{2,1,0:T(8,128)S(1)} async-done(((f32[8,8,128]{2,1,0:T(8,128)}), f32[8,8,128]{2,1,0:T(8,128)S(1)}, u32[]{:S(2)}, u32[]{:S(2)}) %all-to-all-start.1) | async-done | bytes 32800 | tf_op jit(solution)/shard_map/all_to_all | solution.py:299
  47.7 1.4 %clip_part.1 = (f32[4,896]{1,0:T(4,128)S(1)}, f32[4,128]{1,0:T(4,128)S(1)}, f32[4,768]{1,0:T(4,128)S(1)}, f32[16,4,896]{2,1,0:T(4,128)}) custom-call(s32[4]{0:T(128)S(1)} %copy-done.1, f32[8,8,128]{2,1,0:T(8,128)S(1)} %all-to-all-done.1.parts_ref, f32[1,512]{1,0:T(1,128)S(1)} %caption_scales.1.scale_ref, bf16[128,768]{1,0:T(8,128)(2,1)S(1)} %join.1.refs_0_, ...), custom_call_target="tpu_custom_call" | custom-call | flops 104857600 | bytes 1048576 | tf_op jit(solution)/shard_map/clip_part/pallas_call | solution.py:236
  49.1 9.8 %all-to-all-start.2 = ((f32[16,4,896]{2,1,0:T(4,128)}), f32[16,4,896]{2,1,0:T(4,128)S(1)}, u32[]{:S(2)}, u32[]{:S(2)}) async-start(f32[16,4,896]{2,1,0:T(4,128)} %get-tuple-element.9), calls=%async_computation.2 | async-start | bytes 458752 | tf_op jit(solution)/shard_map/all_to_all | solution.py:303
  58.9 1.2 %collective-permute-start.8 = (f32[4,768]{1,0:T(4,128)S(1)}, f32[4,768]{1,0:T(4,128)S(1)}, u32[]{:S(2)}, u32[]{:S(2)}) collective-permute-start(f32[4,768]{1,0:T(4,128)S(1)} %get-tuple-element.6), channel_id=1, source_target_pairs={{0,2},{1,3},{2,0},{3,1},{4,6},{5,7},{6,4},{7,5},{8,10},{9,11},{10,... | collective-permute-start | bytes 36872 | tf_op jit(solution)/shard_map/ppermute | solution.py:282
  60.1 2.2 %collective-permute-start.9 = (f32[4,768]{1,0:T(4,128)S(1)}, f32[4,768]{1,0:T(4,128)S(1)}, u32[]{:S(2)}, u32[]{:S(2)}) collective-permute-start(f32[4,768]{1,0:T(4,128)S(1)} %get-tuple-element.6), channel_id=1, source_target_pairs={{0,3},{1,2},{2,1},{3,0},{4,7},{5,6},{6,5},{7,4},{8,11},{9,10},{10,... | collective-permute-start | bytes 36872 | tf_op jit(solution)/shard_map/ppermute | solution.py:282
  62.2 0.2 collective-permute-start.7
  62.4 1.7 %collective-permute-done.8 = f32[4,768]{1,0:T(4,128)S(1)} collective-permute-done((f32[4,768]{1,0:T(4,128)S(1)}, f32[4,768]{1,0:T(4,128)S(1)}, u32[]{:S(2)}, u32[]{:S(2)}) %collective-permute-start.8) | collective-permute-done | bytes 12320 | tf_op jit(solution)/shard_map/ppermute | solution.py:282
  64.1 0.9 %collective-permute-done.9 = f32[4,768]{1,0:T(4,128)S(1)} collective-permute-done((f32[4,768]{1,0:T(4,128)S(1)}, f32[4,768]{1,0:T(4,128)S(1)}, u32[]{:S(2)}, u32[]{:S(2)}) %collective-permute-start.9) | collective-permute-done | bytes 12320 | tf_op jit(solution)/shard_map/ppermute | solution.py:282
  65.0 0.9 %collective-permute-done.7 = f32[4,768]{1,0:T(4,128)S(1)} collective-permute-done((f32[4,768]{1,0:T(4,128)S(1)}, f32[4,768]{1,0:T(4,128)S(1)}, u32[]{:S(2)}, u32[]{:S(2)}) %collective-permute-start.7) | collective-permute-done | bytes 12320 | tf_op jit(solution)/shard_map/ppermute | solution.py:282
  66.0 2.1 %collective-permute-start.10 = (f32[4,768]{1,0:T(4,128)S(1)}, f32[4,768]{1,0:T(4,128)S(1)}, u32[]{:S(2)}, u32[]{:S(2)}) collective-permute-start(f32[4,768]{1,0:T(4,128)S(1)} %add_add_fusion), channel_id=1, source_target_pairs={{0,4},{1,5},{2,6},{3,7},{4,0},{5,1},{6,2},{7,3},{8,12},{9,13},{10,... | collective-permute-start | bytes 36872 | tf_op jit(solution)/shard_map/ppermute | solution.py:282
  68.1 0.1 slice_reduce_fusion
  68.2 0.5 all-to-all-done.2.units_ref
  68.7 2.5 %collective-permute-done.10 = f32[4,768]{1,0:T(4,128)S(1)} collective-permute-done((f32[4,768]{1,0:T(4,128)S(1)}, f32[4,768]{1,0:T(4,128)S(1)}, u32[]{:S(2)}, u32[]{:S(2)}) %collective-permute-start.10) | collective-permute-done | bytes 12320 | tf_op jit(solution)/shard_map/ppermute | solution.py:282
  71.2 0.1 multiply_reduce_fusion
  71.4 0.7 subtract_divide_fusion
  72.0 0.7 caption_near.1.part_ref
  72.8 1.4 %caption_far.1 = f32[16,768]{1,0:T(8,128)} custom-call(f32[16,4,896]{2,1,0:T(4,128)S(1)} %collective-permute-done.11.units_ref, f32[16,768]{1,0:T(8,128)S(1)} %caption_near.1.part_ref, bf16[16,768]{1,0:T(8,128)(2,1)S(1)} %copy-done), custom_call_target="tpu_custom_call" | custom-call | tf_op jit(solution)/shard_map/caption_far/pallas_call | solution.py:308
  (15 shorter events, 0.1 us)
Async XLA Ops:
  0.6 8.3 %copy-start = (bf16[16,768]{1,0:T(8,128)(2,1)S(1)}, bf16[16,768]{1,0:T(8,128)(2,1)}, u32[]{:S(2)}) copy-start(bf16[16,768]{1,0:T(8,128)(2,1)} %cap_ref.3) | copy-start | bytes 73732
  2.9 23.2 %all-to-all-start = ((bf16[8,64,1024]{2,1,0:T(8,128)(2,1)}), bf16[8,64,1024]{2,1,0:T(8,128)(2,1)S(1)}, u32[]{:S(2)}, u32[]{:S(2)}) async-start(bf16[8,64,1024]{2,1,0:T(8,128)(2,1)} %bitcast.2), calls=%async_computation | async-start | bytes 2097152 | tf_op jit(solution)/shard_map/all_to_all | solution.py:291
  9.0 9.1 %collective-permute-start = (bf16[16,768]{1,0:T(8,128)(2,1)S(1)}, bf16[16,768]{1,0:T(8,128)(2,1)S(1)}, u32[]{:S(2)}, u32[]{:S(2)}) collective-permute-start(bf16[16,768]{1,0:T(8,128)(2,1)S(1)} %copy-done), channel_id=1, source_target_pairs={{0,128},{8,136},{16,144},{24,152},{32,160},{40,168},{48,176},{56,1... | collective-permute-start | bytes 73736 | tf_op jit(solution)/shard_map/ppermute | solution.py:282
  18.1 29.6 %copy-start.1 = (s32[4]{0:T(128)S(1)}, s32[4]{0:T(128)}, u32[]{:S(2)}) copy-start(s32[4]{0:T(128)} %positive_ref.1) | copy-start | bytes 52
  18.1 16.4 %collective-permute-start.1 = (bf16[32,768]{1,0:T(8,128)(2,1)S(1)}, bf16[32,768]{1,0:T(8,128)(2,1)S(1)}, u32[]{:S(2)}, u32[]{:S(2)}) collective-permute-start(bf16[32,768]{1,0:T(8,128)(2,1)S(1)} %constant_dynamic-update-slice_fusion.refs_0_), channel_id=1, source_target_pairs={{0,32},{8,40},{16,48},{24,56},{32,0},{40,8},{48,16},{56,24},{64,96... | collective-permute-start | bytes 147464 | tf_op jit(solution)/shard_map/ppermute | solution.py:282
  19.1 15.4 %collective-permute-start.2 = (bf16[32,768]{1,0:T(8,128)(2,1)S(1)}, bf16[32,768]{1,0:T(8,128)(2,1)S(1)}, u32[]{:S(2)}, u32[]{:S(2)}) collective-permute-start(bf16[32,768]{1,0:T(8,128)(2,1)S(1)} %constant_dynamic-update-slice_fusion.refs_0_), channel_id=1, source_target_pairs={{0,64},{8,72},{16,80},{24,88},{32,96},{40,104},{48,112},{56,120},{... | collective-permute-start | bytes 147464 | tf_op jit(solution)/shard_map/ppermute | solution.py:282
  22.0 12.5 %collective-permute-start.3 = (bf16[32,768]{1,0:T(8,128)(2,1)S(1)}, bf16[32,768]{1,0:T(8,128)(2,1)S(1)}, u32[]{:S(2)}, u32[]{:S(2)}) collective-permute-start(bf16[32,768]{1,0:T(8,128)(2,1)S(1)} %constant_dynamic-update-slice_fusion.refs_0_), channel_id=1, source_target_pairs={{0,96},{8,104},{16,112},{24,120},{32,64},{40,72},{48,80},{56,88},{... | collective-permute-start | bytes 147464 | tf_op jit(solution)/shard_map/ppermute | solution.py:282
  34.5 5.4 %collective-permute-start.4 = (bf16[128,768]{1,0:T(8,128)(2,1)S(1)}, bf16[128,768]{1,0:T(8,128)(2,1)S(1)}, u32[]{:S(2)}, u32[]{:S(2)}) collective-permute-start(bf16[128,768]{1,0:T(8,128)(2,1)S(1)} %join.1.refs_0_), channel_id=1, source_target_pairs={{0,8},{8,0},{16,24},{24,16},{32,40},{40,32},{48,56},{56,48},{64,72... | collective-permute-start | bytes 589832 | tf_op jit(solution)/shard_map/ppermute | solution.py:282
  34.6 7.8 %collective-permute-start.5 = (bf16[128,768]{1,0:T(8,128)(2,1)S(1)}, bf16[128,768]{1,0:T(8,128)(2,1)S(1)}, u32[]{:S(2)}, u32[]{:S(2)}) collective-permute-start(bf16[128,768]{1,0:T(8,128)(2,1)S(1)} %join.1.refs_0_), channel_id=1, source_target_pairs={{0,16},{8,24},{16,0},{24,8},{32,48},{40,56},{48,32},{56,40},{64,80... | collective-permute-start | bytes 589832 | tf_op jit(solution)/shard_map/ppermute | solution.py:282
  36.1 9.8 %collective-permute-start.6 = (bf16[128,768]{1,0:T(8,128)(2,1)S(1)}, bf16[128,768]{1,0:T(8,128)(2,1)S(1)}, u32[]{:S(2)}, u32[]{:S(2)}) collective-permute-start(bf16[128,768]{1,0:T(8,128)(2,1)S(1)} %join.1.refs_0_), channel_id=1, source_target_pairs={{0,24},{8,16},{16,8},{24,0},{32,56},{40,48},{48,40},{56,32},{64,88... | collective-permute-start | bytes 589832 | tf_op jit(solution)/shard_map/ppermute | solution.py:282
  36.5 11.2 %all-to-all-start.1 = ((f32[8,8,128]{2,1,0:T(8,128)}), f32[8,8,128]{2,1,0:T(8,128)S(1)}, u32[]{:S(2)}, u32[]{:S(2)}) async-start(f32[8,8,128]{2,1,0:T(8,128)} %temporal.1.after_ref), calls=%async_computation.1 | async-start | bytes 65536 | tf_op jit(solution)/shard_map/all_to_all | solution.py:299
  49.1 19.6 %all-to-all-start.2 = ((f32[16,4,896]{2,1,0:T(4,128)}), f32[16,4,896]{2,1,0:T(4,128)S(1)}, u32[]{:S(2)}, u32[]{:S(2)}) async-start(f32[16,4,896]{2,1,0:T(4,128)} %get-tuple-element.9), calls=%async_computation.2 | async-start | bytes 458752 | tf_op jit(solution)/shard_map/all_to_all | solution.py:303
  58.9 5.2 %collective-permute-start.8 = (f32[4,768]{1,0:T(4,128)S(1)}, f32[4,768]{1,0:T(4,128)S(1)}, u32[]{:S(2)}, u32[]{:S(2)}) collective-permute-start(f32[4,768]{1,0:T(4,128)S(1)} %get-tuple-element.6), channel_id=1, source_target_pairs={{0,2},{1,3},{2,0},{3,1},{4,6},{5,7},{6,4},{7,5},{8,10},{9,11},{10,... | collective-permute-start | bytes 36872 | tf_op jit(solution)/shard_map/ppermute | solution.py:282
  60.1 4.9 %collective-permute-start.9 = (f32[4,768]{1,0:T(4,128)S(1)}, f32[4,768]{1,0:T(4,128)S(1)}, u32[]{:S(2)}, u32[]{:S(2)}) collective-permute-start(f32[4,768]{1,0:T(4,128)S(1)} %get-tuple-element.6), channel_id=1, source_target_pairs={{0,3},{1,2},{2,1},{3,0},{4,7},{5,6},{6,5},{7,4},{8,11},{9,10},{10,... | collective-permute-start | bytes 36872 | tf_op jit(solution)/shard_map/ppermute | solution.py:282
  62.2 3.7 %collective-permute-start.7 = (f32[4,768]{1,0:T(4,128)S(1)}, f32[4,768]{1,0:T(4,128)S(1)}, u32[]{:S(2)}, u32[]{:S(2)}) collective-permute-start(f32[4,768]{1,0:T(4,128)S(1)} %get-tuple-element.6), channel_id=1, source_target_pairs={{0,1},{1,0},{2,3},{3,2},{4,5},{5,4},{6,7},{7,6},{8,9},{9,8},{10,11... | collective-permute-start | bytes 36872 | tf_op jit(solution)/shard_map/ppermute | solution.py:282
  66.0 5.3 %collective-permute-start.10 = (f32[4,768]{1,0:T(4,128)S(1)}, f32[4,768]{1,0:T(4,128)S(1)}, u32[]{:S(2)}, u32[]{:S(2)}) collective-permute-start(f32[4,768]{1,0:T(4,128)S(1)} %add_add_fusion), channel_id=1, source_target_pairs={{0,4},{1,5},{2,6},{3,7},{4,0},{5,1},{6,2},{7,3},{8,12},{9,13},{10,... | collective-permute-start | bytes 36872 | tf_op jit(solution)/shard_map/ppermute | solution.py:282
  68.7 4.0 %collective-permute-start.11 = (f32[16,4,896]{2,1,0:T(4,128)S(1)}, f32[16,4,896]{2,1,0:T(4,128)S(1)}, u32[]{:S(2)}, u32[]{:S(2)}) collective-permute-start(f32[16,4,896]{2,1,0:T(4,128)S(1)} %all-to-all-done.2.units_ref), channel_id=1, source_target_pairs={{0,8},{8,0},{16,24},{24,16},{32,40},{40,32},{48,56},{56,48},{64,72... | collective-permute-start | bytes 688136 | tf_op jit(solution)/shard_map/ppermute | solution.py:282

commit v4 on v3

--- a/solution.py
+++ b/solution.py
@@ -125,7 +125,7 @@
 def temporal(x, w_qkv, w_out, w_proj):
     return pl.pallas_call(
         temporal_kernel,
-        out_shape=pltpu.HBM((8, 8, LANES), F32),
+        out_shape=pltpu.VMEM((8, 8, LANES), F32),
         in_specs=[IN_VMEM, ANYWHERE, ANYWHERE, ANYWHERE],
         out_specs=IN_VMEM,
         scratch_shapes=[
@@ -153,7 +153,7 @@
     block = spot // rows
     source = lax.axis_index("wide") * jnp.ones(shape, jnp.int32)
     if gathered:
-        source = source ^ (block // 8) ^ (block // 2 % 4 * 4) ^ (block % 2 * 16)
+        source = source ^ (block // 8 % 2 * 2) ^ (block // 16) ^ (block // 2 % 4 * 4) ^ (block % 2 * 16)
     return (source * lax.axis_size("narrow") + lax.axis_index("narrow")) * rows + spot % rows
 
 
@@ -180,29 +180,10 @@
         out_specs=IN_VMEM,
         compiler_params=pltpu.CompilerParams(vmem_limit_bytes=16 << 20),
         name="join",
-    )(pltpu.with_memory_space_constraint(after, pltpu.HBM), *arrays)
-
-
-def scale_kernel(*refs):
-    rows = refs[0].shape[0]
-    for k, ref in enumerate(refs[:-1]):
-        refs[-1][:, k * rows : (k + 1) * rows] = TEMP * inverse_lengths(ref[...])
-
-
-def caption_scales(pieces):
-    return pl.pallas_call(
-        scale_kernel,
-        out_shape=jax.ShapeDtypeStruct((1, 4 * pieces[0].shape[0]), F32),
-        in_specs=[IN_VMEM] * 4,
-        out_specs=IN_VMEM,
-        compiler_params=pltpu.CompilerParams(vmem_limit_bytes=24 << 20),
-        cost_estimate=pl.CostEstimate(flops=20 << 20, bytes_accessed=1 << 20, transcendentals=0),
-        name="caption_scales",
-    )(*pieces)
-
-
-def clip_kernel(rows, positive_ref, parts_ref, scale_ref, *refs):
-    pieces, (unit_ref, length_ref, grad_ref, send_ref) = refs[:4], refs[4:]
+    )(after, *arrays)
+
+
+def unit_kernel(positive_ref, parts_ref, unit_ref, length_ref, send_ref):
     embed = jnp.concatenate(
         [
             jnp.concatenate([parts_ref[2 * c, j : j + 1, :] + parts_ref[2 * c + 1, j : j + 1, :] for j in range(E // LANES)], axis=1)
@@ -212,41 +193,52 @@
     )
     length = jnp.sqrt(jnp.sum(embed * embed, axis=-1, keepdims=True) + EPS)
     unit = embed / length
-    clip = lax.broadcasted_iota(jnp.int32, (4, LANES), 0)
-    positive = jnp.zeros((4, LANES), jnp.int32)
-    for c in range(4):
-        positive = jnp.where(clip == c, positive_ref[c], positive)
+    positive = positive_ref[...]
     unit_ref[:, :E] = unit
-    unit_ref[:, E:] = positive.astype(F32)
+    unit_ref[:, E:] = positive
     length_ref[...] = jnp.broadcast_to(length, length_ref.shape)
     for k in range(send_ref.shape[0]):
         send_ref[k, :, :E] = unit
-        send_ref[k, :, E:] = positive.astype(F32)
-    terms = jnp.concatenate(parts_of(unit, 3), axis=0)
-    caps = [ref[...] for ref in pieces]
-    scale = scale_ref[...]
-    logits = jnp.concatenate([dot_t(terms, cap) for cap in caps], axis=1)
-    logits = (logits[:4] + logits[4:8] + logits[8:12]) * scale + BIAS
-    weight = slope(logits, caption_ids(logits.shape, 1, rows, True) == positive[:, :1])
-    grad = dot(jnp.concatenate(parts_of(weight * scale, 3), axis=0), jnp.concatenate(caps, axis=0))
-    grad_ref[...] = grad[:4] + grad[4:8] + grad[8:12]
-
-
-def clip_part(positive, parts, scales, pieces, rows, copies):
+        send_ref[k, :, E:] = positive
+
+
+def make_units(positive, parts, copies):
     return pl.pallas_call(
-        functools.partial(clip_kernel, rows),
+        unit_kernel,
         out_shape=(
             jax.ShapeDtypeStruct((4, E + LANES), F32),
             jax.ShapeDtypeStruct((4, LANES), F32),
-            jax.ShapeDtypeStruct((4, E), F32),
             pltpu.HBM((copies, 4, E + LANES), F32),
         ),
-        in_specs=[pl.BlockSpec(memory_space=pltpu.SMEM)] + [IN_VMEM] * 6,
-        out_specs=(IN_VMEM,) * 4,
+        in_specs=[IN_VMEM, IN_VMEM],
+        out_specs=(IN_VMEM,) * 3,
+        compiler_params=pltpu.CompilerParams(vmem_limit_bytes=8 << 20),
+        name="units",
+    )(positive, parts)
+
+
+def clip_kernel(rows, unit_ref, *refs):
+    pieces, grad_ref = refs[:-1], refs[-1]
+    terms = jnp.concatenate(parts_of(unit_ref[:, :E], 3), axis=0)
+    caps = [ref[...] for ref in pieces]
+    scale = TEMP * jnp.concatenate([inverse_lengths(cap) for cap in caps], axis=1)
+    logits = jnp.concatenate([dot_t(terms, cap) for cap in caps], axis=1)
+    logits = (logits[:4] + logits[4:8] + logits[8:12]) * scale + BIAS
+    hit = caption_ids(logits.shape, 1, rows, True).astype(F32) == unit_ref[:, E : E + 1]
+    grad = dot(jnp.concatenate(parts_of(slope(logits, hit) * scale, 3), axis=0), jnp.concatenate(caps, axis=0))
+    grad_ref[...] = grad[:4] + grad[4:8] + grad[8:12]
+
+
+def clip_part(unit, pieces, rows):
+    return pl.pallas_call(
+        functools.partial(clip_kernel, rows),
+        out_shape=jax.ShapeDtypeStruct((4, E), F32),
+        in_specs=[IN_VMEM] * 4,
+        out_specs=IN_VMEM,
         compiler_params=pltpu.CompilerParams(vmem_limit_bytes=24 << 20),
         cost_estimate=pl.CostEstimate(flops=100 << 20, bytes_accessed=1 << 20, transcendentals=0),
         name="clip_part",
-    )(positive, parts, scales, *pieces)
+    )(unit, *pieces)
 
 
 def caption_sum(cap_unit, rows):
@@ -295,11 +287,12 @@
 
     parts = temporal(tokens, w_qkv, w_out, w_proj)
     near = join(parts, layers)
-    pieces = [near] + [swapped(near, "wide", bit) for bit in (1, 2, 3)]
+    near = [near, swapped(near, "wide", 2)]
     parts = lax.all_to_all(parts, "narrow", 0, 0, tiled=True)
-    unit, length, grad_unit, outgoing = clip_part(
-        positive, parts, caption_scales(pieces), pieces, captions.shape[0], chips
-    )
+    pieces = near + [swapped(join(parts, near), "wide", 1)]
+    positive = jnp.broadcast_to(positive.astype(F32)[:, None], (4, LANES))
+    unit, length, outgoing = make_units(positive, parts, chips)
+    grad_unit = clip_part(unit, pieces, captions.shape[0])
     units = lax.all_to_all(outgoing, "wide", 0, 0, axis_index_groups=same_core, tiled=True)
     other = swapped(units, "wide", 1)
     small = pltpu.CompilerParams(vmem_limit_bytes=24 << 20)

time: 74.6 us -> 72.9 us (0.977)
  blocking collectives: 0 us -> 10.4 us
  waiting for transfers between devices: 19.4 us -> 12.9 us
  starting transfers between devices: 38.5 us -> 33.1 us
    all_to_all x0 -> x1, blocking collectives: none -> 10.4 us  [per_device(): parts = lax.all_to_all(parts, 'narrow', 0, 0, tiled=True)]
    ppermute x12 -> x11, waiting for transfers between devices: 13.9 us -> 7.37 us  [swapped(): lax.ppermute(value, axis, [(i, i ^ bit) for i in range(lax.axis_size(axis...]
    all_to_all x1 -> x0, starting transfers between devices: 3.41 us -> none  [per_device(): parts = lax.all_to_all(parts, 'narrow', 0, 0, tiled=True)]
    ppermute x12 -> x11, starting transfers between devices: 19.2 us -> 17.3 us  [swapped(): lax.ppermute(value, axis, [(i, i ^ bit) for i in range(lax.axis_size(axis...]
    all_to_all x1, waiting for transfers between devices: 0.54 us -> 1.81 us  [per_device(): lax.all_to_all(outgoing, 'wide', 0, 0, axis_index_groups=same_core, tiled...]
    all_to_all x1 -> x0, waiting for transfers between devices: 1.24 us -> none  [per_device(): parts = lax.all_to_all(parts, 'narrow', 0, 0, tiled=True)]
  transfers between devices with their start and end apart: 15 -> 13, of which waited for: 10 -> 7; matrix products, arithmetic and copies ran while one was open for 1% -> 1% of each run, Pallas kernels for 13% -> 14%
where the time goes in v4:
time: 72.9 us; the launch traced here: 72.2 us
  starting transfers between devices  33.1 us (45%)
  waiting for transfers between devices  12.9 us (18%)
  Pallas kernels  11.8 us (16%)
  blocking collectives  10.4 us (14%)
  local copies, waits for them, and re-layouts  2.5 us (3%)
  other arithmetic  0.81 us (1%)
  between operations  0.73 us (1%)
    ppermute x11, starting transfers between devices, swapped(): lax.ppermute(value, axis, [(i, i ^ bit) for i in range(lax.axis_size(axis...  17.3 us
    all_to_all x1, blocking collectives, per_device(): parts = lax.all_to_all(parts, 'narrow', 0, 0, tiled=True)  10.4 us
    all_to_all x1, starting transfers between devices, per_device(): lax.all_to_all(outgoing, 'wide', 0, 0, axis_index_groups=same_core, tiled...  9.72 us
    pallas_call x1, Pallas kernels, temporal(): pl.pallas_call(temporal_kernel, out_shape=pltpu.VMEM((8, 8, LANES), F32),...  7.67 us
    ppermute x11, waiting for transfers between devices, swapped(): lax.ppermute(value, axis, [(i, i ^ bit) for i in range(lax.axis_size(axis...  7.37 us
    all_to_all x1, starting transfers between devices, per_device(): tokens = lax.all_to_all(send, 'narrow', 0, 0, tiled=True)  6.03 us
    all_to_all x1, waiting for transfers between devices, per_device(): tokens = lax.all_to_all(send, 'narrow', 0, 0, tiled=True)  3.72 us
    reshape x1, local copies, waits for them, and re-layouts, per_device(): video.reshape(4, 2, 8, 8, D).transpose(0, 2, 1, 3, 4).reshape(8, 64, D)  2.3 us
  transfers between devices with their start and end apart: 13, of which 7 were waited for; matrix products, arithmetic and copies ran while one was open for 1% of the time, Pallas kernels for 14%

profile of v4, /device:TPU:8, one launch (start us, length us, event | category | flops | bytes accessed | tf_op | source)
XLA Modules:
  0.0 72.2 jit_solution(12060065096226400990)
XLA Ops:
  0.6 2.3 %copy.9 = bf16[4,2,8,8,1024]{4,3,1,2,0:T(8,128)(2,1)} copy(bf16[4,2,8,8,1024]{4,3,2,1,0:T(8,128)(2,1)} %bitcast.4) | data formatting | bytes 2097152 | tf_op jit(solution)/shard_map/reshape | solution.py:282
  2.9 6.0 %all-to-all-start = ((bf16[8,64,1024]{2,1,0:T(8,128)(2,1)}), bf16[8,64,1024]{2,1,0:T(8,128)(2,1)S(1)}, u32[]{:S(2)}, u32[]{:S(2)}) async-start(bf16[8,64,1024]{2,1,0:T(8,128)(2,1)} %bitcast.2), calls=%async_computation | async-start | bytes 2097152 | tf_op jit(solution)/shard_map/all_to_all | solution.py:283
  9.0 7.3 %collective-permute-start = (bf16[16,768]{1,0:T(8,128)(2,1)S(1)}, bf16[16,768]{1,0:T(8,128)(2,1)S(1)}, u32[]{:S(2)}, u32[]{:S(2)}) collective-permute-start(bf16[16,768]{1,0:T(8,128)(2,1)S(1)} %copy-done), channel_id=1, source_target_pairs={{0,128},{8,136},{16,144},{24,152},{32,160},{40,168},{48,176},{56,1... | collective-permute-start | bytes 73736 | tf_op jit(solution)/shard_map/ppermute | solution.py:274
  16.3 1.8 %collective-permute-done = bf16[16,768]{1,0:T(8,128)(2,1)S(1)} collective-permute-done((bf16[16,768]{1,0:T(8,128)(2,1)S(1)}, bf16[16,768]{1,0:T(8,128)(2,1)S(1)}, u32[]{:S(2)}, u32[]{:S(2)}) %collective-permute-start) | collective-permute-done | bytes 24608 | tf_op jit(solution)/shard_map/ppermute | solution.py:274
  18.1 1.0 %collective-permute-start.1 = (bf16[32,768]{1,0:T(8,128)(2,1)S(1)}, bf16[32,768]{1,0:T(8,128)(2,1)S(1)}, u32[]{:S(2)}, u32[]{:S(2)}) collective-permute-start(bf16[32,768]{1,0:T(8,128)(2,1)S(1)} %constant_dynamic-update-slice_fusion.refs_0_), channel_id=1, source_target_pairs={{0,32},{8,40},{16,48},{24,56},{32,0},{40,8},{48,16},{56,24},{64,96... | collective-permute-start | bytes 147464 | tf_op jit(solution)/shard_map/ppermute | solution.py:274
  19.1 2.9 %collective-permute-start.2 = (bf16[32,768]{1,0:T(8,128)(2,1)S(1)}, bf16[32,768]{1,0:T(8,128)(2,1)S(1)}, u32[]{:S(2)}, u32[]{:S(2)}) collective-permute-start(bf16[32,768]{1,0:T(8,128)(2,1)S(1)} %constant_dynamic-update-slice_fusion.refs_0_), channel_id=1, source_target_pairs={{0,64},{8,72},{16,80},{24,88},{32,96},{40,104},{48,112},{56,120},{... | collective-permute-start | bytes 147464 | tf_op jit(solution)/shard_map/ppermute | solution.py:274
  22.0 0.5 collective-permute-start.3
  22.5 3.7 %all-to-all-done.x_ref = bf16[8,64,1024]{2,1,0:T(8,128)(2,1)S(1)} async-done(((bf16[8,64,1024]{2,1,0:T(8,128)(2,1)}), bf16[8,64,1024]{2,1,0:T(8,128)(2,1)S(1)}, u32[]{:S(2)}, u32[]{:S(2)}) %all-to-all-start) | async-done | bytes 1048608 | tf_op jit(solution)/shard_map/all_to_all | solution.py:283
  26.2 7.7 %temporal.1.after_ref = f32[8,8,128]{2,1,0:T(8,128)S(1)} custom-call(bf16[8,64,1024]{2,1,0:T(8,128)(2,1)S(1)} %all-to-all-done.x_ref, bf16[1024,3072]{1,0:T(8,128)(2,1)} %wqkv_hbm.1, bf16[1024,1024]{1,0:T(8,128)(2,1)} %wout_hbm.1, bf16[1024,768]{1,0:T(8,128)(2,1)} %wproj_hbm.1), custom_call_target="tpu_custom_call" | custom-call | flops 3221225472 | bytes 11534336 | tf_op jit(solution)/shard_map/temporal/pallas_call | solution.py:126
  33.9 0.0 collective-permute-done.1.refs_1_
  33.9 0.0 collective-permute-done.3.refs_3_
  33.9 1.4 %collective-permute-start.4 = (bf16[128,768]{1,0:T(8,128)(2,1)S(1)}, bf16[128,768]{1,0:T(8,128)(2,1)S(1)}, u32[]{:S(2)}, u32[]{:S(2)}) collective-permute-start(bf16[128,768]{1,0:T(8,128)(2,1)S(1)} %join.2.refs_0_), channel_id=1, source_target_pairs={{0,16},{8,24},{16,0},{24,8},{32,48},{40,56},{48,32},{56,40},{64,80... | collective-permute-start | bytes 589832 | tf_op jit(solution)/shard_map/ppermute | solution.py:274
  35.3 10.4 %all_to_all.15.parts_ref.after_ref = f32[8,8,128]{2,1,0:T(8,128)S(1)} all-to-all(f32[8,8,128]{2,1,0:T(8,128)S(1)} %temporal.1.after_ref), channel_id=1, replica_groups=mesh['wide'=32,'narrow'=8] {'narrow'}, dimensions={0} | all-to-all | bytes 65536 | tf_op jit(solution)/shard_map/all_to_all | solution.py:291
  45.7 0.1 collective-permute-start.5
  45.8 0.1 broadcast_in_dim.2.positive_ref
  45.9 0.8 %units.1 = (f32[4,896]{1,0:T(4,128)S(1)}, f32[4,128]{1,0:T(4,128)S(1)}, f32[16,4,896]{2,1,0:T(4,128)}) custom-call(f32[4,128]{1,0:T(4,128)S(1)} %broadcast_in_dim.2.positive_ref, f32[8,8,128]{2,1,0:T(8,128)S(1)} %all_to_all.15.parts_ref.after_ref), custom_call_target="tpu_custom_call" | custom-call | tf_op jit(solution)/shard_map/units/pallas_call | solution.py:206
  46.7 9.7 %all-to-all-start.2 = ((f32[16,4,896]{2,1,0:T(4,128)}), f32[16,4,896]{2,1,0:T(4,128)S(1)}, u32[]{:S(2)}, u32[]{:S(2)}) async-start(f32[16,4,896]{2,1,0:T(4,128)} %get-tuple-element.7), calls=%async_computation.2 | async-start | bytes 458752 | tf_op jit(solution)/shard_map/all_to_all | solution.py:296
  56.5 1.1 %clip_part.1 = f32[4,768]{1,0:T(4,128)S(1)} custom-call(f32[4,896]{1,0:T(4,128)S(1)} %get-tuple-element.5.unit_ref, bf16[128,768]{1,0:T(8,128)(2,1)S(1)} %join.2.refs_0_, bf16[128,768]{1,0:T(8,128)(2,1)S(1)} %collective-permute-done.4.refs_1_, bf16[256,768]{1,0:T(8,128)(2,1)S(1)} %collective-permute-done.5.refs_2_), custom_call_target="tpu_custom_call" | custom-call | flops 104857600 | bytes 1048576 | tf_op jit(solution)/shard_map/clip_part/pallas_call | solution.py:233
  57.6 1.2 %collective-permute-start.7 = (f32[4,768]{1,0:T(4,128)S(1)}, f32[4,768]{1,0:T(4,128)S(1)}, u32[]{:S(2)}, u32[]{:S(2)}) collective-permute-start(f32[4,768]{1,0:T(4,128)S(1)} %clip_part.1), channel_id=1, source_target_pairs={{0,2},{1,3},{2,0},{3,1},{4,6},{5,7},{6,4},{7,5},{8,10},{9,11},{10,... | collective-permute-start | bytes 36872 | tf_op jit(solution)/shard_map/ppermute | solution.py:274
  58.8 2.2 %collective-permute-start.8 = (f32[4,768]{1,0:T(4,128)S(1)}, f32[4,768]{1,0:T(4,128)S(1)}, u32[]{:S(2)}, u32[]{:S(2)}) collective-permute-start(f32[4,768]{1,0:T(4,128)S(1)} %clip_part.1), channel_id=1, source_target_pairs={{0,3},{1,2},{2,1},{3,0},{4,7},{5,6},{6,5},{7,4},{8,11},{9,10},{10,... | collective-permute-start | bytes 36872 | tf_op jit(solution)/shard_map/ppermute | solution.py:274
  60.9 0.2 collective-permute-start.6
  61.1 1.7 %collective-permute-done.7 = f32[4,768]{1,0:T(4,128)S(1)} collective-permute-done((f32[4,768]{1,0:T(4,128)S(1)}, f32[4,768]{1,0:T(4,128)S(1)}, u32[]{:S(2)}, u32[]{:S(2)}) %collective-permute-start.7) | collective-permute-done | bytes 12320 | tf_op jit(solution)/shard_map/ppermute | solution.py:274
  62.8 0.9 %collective-permute-done.8 = f32[4,768]{1,0:T(4,128)S(1)} collective-permute-done((f32[4,768]{1,0:T(4,128)S(1)}, f32[4,768]{1,0:T(4,128)S(1)}, u32[]{:S(2)}, u32[]{:S(2)}) %collective-permute-start.8) | collective-permute-done | bytes 12320 | tf_op jit(solution)/shard_map/ppermute | solution.py:274
  63.7 0.9 %collective-permute-done.6 = f32[4,768]{1,0:T(4,128)S(1)} collective-permute-done((f32[4,768]{1,0:T(4,128)S(1)}, f32[4,768]{1,0:T(4,128)S(1)}, u32[]{:S(2)}, u32[]{:S(2)}) %collective-permute-start.6) | collective-permute-done | bytes 12320 | tf_op jit(solution)/shard_map/ppermute | solution.py:274
  64.6 0.6 collective-permute-start.9
  65.3 0.1 slice_reduce_fusion
  65.4 1.8 %all-to-all-done.2.units_ref = f32[16,4,896]{2,1,0:T(4,128)S(1)} async-done(((f32[16,4,896]{2,1,0:T(4,128)}), f32[16,4,896]{2,1,0:T(4,128)S(1)}, u32[]{:S(2)}, u32[]{:S(2)}) %all-to-all-start.2) | async-done | bytes 229408 | tf_op jit(solution)/shard_map/all_to_all | solution.py:296
  67.2 0.7 caption_near.1.part_ref
  67.9 2.0 %collective-permute-done.9 = f32[4,768]{1,0:T(4,128)S(1)} collective-permute-done((f32[4,768]{1,0:T(4,128)S(1)}, f32[4,768]{1,0:T(4,128)S(1)}, u32[]{:S(2)}, u32[]{:S(2)}) %collective-permute-start.9) | collective-permute-done | bytes 12320 | tf_op jit(solution)/shard_map/ppermute | solution.py:274
  69.9 0.1 multiply_reduce_fusion
  70.1 0.7 subtract_divide_fusion
  70.7 1.4 %caption_far.1 = f32[16,768]{1,0:T(8,128)} custom-call(f32[16,4,896]{2,1,0:T(4,128)S(1)} %collective-permute-done.10.units_ref, f32[16,768]{1,0:T(8,128)S(1)} %caption_near.1.part_ref, bf16[16,768]{1,0:T(8,128)(2,1)S(1)} %copy-done), custom_call_target="tpu_custom_call" | custom-call | tf_op jit(solution)/shard_map/caption_far/pallas_call | solution.py:301
  (15 shorter events, 0.1 us)
Async XLA Ops:
  0.6 8.3 %copy-start = (bf16[16,768]{1,0:T(8,128)(2,1)S(1)}, bf16[16,768]{1,0:T(8,128)(2,1)}, u32[]{:S(2)}) copy-start(bf16[16,768]{1,0:T(8,128)(2,1)} %cap_ref.3) | copy-start | bytes 73732
  2.9 23.2 %all-to-all-start = ((bf16[8,64,1024]{2,1,0:T(8,128)(2,1)}), bf16[8,64,1024]{2,1,0:T(8,128)(2,1)S(1)}, u32[]{:S(2)}, u32[]{:S(2)}) async-start(bf16[8,64,1024]{2,1,0:T(8,128)(2,1)} %bitcast.2), calls=%async_computation | async-start | bytes 2097152 | tf_op jit(solution)/shard_map/all_to_all | solution.py:283
  9.0 9.1 %collective-permute-start = (bf16[16,768]{1,0:T(8,128)(2,1)S(1)}, bf16[16,768]{1,0:T(8,128)(2,1)S(1)}, u32[]{:S(2)}, u32[]{:S(2)}) collective-permute-start(bf16[16,768]{1,0:T(8,128)(2,1)S(1)} %copy-done), channel_id=1, source_target_pairs={{0,128},{8,136},{16,144},{24,152},{32,160},{40,168},{48,176},{56,1... | collective-permute-start | bytes 73736 | tf_op jit(solution)/shard_map/ppermute | solution.py:274
  18.1 27.8 %copy-start.1 = (s32[4]{0:T(128)S(1)}, s32[4]{0:T(128)}, u32[]{:S(2)}) copy-start(s32[4]{0:T(128)} %param.11) | copy-start | bytes 52
  18.1 15.8 %collective-permute-start.1 = (bf16[32,768]{1,0:T(8,128)(2,1)S(1)}, bf16[32,768]{1,0:T(8,128)(2,1)S(1)}, u32[]{:S(2)}, u32[]{:S(2)}) collective-permute-start(bf16[32,768]{1,0:T(8,128)(2,1)S(1)} %constant_dynamic-update-slice_fusion.refs_0_), channel_id=1, source_target_pairs={{0,32},{8,40},{16,48},{24,56},{32,0},{40,8},{48,16},{56,24},{64,96... | collective-permute-start | bytes 147464 | tf_op jit(solution)/shard_map/ppermute | solution.py:274
  19.1 14.8 %collective-permute-start.2 = (bf16[32,768]{1,0:T(8,128)(2,1)S(1)}, bf16[32,768]{1,0:T(8,128)(2,1)S(1)}, u32[]{:S(2)}, u32[]{:S(2)}) collective-permute-start(bf16[32,768]{1,0:T(8,128)(2,1)S(1)} %constant_dynamic-update-slice_fusion.refs_0_), channel_id=1, source_target_pairs={{0,64},{8,72},{16,80},{24,88},{32,96},{40,104},{48,112},{56,120},{... | collective-permute-start | bytes 147464 | tf_op jit(solution)/shard_map/ppermute | solution.py:274
  22.0 11.9 %collective-permute-start.3 = (bf16[32,768]{1,0:T(8,128)(2,1)S(1)}, bf16[32,768]{1,0:T(8,128)(2,1)S(1)}, u32[]{:S(2)}, u32[]{:S(2)}) collective-permute-start(bf16[32,768]{1,0:T(8,128)(2,1)S(1)} %constant_dynamic-update-slice_fusion.refs_0_), channel_id=1, source_target_pairs={{0,96},{8,104},{16,112},{24,120},{32,64},{40,72},{48,80},{56,88},{... | collective-permute-start | bytes 147464 | tf_op jit(solution)/shard_map/ppermute | solution.py:274
  33.9 11.8 %collective-permute-start.4 = (bf16[128,768]{1,0:T(8,128)(2,1)S(1)}, bf16[128,768]{1,0:T(8,128)(2,1)S(1)}, u32[]{:S(2)}, u32[]{:S(2)}) collective-permute-start(bf16[128,768]{1,0:T(8,128)(2,1)S(1)} %join.2.refs_0_), channel_id=1, source_target_pairs={{0,16},{8,24},{16,0},{24,8},{32,48},{40,56},{48,32},{56,40},{64,80... | collective-permute-start | bytes 589832 | tf_op jit(solution)/shard_map/ppermute | solution.py:274
  45.7 10.7 %collective-permute-start.5 = (bf16[256,768]{1,0:T(8,128)(2,1)S(1)}, bf16[256,768]{1,0:T(8,128)(2,1)S(1)}, u32[]{:S(2)}, u32[]{:S(2)}) collective-permute-start(bf16[256,768]{1,0:T(8,128)(2,1)S(1)} %join.3), channel_id=1, source_target_pairs={{0,8},{8,0},{16,24},{24,16},{32,40},{40,32},{48,56},{56,48},{64,72... | collective-permute-start | bytes 1179656 | tf_op jit(solution)/shard_map/ppermute | solution.py:274
  46.7 20.5 %all-to-all-start.2 = ((f32[16,4,896]{2,1,0:T(4,128)}), f32[16,4,896]{2,1,0:T(4,128)S(1)}, u32[]{:S(2)}, u32[]{:S(2)}) async-start(f32[16,4,896]{2,1,0:T(4,128)} %get-tuple-element.7), calls=%async_computation.2 | async-start | bytes 458752 | tf_op jit(solution)/shard_map/all_to_all | solution.py:296
  57.6 5.2 %collective-permute-start.7 = (f32[4,768]{1,0:T(4,128)S(1)}, f32[4,768]{1,0:T(4,128)S(1)}, u32[]{:S(2)}, u32[]{:S(2)}) collective-permute-start(f32[4,768]{1,0:T(4,128)S(1)} %clip_part.1), channel_id=1, source_target_pairs={{0,2},{1,3},{2,0},{3,1},{4,6},{5,7},{6,4},{7,5},{8,10},{9,11},{10,... | collective-permute-start | bytes 36872 | tf_op jit(solution)/shard_map/ppermute | solution.py:274
  58.8 4.9 %collective-permute-start.8 = (f32[4,768]{1,0:T(4,128)S(1)}, f32[4,768]{1,0:T(4,128)S(1)}, u32[]{:S(2)}, u32[]{:S(2)}) collective-permute-start(f32[4,768]{1,0:T(4,128)S(1)} %clip_part.1), channel_id=1, source_target_pairs={{0,3},{1,2},{2,1},{3,0},{4,7},{5,6},{6,5},{7,4},{8,11},{9,10},{10,... | collective-permute-start | bytes 36872 | tf_op jit(solution)/shard_map/ppermute | solution.py:274
  60.9 3.7 %collective-permute-start.6 = (f32[4,768]{1,0:T(4,128)S(1)}, f32[4,768]{1,0:T(4,128)S(1)}, u32[]{:S(2)}, u32[]{:S(2)}) collective-permute-start(f32[4,768]{1,0:T(4,128)S(1)} %clip_part.1), channel_id=1, source_target_pairs={{0,1},{1,0},{2,3},{3,2},{4,5},{5,4},{6,7},{7,6},{8,9},{9,8},{10,11... | collective-permute-start | bytes 36872 | tf_op jit(solution)/shard_map/ppermute | solution.py:274
  64.6 5.3 %collective-permute-start.9 = (f32[4,768]{1,0:T(4,128)S(1)}, f32[4,768]{1,0:T(4,128)S(1)}, u32[]{:S(2)}, u32[]{:S(2)}) collective-permute-start(f32[4,768]{1,0:T(4,128)S(1)} %add_add_fusion), channel_id=1, source_target_pairs={{0,4},{1,5},{2,6},{3,7},{4,0},{5,1},{6,2},{7,3},{8,12},{9,13},{10,... | collective-permute-start | bytes 36872 | tf_op jit(solution)/shard_map/ppermute | solution.py:274
  67.2 3.5 %collective-permute-start.10 = (f32[16,4,896]{2,1,0:T(4,128)S(1)}, f32[16,4,896]{2,1,0:T(4,128)S(1)}, u32[]{:S(2)}, u32[]{:S(2)}) collective-permute-start(f32[16,4,896]{2,1,0:T(4,128)S(1)} %all-to-all-done.2.units_ref), channel_id=1, source_target_pairs={{0,8},{8,0},{16,24},{24,16},{32,40},{40,32},{48,56},{56,48},{64,72... | collective-permute-start | bytes 688136 | tf_op jit(solution)/shard_map/ppermute | solution.py:274

commit v5 on v4

--- a/solution.py
+++ b/solution.py
@@ -17,6 +17,7 @@
 LANES = 128
 GROUP = 4
 WIDTH = GROUP * HEAD
+AHEAD = 2
 BLOCKS = 4
 ROWS = FRAMES * 8
 
@@ -49,7 +50,7 @@
     return terms
 
 
-def temporal_kernel(x_ref, wqkv_hbm, wout_hbm, wproj_hbm, out_ref, wqkv, wout, wproj, sems):
+def temporal_kernel(x_ref, query_ref, keys_ref, wqkv_hbm, wout_hbm, wproj_hbm, out_ref, wqkv, wout, wproj, sems):
     copies = []
 
     def bring(source, target, columns):
@@ -57,7 +58,7 @@
         copy.start()
         copies.append(copy)
 
-    for start, width in ((0, WIDTH), (WIDTH, WIDTH), (2 * WIDTH, 2 * WIDTH)):
+    for start, width in ((2 * WIDTH, 2 * WIDTH),):
         bring(wqkv_hbm, wqkv, pl.ds(start, width))
         bring(wqkv_hbm, wqkv, pl.ds(D + start, width))
     bring(wqkv_hbm, wqkv, pl.ds(2 * D, D))
@@ -70,10 +71,17 @@
     owner = lax.broadcasted_iota(jnp.int32, (GROUP * ROWS, LANES), 0) // ROWS
     column = lax.broadcasted_iota(jnp.int32, (GROUP * ROWS, LANES), 1)
     weights = jnp.zeros((BLOCKS * ROWS, LANES), F32)
+
     def project(j):
-        query = dot(x, wqkv[:, j * WIDTH : (j + 1) * WIDTH]).astype(BF16)
-        keys = dot(x, wqkv[:, D + j * WIDTH : D + (j + 1) * WIDTH]).astype(BF16)
-        return query, keys
+        columns = slice(j * WIDTH, (j + 1) * WIDTH)
+        if j < AHEAD:
+            query, keys = query_ref[:, columns], keys_ref[:, columns]
+        else:
+            if j == AHEAD:
+                copies[0].wait()
+                copies[1].wait()
+            query, keys = wqkv[:, columns], wqkv[:, D + j * WIDTH : D + (j + 1) * WIDTH]
+        return dot(x, query).astype(BF16), dot(x, keys).astype(BF16)
 
     def attend(query, keys, b):
         q = query[b * ROWS : (b + 1) * ROWS]
@@ -88,14 +96,9 @@
     def place(j):
         return jnp.where(owner + j * GROUP == column, 1.0, 0.0).astype(BF16)
 
-    copies[0].wait()
-    copies[1].wait()
     ready = project(0)
     for j in range(HEADS // GROUP):
         current = ready
-        if j < 2:
-            copies[2 * j + 2].wait()
-            copies[2 * j + 3].wait()
         if j + 1 < HEADS // GROUP:
             ready = project(j + 1)
         probs = [attend(*current, b) for b in range(BLOCKS)]
@@ -122,11 +125,35 @@
     out_ref[:, E // LANES :, :] = jnp.zeros((8, 8 - E // LANES, LANES), F32)
 
 
-def temporal(x, w_qkv, w_out, w_proj):
+def fetch_kernel(source, query_ref, keys_ref, sems):
+    copies = [
+        pltpu.make_async_copy(source.at[:, pl.ds(k * D, AHEAD * WIDTH)], target, sems.at[k])
+        for k, target in enumerate((query_ref, keys_ref))
+    ]
+    for copy in copies:
+        copy.start()
+    for copy in copies:
+        copy.wait()
+
+
+def fetch(w_qkv):
+    return pl.pallas_call(
+        fetch_kernel,
+        out_shape=(pltpu.VMEM((D, AHEAD * WIDTH), BF16),) * 2,
+        in_specs=[ANYWHERE],
+        out_specs=(IN_VMEM,) * 2,
+        scratch_shapes=[pltpu.SemaphoreType.DMA((2,))],
+        compiler_params=pltpu.CompilerParams(vmem_limit_bytes=4 << 20),
+        cost_estimate=pl.CostEstimate(flops=0, bytes_accessed=4 << 20, transcendentals=0),
+        name="fetch",
+    )(pltpu.with_memory_space_constraint(w_qkv, pltpu.HBM))
+
+
+def temporal(x, first, w_qkv, w_out, w_proj):
     return pl.pallas_call(
         temporal_kernel,
         out_shape=pltpu.VMEM((8, 8, LANES), F32),
-        in_specs=[IN_VMEM, ANYWHERE, ANYWHERE, ANYWHERE],
+        in_specs=[IN_VMEM] * 3 + [ANYWHERE] * 3,
         out_specs=IN_VMEM,
         scratch_shapes=[
             pltpu.VMEM((D, 3 * D), BF16),
@@ -138,7 +165,7 @@
         cost_estimate=pl.CostEstimate(flops=3 << 30, bytes_accessed=11 << 20, transcendentals=0),
         name="temporal",
     )(
-        pltpu.with_memory_space_constraint(x, pltpu.VMEM),
+        *(pltpu.with_memory_space_constraint(a, pltpu.VMEM) for a in (x, *first)),
         *(pltpu.with_memory_space_constraint(w, pltpu.HBM) for w in (w_qkv, w_out, w_proj)),
     )
 
@@ -241,32 +268,36 @@
     )(unit, *pieces)
 
 
-def caption_sum(cap_unit, rows):
-    unit = rows[:, :E]
+def caption_sum(cap, length, rows):
+    count = cap.shape[0]
+    units = parts_of(rows[:, :E], 3)
     positive = rows[:, E:].T[:1]
-    logits = lax.dot_general(
-        cap_unit, unit, (((1,), (1,)), ((), ())), precision=lax.Precision.HIGHEST, preferred_element_type=F32
-    )
-    ids = caption_ids(logits.shape, 0, logits.shape[0], False).astype(F32)
-    weight = slope(TEMP * logits + BIAS, ids == positive)
-    return TEMP * jnp.dot(weight, unit, precision=lax.Precision.HIGHEST, preferred_element_type=F32)
+    logits = sum(dot_t(cap, unit) for unit in units) * (TEMP / length) + BIAS
+    ids = caption_ids(logits.shape, 0, count, False).astype(F32)
+    weight = jnp.concatenate(parts_of(TEMP * slope(logits, ids == positive), 3), axis=0)
+    terms = [dot(weight[: (3 - k) * count], unit) for k, unit in enumerate(units)]
+    return sum(term[j * count : (j + 1) * count] for k, term in enumerate(terms) for j in range(3 - k))
 
 
 def stacked(ref):
     return jnp.concatenate([ref[g] for g in range(ref.shape[0])], axis=0)
 
 
+def lengths(value):
+    return jnp.sqrt(jnp.sum(value * value, axis=-1, keepdims=True) + EPS)
+
+
 def near_kernel(units_ref, cap_ref, out_ref):
-    cap = cap_ref[...].astype(F32)
-    length = jnp.sqrt(jnp.sum(cap * cap, axis=-1, keepdims=True) + EPS)
-    out_ref[...] = caption_sum(cap / length, stacked(units_ref))
+    cap = cap_ref[...]
+    out_ref[...] = caption_sum(cap, lengths(cap.astype(F32)), stacked(units_ref))
 
 
 def far_kernel(units_ref, part_ref, cap_ref, out_ref):
-    cap = cap_ref[...].astype(F32)
-    length = jnp.sqrt(jnp.sum(cap * cap, axis=-1, keepdims=True) + EPS)
-    cap_unit = cap / length
-    grad = part_ref[...] + caption_sum(cap_unit, stacked(units_ref))
+    cap = cap_ref[...]
+    value = cap.astype(F32)
+    length = lengths(value)
+    cap_unit = value / length
+    grad = part_ref[...] + caption_sum(cap, length, stacked(units_ref))
     out_ref[...] = (grad - cap_unit * jnp.sum(cap_unit * grad, axis=-1, keepdims=True)) / length
 
 
@@ -285,7 +316,7 @@
     near = jnp.concatenate([captions, swapped(captions, "wide", 16)], axis=0)
     layers = [near] + [swapped(near, "wide", bit) for bit in (4, 8, 12)]
 
-    parts = temporal(tokens, w_qkv, w_out, w_proj)
+    parts = temporal(tokens, fetch(w_qkv), w_qkv, w_out, w_proj)
     near = join(parts, layers)
     near = [near, swapped(near, "wide", 2)]
     parts = lax.all_to_all(parts, "narrow", 0, 0, tiled=True)

time: 72.9 us -> 71.9 us (0.986)
  waiting for transfers between devices: 12.9 us -> 11.6 us
    pallas_call x0 -> x1, Pallas kernels: none -> 1.56 us  [fetch(): pl.pallas_call(fetch_kernel, out_shape=(pltpu.VMEM((D, AHEAD * WIDTH), BF...]
    ppermute x11, waiting for transfers between devices: 7.37 us -> 6.03 us  [swapped(): lax.ppermute(value, axis, [(i, i ^ bit) for i in range(lax.axis_size(axis...]
  transfers between devices with their start and end apart: 13 -> 13, of which waited for: 7 -> 7; matrix products, arithmetic and copies ran while one was open for 1% -> 1% of each run, Pallas kernels for 14% -> 15%
where the time goes in v5:
time: 71.9 us; the launch traced here: 71.4 us
  starting transfers between devices  33.1 us (46%)
  Pallas kernels  12.3 us (17%)
  waiting for transfers between devices  11.6 us (16%)
  blocking collectives  10.3 us (14%)
  local copies, waits for them, and re-layouts  2.51 us (3%)
  other arithmetic  0.81 us (1%)
  between operations  0.74 us (1%)
    ppermute x11, starting transfers between devices, swapped(): lax.ppermute(value, axis, [(i, i ^ bit) for i in range(lax.axis_size(axis...  17.3 us
    all_to_all x1, blocking collectives, per_device(): parts = lax.all_to_all(parts, 'narrow', 0, 0, tiled=True)  10.3 us
    all_to_all x1, starting transfers between devices, per_device(): lax.all_to_all(outgoing, 'wide', 0, 0, axis_index_groups=same_core, tiled...  9.73 us
    pallas_call x1, Pallas kernels, temporal(): pl.pallas_call(temporal_kernel, out_shape=pltpu.VMEM((8, 8, LANES), F32),...  7.1 us
    all_to_all x1, starting transfers between devices, per_device(): tokens = lax.all_to_all(send, 'narrow', 0, 0, tiled=True)  6.03 us
    ppermute x11, waiting for transfers between devices, swapped(): lax.ppermute(value, axis, [(i, i ^ bit) for i in range(lax.axis_size(axis...  6.03 us
    all_to_all x1, waiting for transfers between devices, per_device(): tokens = lax.all_to_all(send, 'narrow', 0, 0, tiled=True)  3.72 us
    reshape x1, local copies, waits for them, and re-layouts, per_device(): video.reshape(4, 2, 8, 8, D).transpose(0, 2, 1, 3, 4).reshape(8, 64, D)  2.31 us
  transfers between devices with their start and end apart: 13, of which 7 were waited for; matrix products, arithmetic and copies ran while one was open for 1% of the time, Pallas kernels for 15%

profile of v5, /device:TPU:8, one launch (start us, length us, event | category | flops | bytes accessed | tf_op | source)
XLA Modules:
  0.0 71.4 jit_solution(10235326280107617564)
XLA Ops:
  0.6 2.3 %copy.9 = bf16[4,2,8,8,1024]{4,3,1,2,0:T(8,128)(2,1)} copy(bf16[4,2,8,8,1024]{4,3,2,1,0:T(8,128)(2,1)} %bitcast.4) | data formatting | bytes 2097152 | tf_op jit(solution)/shard_map/reshape | solution.py:313
  2.9 6.0 %all-to-all-start = ((bf16[8,64,1024]{2,1,0:T(8,128)(2,1)}), bf16[8,64,1024]{2,1,0:T(8,128)(2,1)S(1)}, u32[]{:S(2)}, u32[]{:S(2)}) async-start(bf16[8,64,1024]{2,1,0:T(8,128)(2,1)} %bitcast.2), calls=%async_computation | async-start | bytes 2097152 | tf_op jit(solution)/shard_map/all_to_all | solution.py:314
  9.0 7.3 %collective-permute-start = (bf16[16,768]{1,0:T(8,128)(2,1)S(1)}, bf16[16,768]{1,0:T(8,128)(2,1)S(1)}, u32[]{:S(2)}, u32[]{:S(2)}) collective-permute-start(bf16[16,768]{1,0:T(8,128)(2,1)S(1)} %copy-done), channel_id=1, source_target_pairs={{0,128},{8,136},{16,144},{24,152},{32,160},{40,168},{48,176},{56,1... | collective-permute-start | bytes 73736 | tf_op jit(solution)/shard_map/ppermute | solution.py:305
  16.3 1.6 %fetch.1 = (bf16[1024,512]{1,0:T(8,128)(2,1)S(1)}, bf16[1024,512]{1,0:T(8,128)(2,1)S(1)}) custom-call(bf16[1024,3072]{1,0:T(8,128)(2,1)} %wqkv_hbm.1), custom_call_target="tpu_custom_call" | custom-call | bytes 4194304 | tf_op jit(solution)/shard_map/fetch/pallas_call | solution.py:140
  17.8 0.2 collective-permute-done
  18.1 1.0 %collective-permute-start.1 = (bf16[32,768]{1,0:T(8,128)(2,1)S(1)}, bf16[32,768]{1,0:T(8,128)(2,1)S(1)}, u32[]{:S(2)}, u32[]{:S(2)}) collective-permute-start(bf16[32,768]{1,0:T(8,128)(2,1)S(1)} %constant_dynamic-update-slice_fusion.refs_0_), channel_id=1, source_target_pairs={{0,32},{8,40},{16,48},{24,56},{32,0},{40,8},{48,16},{56,24},{64,96... | collective-permute-start | bytes 147464 | tf_op jit(solution)/shard_map/ppermute | solution.py:305
  19.1 2.9 %collective-permute-start.2 = (bf16[32,768]{1,0:T(8,128)(2,1)S(1)}, bf16[32,768]{1,0:T(8,128)(2,1)S(1)}, u32[]{:S(2)}, u32[]{:S(2)}) collective-permute-start(bf16[32,768]{1,0:T(8,128)(2,1)S(1)} %constant_dynamic-update-slice_fusion.refs_0_), channel_id=1, source_target_pairs={{0,64},{8,72},{16,80},{24,88},{32,96},{40,104},{48,112},{56,120},{... | collective-permute-start | bytes 147464 | tf_op jit(solution)/shard_map/ppermute | solution.py:305
  22.0 0.5 collective-permute-start.3
  22.5 3.7 %all-to-all-done.x_ref = bf16[8,64,1024]{2,1,0:T(8,128)(2,1)S(1)} async-done(((bf16[8,64,1024]{2,1,0:T(8,128)(2,1)}), bf16[8,64,1024]{2,1,0:T(8,128)(2,1)S(1)}, u32[]{:S(2)}, u32[]{:S(2)}) %all-to-all-start) | async-done | bytes 1048608 | tf_op jit(solution)/shard_map/all_to_all | solution.py:314
  26.2 7.1 %temporal.1.after_ref = f32[8,8,128]{2,1,0:T(8,128)S(1)} custom-call(bf16[8,64,1024]{2,1,0:T(8,128)(2,1)S(1)} %all-to-all-done.x_ref, bf16[1024,512]{1,0:T(8,128)(2,1)S(1)} %get-tuple-element.7.query_ref, bf16[1024,512]{1,0:T(8,128)(2,1)S(1)} %get-tuple-element.8.keys_ref, bf16[1024,3072]{1,0:T(8,128)(2,1)} %wqkv_hbm.1, bf16[1024,1024]{1,0:T(8,128)(2,1)} %wout_hbm.1, ...), custom_call_target="tpu_custom_call" | custom-call | flops 3221225472 | bytes 11534336 | tf_op jit(solution)/shard_map/temporal/pallas_call | solution.py:153
  33.3 0.0 collective-permute-done.1.refs_1_
  33.3 1.4 %collective-permute-start.4 = (bf16[128,768]{1,0:T(8,128)(2,1)S(1)}, bf16[128,768]{1,0:T(8,128)(2,1)S(1)}, u32[]{:S(2)}, u32[]{:S(2)}) collective-permute-start(bf16[128,768]{1,0:T(8,128)(2,1)S(1)} %join.2.refs_0_), channel_id=1, source_target_pairs={{0,16},{8,24},{16,0},{24,8},{32,48},{40,56},{48,32},{56,40},{64,80... | collective-permute-start | bytes 589832 | tf_op jit(solution)/shard_map/ppermute | solution.py:305
  34.8 10.3 %all_to_all.15.parts_ref.after_ref = f32[8,8,128]{2,1,0:T(8,128)S(1)} all-to-all(f32[8,8,128]{2,1,0:T(8,128)S(1)} %temporal.1.after_ref), channel_id=1, replica_groups=mesh['wide'=32,'narrow'=8] {'narrow'}, dimensions={0} | all-to-all | bytes 65536 | tf_op jit(solution)/shard_map/all_to_all | solution.py:322
  45.2 0.1 collective-permute-start.5
  45.3 0.1 broadcast_in_dim.2.positive_ref
  45.3 0.8 %units.1 = (f32[4,896]{1,0:T(4,128)S(1)}, f32[4,128]{1,0:T(4,128)S(1)}, f32[16,4,896]{2,1,0:T(4,128)}) custom-call(f32[4,128]{1,0:T(4,128)S(1)} %broadcast_in_dim.2.positive_ref, f32[8,8,128]{2,1,0:T(8,128)S(1)} %all_to_all.15.parts_ref.after_ref), custom_call_target="tpu_custom_call" | custom-call | tf_op jit(solution)/shard_map/units/pallas_call | solution.py:233
  46.2 9.7 %all-to-all-start.2 = ((f32[16,4,896]{2,1,0:T(4,128)}), f32[16,4,896]{2,1,0:T(4,128)S(1)}, u32[]{:S(2)}, u32[]{:S(2)}) async-start(f32[16,4,896]{2,1,0:T(4,128)} %get-tuple-element.11), calls=%async_computation.2 | async-start | bytes 458752 | tf_op jit(solution)/shard_map/all_to_all | solution.py:327
  55.9 1.1 %clip_part.1 = f32[4,768]{1,0:T(4,128)S(1)} custom-call(f32[4,896]{1,0:T(4,128)S(1)} %get-tuple-element.9.unit_ref, bf16[128,768]{1,0:T(8,128)(2,1)S(1)} %join.2.refs_0_, bf16[128,768]{1,0:T(8,128)(2,1)S(1)} %collective-permute-done.4.refs_1_, bf16[256,768]{1,0:T(8,128)(2,1)S(1)} %collective-permute-done.5.refs_2_), custom_call_target="tpu_custom_call" | custom-call | flops 104857600 | bytes 1048576 | tf_op jit(solution)/shard_map/clip_part/pallas_call | solution.py:260
  57.0 1.2 %collective-permute-start.7 = (f32[4,768]{1,0:T(4,128)S(1)}, f32[4,768]{1,0:T(4,128)S(1)}, u32[]{:S(2)}, u32[]{:S(2)}) collective-permute-start(f32[4,768]{1,0:T(4,128)S(1)} %clip_part.1), channel_id=1, source_target_pairs={{0,2},{1,3},{2,0},{3,1},{4,6},{5,7},{6,4},{7,5},{8,10},{9,11},{10,... | collective-permute-start | bytes 36872 | tf_op jit(solution)/shard_map/ppermute | solution.py:305
  58.2 2.2 %collective-permute-start.8 = (f32[4,768]{1,0:T(4,128)S(1)}, f32[4,768]{1,0:T(4,128)S(1)}, u32[]{:S(2)}, u32[]{:S(2)}) collective-permute-start(f32[4,768]{1,0:T(4,128)S(1)} %clip_part.1), channel_id=1, source_target_pairs={{0,3},{1,2},{2,1},{3,0},{4,7},{5,6},{6,5},{7,4},{8,11},{9,10},{10,... | collective-permute-start | bytes 36872 | tf_op jit(solution)/shard_map/ppermute | solution.py:305
  60.4 0.2 collective-permute-start.6
  60.5 1.7 %collective-permute-done.7 = f32[4,768]{1,0:T(4,128)S(1)} collective-permute-done((f32[4,768]{1,0:T(4,128)S(1)}, f32[4,768]{1,0:T(4,128)S(1)}, u32[]{:S(2)}, u32[]{:S(2)}) %collective-permute-start.7) | collective-permute-done | bytes 12320 | tf_op jit(solution)/shard_map/ppermute | solution.py:305
  62.2 0.9 %collective-permute-done.8 = f32[4,768]{1,0:T(4,128)S(1)} collective-permute-done((f32[4,768]{1,0:T(4,128)S(1)}, f32[4,768]{1,0:T(4,128)S(1)}, u32[]{:S(2)}, u32[]{:S(2)}) %collective-permute-start.8) | collective-permute-done | bytes 12320 | tf_op jit(solution)/shard_map/ppermute | solution.py:305
  63.1 0.9 %collective-permute-done.6 = f32[4,768]{1,0:T(4,128)S(1)} collective-permute-done((f32[4,768]{1,0:T(4,128)S(1)}, f32[4,768]{1,0:T(4,128)S(1)}, u32[]{:S(2)}, u32[]{:S(2)}) %collective-permute-start.6) | collective-permute-done | bytes 12320 | tf_op jit(solution)/shard_map/ppermute | solution.py:305
  64.1 0.6 collective-permute-start.9
  64.7 0.1 slice_reduce_fusion
  64.8 1.8 %all-to-all-done.2.units_ref = f32[16,4,896]{2,1,0:T(4,128)S(1)} async-done(((f32[16,4,896]{2,1,0:T(4,128)}), f32[16,4,896]{2,1,0:T(4,128)S(1)}, u32[]{:S(2)}, u32[]{:S(2)}) %all-to-all-start.2) | async-done | bytes 229408 | tf_op jit(solution)/shard_map/all_to_all | solution.py:327
  66.6 0.5 caption_near.1.part_ref
  67.1 2.3 %collective-permute-done.9 = f32[4,768]{1,0:T(4,128)S(1)} collective-permute-done((f32[4,768]{1,0:T(4,128)S(1)}, f32[4,768]{1,0:T(4,128)S(1)}, u32[]{:S(2)}, u32[]{:S(2)}) %collective-permute-start.9) | collective-permute-done | bytes 12320 | tf_op jit(solution)/shard_map/ppermute | solution.py:305
  69.4 0.1 multiply_reduce_fusion
  69.5 0.7 subtract_divide_fusion
  70.2 1.2 %caption_far.1 = f32[16,768]{1,0:T(8,128)} custom-call(f32[16,4,896]{2,1,0:T(4,128)S(1)} %collective-permute-done.10.units_ref, f32[16,768]{1,0:T(8,128)S(1)} %caption_near.1.part_ref, bf16[16,768]{1,0:T(8,128)(2,1)S(1)} %copy-done), custom_call_target="tpu_custom_call" | custom-call | tf_op jit(solution)/shard_map/caption_far/pallas_call | solution.py:332
  (16 shorter events, 0.1 us)
Async XLA Ops:
  0.6 8.4 %copy-start = (bf16[16,768]{1,0:T(8,128)(2,1)S(1)}, bf16[16,768]{1,0:T(8,128)(2,1)}, u32[]{:S(2)}) copy-start(bf16[16,768]{1,0:T(8,128)(2,1)} %cap_ref.3) | copy-start | bytes 73732
  2.9 23.2 %all-to-all-start = ((bf16[8,64,1024]{2,1,0:T(8,128)(2,1)}), bf16[8,64,1024]{2,1,0:T(8,128)(2,1)S(1)}, u32[]{:S(2)}, u32[]{:S(2)}) async-start(bf16[8,64,1024]{2,1,0:T(8,128)(2,1)} %bitcast.2), calls=%async_computation | async-start | bytes 2097152 | tf_op jit(solution)/shard_map/all_to_all | solution.py:314
  9.0 9.1 %collective-permute-start = (bf16[16,768]{1,0:T(8,128)(2,1)S(1)}, bf16[16,768]{1,0:T(8,128)(2,1)S(1)}, u32[]{:S(2)}, u32[]{:S(2)}) collective-permute-start(bf16[16,768]{1,0:T(8,128)(2,1)S(1)} %copy-done), channel_id=1, source_target_pairs={{0,128},{8,136},{16,144},{24,152},{32,160},{40,168},{48,176},{56,1... | collective-permute-start | bytes 73736 | tf_op jit(solution)/shard_map/ppermute | solution.py:305
  18.1 15.2 %collective-permute-start.1 = (bf16[32,768]{1,0:T(8,128)(2,1)S(1)}, bf16[32,768]{1,0:T(8,128)(2,1)S(1)}, u32[]{:S(2)}, u32[]{:S(2)}) collective-permute-start(bf16[32,768]{1,0:T(8,128)(2,1)S(1)} %constant_dynamic-update-slice_fusion.refs_0_), channel_id=1, source_target_pairs={{0,32},{8,40},{16,48},{24,56},{32,0},{40,8},{48,16},{56,24},{64,96... | collective-permute-start | bytes 147464 | tf_op jit(solution)/shard_map/ppermute | solution.py:305
  19.1 14.2 %collective-permute-start.2 = (bf16[32,768]{1,0:T(8,128)(2,1)S(1)}, bf16[32,768]{1,0:T(8,128)(2,1)S(1)}, u32[]{:S(2)}, u32[]{:S(2)}) collective-permute-start(bf16[32,768]{1,0:T(8,128)(2,1)S(1)} %constant_dynamic-update-slice_fusion.refs_0_), channel_id=1, source_target_pairs={{0,64},{8,72},{16,80},{24,88},{32,96},{40,104},{48,112},{56,120},{... | collective-permute-start | bytes 147464 | tf_op jit(solution)/shard_map/ppermute | solution.py:305
  22.0 11.3 %collective-permute-start.3 = (bf16[32,768]{1,0:T(8,128)(2,1)S(1)}, bf16[32,768]{1,0:T(8,128)(2,1)S(1)}, u32[]{:S(2)}, u32[]{:S(2)}) collective-permute-start(bf16[32,768]{1,0:T(8,128)(2,1)S(1)} %constant_dynamic-update-slice_fusion.refs_0_), channel_id=1, source_target_pairs={{0,96},{8,104},{16,112},{24,120},{32,64},{40,72},{48,80},{56,88},{... | collective-permute-start | bytes 147464 | tf_op jit(solution)/shard_map/ppermute | solution.py:305
  26.2 19.1 %copy-start.1 = (s32[4]{0:T(128)S(1)}, s32[4]{0:T(128)}, u32[]{:S(2)}) copy-start(s32[4]{0:T(128)} %param.11) | copy-start | bytes 52
  33.3 11.8 %collective-permute-start.4 = (bf16[128,768]{1,0:T(8,128)(2,1)S(1)}, bf16[128,768]{1,0:T(8,128)(2,1)S(1)}, u32[]{:S(2)}, u32[]{:S(2)}) collective-permute-start(bf16[128,768]{1,0:T(8,128)(2,1)S(1)} %join.2.refs_0_), channel_id=1, source_target_pairs={{0,16},{8,24},{16,0},{24,8},{32,48},{40,56},{48,32},{56,40},{64,80... | collective-permute-start | bytes 589832 | tf_op jit(solution)/shard_map/ppermute | solution.py:305
  45.2 10.7 %collective-permute-start.5 = (bf16[256,768]{1,0:T(8,128)(2,1)S(1)}, bf16[256,768]{1,0:T(8,128)(2,1)S(1)}, u32[]{:S(2)}, u32[]{:S(2)}) collective-permute-start(bf16[256,768]{1,0:T(8,128)(2,1)S(1)} %join.3), channel_id=1, source_target_pairs={{0,8},{8,0},{16,24},{24,16},{32,40},{40,32},{48,56},{56,48},{64,72... | collective-permute-start | bytes 1179656 | tf_op jit(solution)/shard_map/ppermute | solution.py:305
  46.2 20.5 %all-to-all-start.2 = ((f32[16,4,896]{2,1,0:T(4,128)}), f32[16,4,896]{2,1,0:T(4,128)S(1)}, u32[]{:S(2)}, u32[]{:S(2)}) async-start(f32[16,4,896]{2,1,0:T(4,128)} %get-tuple-element.11), calls=%async_computation.2 | async-start | bytes 458752 | tf_op jit(solution)/shard_map/all_to_all | solution.py:327
  57.0 5.2 %collective-permute-start.7 = (f32[4,768]{1,0:T(4,128)S(1)}, f32[4,768]{1,0:T(4,128)S(1)}, u32[]{:S(2)}, u32[]{:S(2)}) collective-permute-start(f32[4,768]{1,0:T(4,128)S(1)} %clip_part.1), channel_id=1, source_target_pairs={{0,2},{1,3},{2,0},{3,1},{4,6},{5,7},{6,4},{7,5},{8,10},{9,11},{10,... | collective-permute-start | bytes 36872 | tf_op jit(solution)/shard_map/ppermute | solution.py:305
  58.2 4.9 %collective-permute-start.8 = (f32[4,768]{1,0:T(4,128)S(1)}, f32[4,768]{1,0:T(4,128)S(1)}, u32[]{:S(2)}, u32[]{:S(2)}) collective-permute-start(f32[4,768]{1,0:T(4,128)S(1)} %clip_part.1), channel_id=1, source_target_pairs={{0,3},{1,2},{2,1},{3,0},{4,7},{5,6},{6,5},{7,4},{8,11},{9,10},{10,... | collective-permute-start | bytes 36872 | tf_op jit(solution)/shard_map/ppermute | solution.py:305
  60.4 3.7 %collective-permute-start.6 = (f32[4,768]{1,0:T(4,128)S(1)}, f32[4,768]{1,0:T(4,128)S(1)}, u32[]{:S(2)}, u32[]{:S(2)}) collective-permute-start(f32[4,768]{1,0:T(4,128)S(1)} %clip_part.1), channel_id=1, source_target_pairs={{0,1},{1,0},{2,3},{3,2},{4,5},{5,4},{6,7},{7,6},{8,9},{9,8},{10,11... | collective-permute-start | bytes 36872 | tf_op jit(solution)/shard_map/ppermute | solution.py:305
  64.1 5.3 %collective-permute-start.9 = (f32[4,768]{1,0:T(4,128)S(1)}, f32[4,768]{1,0:T(4,128)S(1)}, u32[]{:S(2)}, u32[]{:S(2)}) collective-permute-start(f32[4,768]{1,0:T(4,128)S(1)} %add_add_fusion), channel_id=1, source_target_pairs={{0,4},{1,5},{2,6},{3,7},{4,0},{5,1},{6,2},{7,3},{8,12},{9,13},{10,... | collective-permute-start | bytes 36872 | tf_op jit(solution)/shard_map/ppermute | solution.py:305
  66.6 3.5 %collective-permute-start.10 = (f32[16,4,896]{2,1,0:T(4,128)S(1)}, f32[16,4,896]{2,1,0:T(4,128)S(1)}, u32[]{:S(2)}, u32[]{:S(2)}) collective-permute-start(f32[16,4,896]{2,1,0:T(4,128)S(1)} %all-to-all-done.2.units_ref), channel_id=1, source_target_pairs={{0,8},{8,0},{16,24},{24,16},{32,40},{40,32},{48,56},{56,48},{64,72... | collective-permute-start | bytes 688136 | tf_op jit(solution)/shard_map/ppermute | solution.py:305

commit v6 on v5

--- a/solution.py
+++ b/solution.py
@@ -61,9 +61,6 @@
     for start, width in ((2 * WIDTH, 2 * WIDTH),):
         bring(wqkv_hbm, wqkv, pl.ds(start, width))
         bring(wqkv_hbm, wqkv, pl.ds(D + start, width))
-    bring(wqkv_hbm, wqkv, pl.ds(2 * D, D))
-    bring(wout_hbm, wout, pl.ds(0, D))
-    bring(wproj_hbm, wproj, pl.ds(0, E))
 
     x = jnp.concatenate([x_ref[:, 16 * b : 16 * b + 16, :].reshape(ROWS, D) for b in range(BLOCKS)], axis=0)
     lane = lax.broadcasted_iota(jnp.int32, (ROWS, WIDTH), 1) // HEAD
@@ -80,6 +77,9 @@
             if j == AHEAD:
                 copies[0].wait()
                 copies[1].wait()
+                bring(wqkv_hbm, wqkv, pl.ds(2 * D, D))
+                bring(wout_hbm, wout, pl.ds(0, D))
+                bring(wproj_hbm, wproj, pl.ds(0, E))
             query, keys = wqkv[:, columns], wqkv[:, D + j * WIDTH : D + (j + 1) * WIDTH]
         return dot(x, query).astype(BF16), dot(x, keys).astype(BF16)
 

time: 71.9 us -> 71.1 us (0.989)
  Pallas kernels: 12.3 us -> 11.5 us
    pallas_call x1, Pallas kernels: 7.1 us -> 6.28 us  [temporal(): pl.pallas_call(temporal_kernel, out_shape=pltpu.VMEM((8, 8, LANES), F32),...]
where the time goes in v6:
time: 71.1 us; the launch traced here: 70.5 us
  starting transfers between devices  33.1 us (47%)
  waiting for transfers between devices  11.6 us (16%)
  Pallas kernels  11.5 us (16%)
  blocking collectives  10.3 us (14%)
  local copies, waits for them, and re-layouts  2.51 us (4%)
  other arithmetic  0.81 us (1%)
  between operations  0.74 us (1%)
    ppermute x11, starting transfers between devices, swapped(): lax.ppermute(value, axis, [(i, i ^ bit) for i in range(lax.axis_size(axis...  17.4 us
    all_to_all x1, blocking collectives, per_device(): parts = lax.all_to_all(parts, 'narrow', 0, 0, tiled=True)  10.3 us
    all_to_all x1, starting transfers between devices, per_device(): lax.all_to_all(outgoing, 'wide', 0, 0, axis_index_groups=same_core, tiled...  9.73 us
    pallas_call x1, Pallas kernels, temporal(): pl.pallas_call(temporal_kernel, out_shape=pltpu.VMEM((8, 8, LANES), F32),...  6.28 us
    all_to_all x1, starting transfers between devices, per_device(): tokens = lax.all_to_all(send, 'narrow', 0, 0, tiled=True)  6.03 us
    ppermute x11, waiting for transfers between devices, swapped(): lax.ppermute(value, axis, [(i, i ^ bit) for i in range(lax.axis_size(axis...  6.03 us
    all_to_all x1, waiting for transfers between devices, per_device(): tokens = lax.all_to_all(send, 'narrow', 0, 0, tiled=True)  3.72 us
    reshape x1, local copies, waits for them, and re-layouts, per_device(): video.reshape(4, 2, 8, 8, D).transpose(0, 2, 1, 3, 4).reshape(8, 64, D)  2.31 us
  transfers between devices with their start and end apart: 13, of which 7 were waited for; matrix products, arithmetic and copies ran while one was open for 1% of the time, Pallas kernels for 15%

profile of v6, /device:TPU:8, one launch (start us, length us, event | category | flops | bytes accessed | tf_op | source)
XLA Modules:
  0.0 70.5 jit_solution(670142867379768866)
XLA Ops:
  0.6 2.3 %copy.9 = bf16[4,2,8,8,1024]{4,3,1,2,0:T(8,128)(2,1)} copy(bf16[4,2,8,8,1024]{4,3,2,1,0:T(8,128)(2,1)} %bitcast.4) | data formatting | bytes 2097152 | tf_op jit(solution)/shard_map/reshape | solution.py:313
  2.9 6.0 %all-to-all-start = ((bf16[8,64,1024]{2,1,0:T(8,128)(2,1)}), bf16[8,64,1024]{2,1,0:T(8,128)(2,1)S(1)}, u32[]{:S(2)}, u32[]{:S(2)}) async-start(bf16[8,64,1024]{2,1,0:T(8,128)(2,1)} %bitcast.2), calls=%async_computation | async-start | bytes 2097152 | tf_op jit(solution)/shard_map/all_to_all | solution.py:314
  9.0 7.3 %collective-permute-start = (bf16[16,768]{1,0:T(8,128)(2,1)S(1)}, bf16[16,768]{1,0:T(8,128)(2,1)S(1)}, u32[]{:S(2)}, u32[]{:S(2)}) collective-permute-start(bf16[16,768]{1,0:T(8,128)(2,1)S(1)} %copy-done), channel_id=1, source_target_pairs={{0,128},{8,136},{16,144},{24,152},{32,160},{40,168},{48,176},{56,1... | collective-permute-start | bytes 73736 | tf_op jit(solution)/shard_map/ppermute | solution.py:305
  16.3 1.6 %fetch.1 = (bf16[1024,512]{1,0:T(8,128)(2,1)S(1)}, bf16[1024,512]{1,0:T(8,128)(2,1)S(1)}) custom-call(bf16[1024,3072]{1,0:T(8,128)(2,1)} %wqkv_hbm.1), custom_call_target="tpu_custom_call" | custom-call | bytes 4194304 | tf_op jit(solution)/shard_map/fetch/pallas_call | solution.py:140
  17.8 0.2 collective-permute-done
  18.1 1.0 %collective-permute-start.1 = (bf16[32,768]{1,0:T(8,128)(2,1)S(1)}, bf16[32,768]{1,0:T(8,128)(2,1)S(1)}, u32[]{:S(2)}, u32[]{:S(2)}) collective-permute-start(bf16[32,768]{1,0:T(8,128)(2,1)S(1)} %constant_dynamic-update-slice_fusion.refs_0_), channel_id=1, source_target_pairs={{0,32},{8,40},{16,48},{24,56},{32,0},{40,8},{48,16},{56,24},{64,96... | collective-permute-start | bytes 147464 | tf_op jit(solution)/shard_map/ppermute | solution.py:305
  19.1 2.9 %collective-permute-start.2 = (bf16[32,768]{1,0:T(8,128)(2,1)S(1)}, bf16[32,768]{1,0:T(8,128)(2,1)S(1)}, u32[]{:S(2)}, u32[]{:S(2)}) collective-permute-start(bf16[32,768]{1,0:T(8,128)(2,1)S(1)} %constant_dynamic-update-slice_fusion.refs_0_), channel_id=1, source_target_pairs={{0,64},{8,72},{16,80},{24,88},{32,96},{40,104},{48,112},{56,120},{... | collective-permute-start | bytes 147464 | tf_op jit(solution)/shard_map/ppermute | solution.py:305
  22.0 0.5 collective-permute-start.3
  22.5 3.7 %all-to-all-done.x_ref = bf16[8,64,1024]{2,1,0:T(8,128)(2,1)S(1)} async-done(((bf16[8,64,1024]{2,1,0:T(8,128)(2,1)}), bf16[8,64,1024]{2,1,0:T(8,128)(2,1)S(1)}, u32[]{:S(2)}, u32[]{:S(2)}) %all-to-all-start) | async-done | bytes 1048608 | tf_op jit(solution)/shard_map/all_to_all | solution.py:314
  26.2 6.3 %temporal.1.after_ref = f32[8,8,128]{2,1,0:T(8,128)S(1)} custom-call(bf16[8,64,1024]{2,1,0:T(8,128)(2,1)S(1)} %all-to-all-done.x_ref, bf16[1024,512]{1,0:T(8,128)(2,1)S(1)} %get-tuple-element.7.query_ref, bf16[1024,512]{1,0:T(8,128)(2,1)S(1)} %get-tuple-element.8.keys_ref, bf16[1024,3072]{1,0:T(8,128)(2,1)} %wqkv_hbm.1, bf16[1024,1024]{1,0:T(8,128)(2,1)} %wout_hbm.1, ...), custom_call_target="tpu_custom_call" | custom-call | flops 3221225472 | bytes 11534336 | tf_op jit(solution)/shard_map/temporal/pallas_call | solution.py:153
  32.5 0.0 collective-permute-done.2.refs_2_
  32.5 1.4 %collective-permute-start.4 = (bf16[128,768]{1,0:T(8,128)(2,1)S(1)}, bf16[128,768]{1,0:T(8,128)(2,1)S(1)}, u32[]{:S(2)}, u32[]{:S(2)}) collective-permute-start(bf16[128,768]{1,0:T(8,128)(2,1)S(1)} %join.2.refs_0_), channel_id=1, source_target_pairs={{0,16},{8,24},{16,0},{24,8},{32,48},{40,56},{48,32},{56,40},{64,80... | collective-permute-start | bytes 589832 | tf_op jit(solution)/shard_map/ppermute | solution.py:305
  34.0 10.3 %all_to_all.15.parts_ref.after_ref = f32[8,8,128]{2,1,0:T(8,128)S(1)} all-to-all(f32[8,8,128]{2,1,0:T(8,128)S(1)} %temporal.1.after_ref), channel_id=1, replica_groups=mesh['wide'=32,'narrow'=8] {'narrow'}, dimensions={0} | all-to-all | bytes 65536 | tf_op jit(solution)/shard_map/all_to_all | solution.py:322
  44.3 0.1 collective-permute-start.5
  44.5 0.1 broadcast_in_dim.2.positive_ref
  44.5 0.8 %units.1 = (f32[4,896]{1,0:T(4,128)S(1)}, f32[4,128]{1,0:T(4,128)S(1)}, f32[16,4,896]{2,1,0:T(4,128)}) custom-call(f32[4,128]{1,0:T(4,128)S(1)} %broadcast_in_dim.2.positive_ref, f32[8,8,128]{2,1,0:T(8,128)S(1)} %all_to_all.15.parts_ref.after_ref), custom_call_target="tpu_custom_call" | custom-call | tf_op jit(solution)/shard_map/units/pallas_call | solution.py:233
  45.3 9.7 %all-to-all-start.2 = ((f32[16,4,896]{2,1,0:T(4,128)}), f32[16,4,896]{2,1,0:T(4,128)S(1)}, u32[]{:S(2)}, u32[]{:S(2)}) async-start(f32[16,4,896]{2,1,0:T(4,128)} %get-tuple-element.11), calls=%async_computation.2 | async-start | bytes 458752 | tf_op jit(solution)/shard_map/all_to_all | solution.py:327
  55.1 1.1 %clip_part.1 = f32[4,768]{1,0:T(4,128)S(1)} custom-call(f32[4,896]{1,0:T(4,128)S(1)} %get-tuple-element.9.unit_ref, bf16[128,768]{1,0:T(8,128)(2,1)S(1)} %join.2.refs_0_, bf16[128,768]{1,0:T(8,128)(2,1)S(1)} %collective-permute-done.4.refs_1_, bf16[256,768]{1,0:T(8,128)(2,1)S(1)} %collective-permute-done.5.refs_2_), custom_call_target="tpu_custom_call" | custom-call | flops 104857600 | bytes 1048576 | tf_op jit(solution)/shard_map/clip_part/pallas_call | solution.py:260
  56.2 1.2 %collective-permute-start.7 = (f32[4,768]{1,0:T(4,128)S(1)}, f32[4,768]{1,0:T(4,128)S(1)}, u32[]{:S(2)}, u32[]{:S(2)}) collective-permute-start(f32[4,768]{1,0:T(4,128)S(1)} %clip_part.1), channel_id=1, source_target_pairs={{0,2},{1,3},{2,0},{3,1},{4,6},{5,7},{6,4},{7,5},{8,10},{9,11},{10,... | collective-permute-start | bytes 36872 | tf_op jit(solution)/shard_map/ppermute | solution.py:305
  57.4 2.2 %collective-permute-start.8 = (f32[4,768]{1,0:T(4,128)S(1)}, f32[4,768]{1,0:T(4,128)S(1)}, u32[]{:S(2)}, u32[]{:S(2)}) collective-permute-start(f32[4,768]{1,0:T(4,128)S(1)} %clip_part.1), channel_id=1, source_target_pairs={{0,3},{1,2},{2,1},{3,0},{4,7},{5,6},{6,5},{7,4},{8,11},{9,10},{10,... | collective-permute-start | bytes 36872 | tf_op jit(solution)/shard_map/ppermute | solution.py:305
  59.6 0.2 collective-permute-start.6
  59.7 1.7 %collective-permute-done.7 = f32[4,768]{1,0:T(4,128)S(1)} collective-permute-done((f32[4,768]{1,0:T(4,128)S(1)}, f32[4,768]{1,0:T(4,128)S(1)}, u32[]{:S(2)}, u32[]{:S(2)}) %collective-permute-start.7) | collective-permute-done | bytes 12320 | tf_op jit(solution)/shard_map/ppermute | solution.py:305
  61.4 0.9 %collective-permute-done.8 = f32[4,768]{1,0:T(4,128)S(1)} collective-permute-done((f32[4,768]{1,0:T(4,128)S(1)}, f32[4,768]{1,0:T(4,128)S(1)}, u32[]{:S(2)}, u32[]{:S(2)}) %collective-permute-start.8) | collective-permute-done | bytes 12320 | tf_op jit(solution)/shard_map/ppermute | solution.py:305
  62.3 0.9 %collective-permute-done.6 = f32[4,768]{1,0:T(4,128)S(1)} collective-permute-done((f32[4,768]{1,0:T(4,128)S(1)}, f32[4,768]{1,0:T(4,128)S(1)}, u32[]{:S(2)}, u32[]{:S(2)}) %collective-permute-start.6) | collective-permute-done | bytes 12320 | tf_op jit(solution)/shard_map/ppermute | solution.py:305
  63.3 0.6 collective-permute-start.9
  63.9 0.1 slice_reduce_fusion
  64.0 1.8 %all-to-all-done.2.units_ref = f32[16,4,896]{2,1,0:T(4,128)S(1)} async-done(((f32[16,4,896]{2,1,0:T(4,128)}), f32[16,4,896]{2,1,0:T(4,128)S(1)}, u32[]{:S(2)}, u32[]{:S(2)}) %all-to-all-start.2) | async-done | bytes 229408 | tf_op jit(solution)/shard_map/all_to_all | solution.py:327
  65.8 0.5 caption_near.1.part_ref
  66.3 2.3 %collective-permute-done.9 = f32[4,768]{1,0:T(4,128)S(1)} collective-permute-done((f32[4,768]{1,0:T(4,128)S(1)}, f32[4,768]{1,0:T(4,128)S(1)}, u32[]{:S(2)}, u32[]{:S(2)}) %collective-permute-start.9) | collective-permute-done | bytes 12320 | tf_op jit(solution)/shard_map/ppermute | solution.py:305
  68.5 0.1 multiply_reduce_fusion
  68.7 0.7 subtract_divide_fusion
  69.4 1.2 %caption_far.1 = f32[16,768]{1,0:T(8,128)} custom-call(f32[16,4,896]{2,1,0:T(4,128)S(1)} %collective-permute-done.10.units_ref, f32[16,768]{1,0:T(8,128)S(1)} %caption_near.1.part_ref, bf16[16,768]{1,0:T(8,128)(2,1)S(1)} %copy-done), custom_call_target="tpu_custom_call" | custom-call | tf_op jit(solution)/shard_map/caption_far/pallas_call | solution.py:332
  (16 shorter events, 0.1 us)
Async XLA Ops:
  0.6 8.4 %copy-start = (bf16[16,768]{1,0:T(8,128)(2,1)S(1)}, bf16[16,768]{1,0:T(8,128)(2,1)}, u32[]{:S(2)}) copy-start(bf16[16,768]{1,0:T(8,128)(2,1)} %cap_ref.3) | copy-start | bytes 73732
  2.9 23.2 %all-to-all-start = ((bf16[8,64,1024]{2,1,0:T(8,128)(2,1)}), bf16[8,64,1024]{2,1,0:T(8,128)(2,1)S(1)}, u32[]{:S(2)}, u32[]{:S(2)}) async-start(bf16[8,64,1024]{2,1,0:T(8,128)(2,1)} %bitcast.2), calls=%async_computation | async-start | bytes 2097152 | tf_op jit(solution)/shard_map/all_to_all | solution.py:314
  9.0 9.1 %collective-permute-start = (bf16[16,768]{1,0:T(8,128)(2,1)S(1)}, bf16[16,768]{1,0:T(8,128)(2,1)S(1)}, u32[]{:S(2)}, u32[]{:S(2)}) collective-permute-start(bf16[16,768]{1,0:T(8,128)(2,1)S(1)} %copy-done), channel_id=1, source_target_pairs={{0,128},{8,136},{16,144},{24,152},{32,160},{40,168},{48,176},{56,1... | collective-permute-start | bytes 73736 | tf_op jit(solution)/shard_map/ppermute | solution.py:305
  18.1 14.4 %collective-permute-start.1 = (bf16[32,768]{1,0:T(8,128)(2,1)S(1)}, bf16[32,768]{1,0:T(8,128)(2,1)S(1)}, u32[]{:S(2)}, u32[]{:S(2)}) collective-permute-start(bf16[32,768]{1,0:T(8,128)(2,1)S(1)} %constant_dynamic-update-slice_fusion.refs_0_), channel_id=1, source_target_pairs={{0,32},{8,40},{16,48},{24,56},{32,0},{40,8},{48,16},{56,24},{64,96... | collective-permute-start | bytes 147464 | tf_op jit(solution)/shard_map/ppermute | solution.py:305
  19.1 13.4 %collective-permute-start.2 = (bf16[32,768]{1,0:T(8,128)(2,1)S(1)}, bf16[32,768]{1,0:T(8,128)(2,1)S(1)}, u32[]{:S(2)}, u32[]{:S(2)}) collective-permute-start(bf16[32,768]{1,0:T(8,128)(2,1)S(1)} %constant_dynamic-update-slice_fusion.refs_0_), channel_id=1, source_target_pairs={{0,64},{8,72},{16,80},{24,88},{32,96},{40,104},{48,112},{56,120},{... | collective-permute-start | bytes 147464 | tf_op jit(solution)/shard_map/ppermute | solution.py:305
  22.0 10.5 %collective-permute-start.3 = (bf16[32,768]{1,0:T(8,128)(2,1)S(1)}, bf16[32,768]{1,0:T(8,128)(2,1)S(1)}, u32[]{:S(2)}, u32[]{:S(2)}) collective-permute-start(bf16[32,768]{1,0:T(8,128)(2,1)S(1)} %constant_dynamic-update-slice_fusion.refs_0_), channel_id=1, source_target_pairs={{0,96},{8,104},{16,112},{24,120},{32,64},{40,72},{48,80},{56,88},{... | collective-permute-start | bytes 147464 | tf_op jit(solution)/shard_map/ppermute | solution.py:305
  26.2 18.3 %copy-start.1 = (s32[4]{0:T(128)S(1)}, s32[4]{0:T(128)}, u32[]{:S(2)}) copy-start(s32[4]{0:T(128)} %param.11) | copy-start | bytes 52
  32.5 11.8 %collective-permute-start.4 = (bf16[128,768]{1,0:T(8,128)(2,1)S(1)}, bf16[128,768]{1,0:T(8,128)(2,1)S(1)}, u32[]{:S(2)}, u32[]{:S(2)}) collective-permute-start(bf16[128,768]{1,0:T(8,128)(2,1)S(1)} %join.2.refs_0_), channel_id=1, source_target_pairs={{0,16},{8,24},{16,0},{24,8},{32,48},{40,56},{48,32},{56,40},{64,80... | collective-permute-start | bytes 589832 | tf_op jit(solution)/shard_map/ppermute | solution.py:305
  44.3 10.7 %collective-permute-start.5 = (bf16[256,768]{1,0:T(8,128)(2,1)S(1)}, bf16[256,768]{1,0:T(8,128)(2,1)S(1)}, u32[]{:S(2)}, u32[]{:S(2)}) collective-permute-start(bf16[256,768]{1,0:T(8,128)(2,1)S(1)} %join.3), channel_id=1, source_target_pairs={{0,8},{8,0},{16,24},{24,16},{32,40},{40,32},{48,56},{56,48},{64,72... | collective-permute-start | bytes 1179656 | tf_op jit(solution)/shard_map/ppermute | solution.py:305
  45.3 20.5 %all-to-all-start.2 = ((f32[16,4,896]{2,1,0:T(4,128)}), f32[16,4,896]{2,1,0:T(4,128)S(1)}, u32[]{:S(2)}, u32[]{:S(2)}) async-start(f32[16,4,896]{2,1,0:T(4,128)} %get-tuple-element.11), calls=%async_computation.2 | async-start | bytes 458752 | tf_op jit(solution)/shard_map/all_to_all | solution.py:327
  56.2 5.2 %collective-permute-start.7 = (f32[4,768]{1,0:T(4,128)S(1)}, f32[4,768]{1,0:T(4,128)S(1)}, u32[]{:S(2)}, u32[]{:S(2)}) collective-permute-start(f32[4,768]{1,0:T(4,128)S(1)} %clip_part.1), channel_id=1, source_target_pairs={{0,2},{1,3},{2,0},{3,1},{4,6},{5,7},{6,4},{7,5},{8,10},{9,11},{10,... | collective-permute-start | bytes 36872 | tf_op jit(solution)/shard_map/ppermute | solution.py:305
  57.4 4.9 %collective-permute-start.8 = (f32[4,768]{1,0:T(4,128)S(1)}, f32[4,768]{1,0:T(4,128)S(1)}, u32[]{:S(2)}, u32[]{:S(2)}) collective-permute-start(f32[4,768]{1,0:T(4,128)S(1)} %clip_part.1), channel_id=1, source_target_pairs={{0,3},{1,2},{2,1},{3,0},{4,7},{5,6},{6,5},{7,4},{8,11},{9,10},{10,... | collective-permute-start | bytes 36872 | tf_op jit(solution)/shard_map/ppermute | solution.py:305
  59.6 3.7 %collective-permute-start.6 = (f32[4,768]{1,0:T(4,128)S(1)}, f32[4,768]{1,0:T(4,128)S(1)}, u32[]{:S(2)}, u32[]{:S(2)}) collective-permute-start(f32[4,768]{1,0:T(4,128)S(1)} %clip_part.1), channel_id=1, source_target_pairs={{0,1},{1,0},{2,3},{3,2},{4,5},{5,4},{6,7},{7,6},{8,9},{9,8},{10,11... | collective-permute-start | bytes 36872 | tf_op jit(solution)/shard_map/ppermute | solution.py:305
  63.3 5.3 %collective-permute-start.9 = (f32[4,768]{1,0:T(4,128)S(1)}, f32[4,768]{1,0:T(4,128)S(1)}, u32[]{:S(2)}, u32[]{:S(2)}) collective-permute-start(f32[4,768]{1,0:T(4,128)S(1)} %add_add_fusion), channel_id=1, source_target_pairs={{0,4},{1,5},{2,6},{3,7},{4,0},{5,1},{6,2},{7,3},{8,12},{9,13},{10,... | collective-permute-start | bytes 36872 | tf_op jit(solution)/shard_map/ppermute | solution.py:305
  65.8 3.5 %collective-permute-start.10 = (f32[16,4,896]{2,1,0:T(4,128)S(1)}, f32[16,4,896]{2,1,0:T(4,128)S(1)}, u32[]{:S(2)}, u32[]{:S(2)}) collective-permute-start(f32[16,4,896]{2,1,0:T(4,128)S(1)} %all-to-all-done.2.units_ref), channel_id=1, source_target_pairs={{0,8},{8,0},{16,24},{24,16},{32,40},{40,32},{48,56},{56,48},{64,72... | collective-permute-start | bytes 688136 | tf_op jit(solution)/shard_map/ppermute | solution.py:305

commit v7 on v6

--- a/solution.py
+++ b/solution.py
@@ -292,13 +292,16 @@
     out_ref[...] = caption_sum(cap, lengths(cap.astype(F32)), stacked(units_ref))
 
 
-def far_kernel(units_ref, part_ref, cap_ref, out_ref):
+def last_kernel(units_ref, part_ref, cap_ref, own_ref, along_ref, unit_ref, length_ref, caption_ref, clip_ref):
+    unit = unit_ref[:, :E]
+    grad = own_ref[...]
+    clip_ref[...] = (grad - unit * along_ref[...]) / length_ref[:, :1]
     cap = cap_ref[...]
     value = cap.astype(F32)
     length = lengths(value)
     cap_unit = value / length
     grad = part_ref[...] + caption_sum(cap, length, stacked(units_ref))
-    out_ref[...] = (grad - cap_unit * jnp.sum(cap_unit * grad, axis=-1, keepdims=True)) / length
+    caption_ref[...] = (grad - cap_unit * jnp.sum(cap_unit * grad, axis=-1, keepdims=True)) / length
 
 
 def swapped(value, axis, bit):
@@ -329,13 +332,16 @@
     small = pltpu.CompilerParams(vmem_limit_bytes=24 << 20)
     shape = jax.ShapeDtypeStruct(captions.shape, F32)
     part = pl.pallas_call(near_kernel, out_shape=shape, compiler_params=small, name="caption_near")(units, captions)
-    caption_grad = pl.pallas_call(far_kernel, out_shape=shape, compiler_params=small, name="caption_far")(other, part, captions)
-
     others = [swapped(grad_unit, "narrow", bit) for bit in (1, 2, 3)]
     grad_unit = (grad_unit + others[0]) + (others[1] + others[2])
     grad_unit = grad_unit + swapped(grad_unit, "narrow", 4)
-    unit = unit[:, :E]
-    clip_grad = (grad_unit - unit * jnp.sum(unit * grad_unit, axis=-1, keepdims=True)) / length[:, :1]
+    along = jnp.sum(unit[:, :E] * grad_unit, axis=-1, keepdims=True)
+    caption_grad, clip_grad = pl.pallas_call(
+        last_kernel,
+        out_shape=(shape, jax.ShapeDtypeStruct((4, E), F32)),
+        compiler_params=small,
+        name="gradients",
+    )(other, part, captions, grad_unit, along, unit, length)
     return (clip_grad, caption_grad)
 
 

time: 71.1 us -> 70.9 us (level)
  transfers between devices with their start and end apart: 13 -> 13, of which waited for: 7 -> 7; matrix products, arithmetic and copies ran while one was open for 1% -> 0% of each run, Pallas kernels for 15% -> 15%
where the time goes in v7:
time: 70.9 us; the launch traced here: 70 us
  starting transfers between devices  33.1 us (47%)
  waiting for transfers between devices  11.7 us (17%)
  Pallas kernels  11.5 us (16%)
  blocking collectives  10.3 us (15%)
  local copies, waits for them, and re-layouts  2.49 us (4%)
  between operations  0.74 us (1%)
    ppermute x11, starting transfers between devices, swapped(): lax.ppermute(value, axis, [(i, i ^ bit) for i in range(lax.axis_size(axis...  17.3 us
    all_to_all x1, blocking collectives, per_device(): parts = lax.all_to_all(parts, 'narrow', 0, 0, tiled=True)  10.3 us
    all_to_all x1, starting transfers between devices, per_device(): lax.all_to_all(outgoing, 'wide', 0, 0, axis_index_groups=same_core, tiled...  9.73 us
    pallas_call x1, Pallas kernels, temporal(): pl.pallas_call(temporal_kernel, out_shape=pltpu.VMEM((8, 8, LANES), F32),...  6.28 us
    ppermute x11, waiting for transfers between devices, swapped(): lax.ppermute(value, axis, [(i, i ^ bit) for i in range(lax.axis_size(axis...  6.03 us
    all_to_all x1, starting transfers between devices, per_device(): tokens = lax.all_to_all(send, 'narrow', 0, 0, tiled=True)  6.03 us
    all_to_all x1, waiting for transfers between devices, per_device(): tokens = lax.all_to_all(send, 'narrow', 0, 0, tiled=True)  3.72 us
    reshape x1, local copies, waits for them, and re-layouts, per_device(): video.reshape(4, 2, 8, 8, D).transpose(0, 2, 1, 3, 4).reshape(8, 64, D)  2.31 us
  transfers between devices with their start and end apart: 13, of which 7 were waited for; matrix products, arithmetic and copies ran while one was open for 0% of the time, Pallas kernels for 15%

profile of v7, /device:TPU:8, one launch (start us, length us, event | category | flops | bytes accessed | tf_op | source)
XLA Modules:
  0.0 70.0 jit_solution(18023731956361168249)
XLA Ops:
  0.6 2.3 %copy.8 = bf16[4,2,8,8,1024]{4,3,1,2,0:T(8,128)(2,1)} copy(bf16[4,2,8,8,1024]{4,3,2,1,0:T(8,128)(2,1)} %bitcast.5) | data formatting | bytes 2097152 | tf_op jit(solution)/shard_map/reshape | solution.py:316
  2.9 6.0 %all-to-all-start = ((bf16[8,64,1024]{2,1,0:T(8,128)(2,1)}), bf16[8,64,1024]{2,1,0:T(8,128)(2,1)S(1)}, u32[]{:S(2)}, u32[]{:S(2)}) async-start(bf16[8,64,1024]{2,1,0:T(8,128)(2,1)} %bitcast.2), calls=%async_computation | async-start | bytes 2097152 | tf_op jit(solution)/shard_map/all_to_all | solution.py:317
  9.0 7.3 %collective-permute-start.1 = (bf16[16,768]{1,0:T(8,128)(2,1)S(1)}, bf16[16,768]{1,0:T(8,128)(2,1)S(1)}, u32[]{:S(2)}, u32[]{:S(2)}) collective-permute-start(bf16[16,768]{1,0:T(8,128)(2,1)S(1)} %copy-done), channel_id=1, source_target_pairs={{0,128},{8,136},{16,144},{24,152},{32,160},{40,168},{48,176},{56,1... | collective-permute-start | bytes 73736 | tf_op jit(solution)/shard_map/ppermute | solution.py:308
  16.3 1.6 %fetch.1 = (bf16[1024,512]{1,0:T(8,128)(2,1)S(1)}, bf16[1024,512]{1,0:T(8,128)(2,1)S(1)}) custom-call(bf16[1024,3072]{1,0:T(8,128)(2,1)} %wqkv_hbm.1), custom_call_target="tpu_custom_call" | custom-call | bytes 4194304 | tf_op jit(solution)/shard_map/fetch/pallas_call | solution.py:140
  17.8 0.2 collective-permute-done.1
  18.1 1.0 %collective-permute-start.2 = (bf16[32,768]{1,0:T(8,128)(2,1)S(1)}, bf16[32,768]{1,0:T(8,128)(2,1)S(1)}, u32[]{:S(2)}, u32[]{:S(2)}) collective-permute-start(bf16[32,768]{1,0:T(8,128)(2,1)S(1)} %constant_dynamic-update-slice_fusion.refs_0_), channel_id=1, source_target_pairs={{0,32},{8,40},{16,48},{24,56},{32,0},{40,8},{48,16},{56,24},{64,96... | collective-permute-start | bytes 147464 | tf_op jit(solution)/shard_map/ppermute | solution.py:308
  19.1 2.9 %collective-permute-start.3 = (bf16[32,768]{1,0:T(8,128)(2,1)S(1)}, bf16[32,768]{1,0:T(8,128)(2,1)S(1)}, u32[]{:S(2)}, u32[]{:S(2)}) collective-permute-start(bf16[32,768]{1,0:T(8,128)(2,1)S(1)} %constant_dynamic-update-slice_fusion.refs_0_), channel_id=1, source_target_pairs={{0,64},{8,72},{16,80},{24,88},{32,96},{40,104},{48,112},{56,120},{... | collective-permute-start | bytes 147464 | tf_op jit(solution)/shard_map/ppermute | solution.py:308
  22.0 0.5 collective-permute-start.4
  22.5 3.7 %all-to-all-done.x_ref = bf16[8,64,1024]{2,1,0:T(8,128)(2,1)S(1)} async-done(((bf16[8,64,1024]{2,1,0:T(8,128)(2,1)}), bf16[8,64,1024]{2,1,0:T(8,128)(2,1)S(1)}, u32[]{:S(2)}, u32[]{:S(2)}) %all-to-all-start) | async-done | bytes 1048608 | tf_op jit(solution)/shard_map/all_to_all | solution.py:317
  26.2 6.3 %temporal.1.after_ref = f32[8,8,128]{2,1,0:T(8,128)S(1)} custom-call(bf16[8,64,1024]{2,1,0:T(8,128)(2,1)S(1)} %all-to-all-done.x_ref, bf16[1024,512]{1,0:T(8,128)(2,1)S(1)} %get-tuple-element.9.query_ref, bf16[1024,512]{1,0:T(8,128)(2,1)S(1)} %get-tuple-element.10.keys_ref, bf16[1024,3072]{1,0:T(8,128)(2,1)} %wqkv_hbm.1, bf16[1024,1024]{1,0:T(8,128)(2,1)} %wout_hbm.1, ...), custom_call_target="tpu_custom_call" | custom-call | flops 3221225472 | bytes 11534336 | tf_op jit(solution)/shard_map/temporal/pallas_call | solution.py:153
  32.5 0.0 collective-permute-done.2.refs_1_
  32.5 0.0 collective-permute-done.3.refs_2_
  32.5 1.4 %collective-permute-start.5 = (bf16[128,768]{1,0:T(8,128)(2,1)S(1)}, bf16[128,768]{1,0:T(8,128)(2,1)S(1)}, u32[]{:S(2)}, u32[]{:S(2)}) collective-permute-start(bf16[128,768]{1,0:T(8,128)(2,1)S(1)} %join.2.refs_0_), channel_id=1, source_target_pairs={{0,16},{8,24},{16,0},{24,8},{32,48},{40,56},{48,32},{56,40},{64,80... | collective-permute-start | bytes 589832 | tf_op jit(solution)/shard_map/ppermute | solution.py:308
  34.0 10.3 %all_to_all.15.parts_ref.after_ref = f32[8,8,128]{2,1,0:T(8,128)S(1)} all-to-all(f32[8,8,128]{2,1,0:T(8,128)S(1)} %temporal.1.after_ref), channel_id=1, replica_groups=mesh['wide'=32,'narrow'=8] {'narrow'}, dimensions={0} | all-to-all | bytes 65536 | tf_op jit(solution)/shard_map/all_to_all | solution.py:325
  44.3 0.1 collective-permute-start.6
  44.5 0.1 broadcast_in_dim.4.positive_ref
  44.5 0.8 %units.1 = (f32[4,896]{1,0:T(4,128)S(1)}, f32[4,128]{1,0:T(4,128)S(1)}, f32[16,4,896]{2,1,0:T(4,128)}) custom-call(f32[4,128]{1,0:T(4,128)S(1)} %broadcast_in_dim.4.positive_ref, f32[8,8,128]{2,1,0:T(8,128)S(1)} %all_to_all.15.parts_ref.after_ref), custom_call_target="tpu_custom_call" | custom-call | tf_op jit(solution)/shard_map/units/pallas_call | solution.py:233
  45.3 9.7 %all-to-all-start.2 = ((f32[16,4,896]{2,1,0:T(4,128)}), f32[16,4,896]{2,1,0:T(4,128)S(1)}, u32[]{:S(2)}, u32[]{:S(2)}) async-start(f32[16,4,896]{2,1,0:T(4,128)} %get-tuple-element.11), calls=%async_computation.2 | async-start | bytes 458752 | tf_op jit(solution)/shard_map/all_to_all | solution.py:330
  55.1 1.1 %clip_part.1 = f32[4,768]{1,0:T(4,128)S(1)} custom-call(f32[4,896]{1,0:T(4,128)S(1)} %get-tuple-element.12.unit_ref, bf16[128,768]{1,0:T(8,128)(2,1)S(1)} %join.2.refs_0_, bf16[128,768]{1,0:T(8,128)(2,1)S(1)} %collective-permute-done.5.refs_1_, bf16[256,768]{1,0:T(8,128)(2,1)S(1)} %collective-permute-done.6.refs_2_), custom_call_target="tpu_custom_call" | custom-call | flops 104857600 | bytes 1048576 | tf_op jit(solution)/shard_map/clip_part/pallas_call | solution.py:260
  56.2 1.2 %collective-permute-start.8 = (f32[4,768]{1,0:T(4,128)S(1)}, f32[4,768]{1,0:T(4,128)S(1)}, u32[]{:S(2)}, u32[]{:S(2)}) collective-permute-start(f32[4,768]{1,0:T(4,128)S(1)} %clip_part.1), channel_id=1, source_target_pairs={{0,2},{1,3},{2,0},{3,1},{4,6},{5,7},{6,4},{7,5},{8,10},{9,11},{10,... | collective-permute-start | bytes 36872 | tf_op jit(solution)/shard_map/ppermute | solution.py:308
  57.4 2.2 %collective-permute-start.9 = (f32[4,768]{1,0:T(4,128)S(1)}, f32[4,768]{1,0:T(4,128)S(1)}, u32[]{:S(2)}, u32[]{:S(2)}) collective-permute-start(f32[4,768]{1,0:T(4,128)S(1)} %clip_part.1), channel_id=1, source_target_pairs={{0,3},{1,2},{2,1},{3,0},{4,7},{5,6},{6,5},{7,4},{8,11},{9,10},{10,... | collective-permute-start | bytes 36872 | tf_op jit(solution)/shard_map/ppermute | solution.py:308
  59.6 0.2 collective-permute-start.7
  59.7 1.7 %collective-permute-done.8 = f32[4,768]{1,0:T(4,128)S(1)} collective-permute-done((f32[4,768]{1,0:T(4,128)S(1)}, f32[4,768]{1,0:T(4,128)S(1)}, u32[]{:S(2)}, u32[]{:S(2)}) %collective-permute-start.8) | collective-permute-done | bytes 12320 | tf_op jit(solution)/shard_map/ppermute | solution.py:308
  61.4 0.9 %collective-permute-done.9 = f32[4,768]{1,0:T(4,128)S(1)} collective-permute-done((f32[4,768]{1,0:T(4,128)S(1)}, f32[4,768]{1,0:T(4,128)S(1)}, u32[]{:S(2)}, u32[]{:S(2)}) %collective-permute-start.9) | collective-permute-done | bytes 12320 | tf_op jit(solution)/shard_map/ppermute | solution.py:308
  62.3 0.9 %collective-permute-done.7 = f32[4,768]{1,0:T(4,128)S(1)} collective-permute-done((f32[4,768]{1,0:T(4,128)S(1)}, f32[4,768]{1,0:T(4,128)S(1)}, u32[]{:S(2)}, u32[]{:S(2)}) %collective-permute-start.7) | collective-permute-done | bytes 12320 | tf_op jit(solution)/shard_map/ppermute | solution.py:308
  63.3 0.6 collective-permute-start.10
  63.9 1.9 %all-to-all-done.2.units_ref = f32[16,4,896]{2,1,0:T(4,128)S(1)} async-done(((f32[16,4,896]{2,1,0:T(4,128)}), f32[16,4,896]{2,1,0:T(4,128)S(1)}, u32[]{:S(2)}, u32[]{:S(2)}) %all-to-all-start.2) | async-done | bytes 229408 | tf_op jit(solution)/shard_map/all_to_all | solution.py:330
  65.8 0.5 caption_near.1.part_ref
  66.3 2.3 %collective-permute-done.10 = f32[4,768]{1,0:T(4,128)S(1)} collective-permute-done((f32[4,768]{1,0:T(4,128)S(1)}, f32[4,768]{1,0:T(4,128)S(1)}, u32[]{:S(2)}, u32[]{:S(2)}) %collective-permute-start.10) | collective-permute-done | bytes 12320 | tf_op jit(solution)/shard_map/ppermute | solution.py:308
  68.5 0.1 multiply_reduce_fusion
  68.7 0.1 copy.9.along_ref
  68.8 1.2 %gradients.1 = (f32[16,768]{1,0:T(8,128)}, f32[4,768]{1,0:T(4,128)}) custom-call(f32[16,4,896]{2,1,0:T(4,128)S(1)} %collective-permute-done.units_ref, f32[16,768]{1,0:T(8,128)S(1)} %caption_near.1.part_ref, bf16[16,768]{1,0:T(8,128)(2,1)S(1)} %copy-done, f32[4,768]{1,0:T(4,128)S(1)} %get-tuple-element.17.own_ref, f32[4,1]{1,0:T(4,128)S(1)} %copy.9.along_ref, ...), custom_call_target="tpu_custom_call" | custom-call | tf_op jit(solution)/shard_map/gradients/pallas_call | solution.py:339
  (15 shorter events, 0.1 us)
Async XLA Ops:
  0.6 8.4 %copy-start = (bf16[16,768]{1,0:T(8,128)(2,1)S(1)}, bf16[16,768]{1,0:T(8,128)(2,1)}, u32[]{:S(2)}) copy-start(bf16[16,768]{1,0:T(8,128)(2,1)} %cap_ref.3) | copy-start | bytes 73732
  2.9 23.2 %all-to-all-start = ((bf16[8,64,1024]{2,1,0:T(8,128)(2,1)}), bf16[8,64,1024]{2,1,0:T(8,128)(2,1)S(1)}, u32[]{:S(2)}, u32[]{:S(2)}) async-start(bf16[8,64,1024]{2,1,0:T(8,128)(2,1)} %bitcast.2), calls=%async_computation | async-start | bytes 2097152 | tf_op jit(solution)/shard_map/all_to_all | solution.py:317
  9.0 9.1 %collective-permute-start.1 = (bf16[16,768]{1,0:T(8,128)(2,1)S(1)}, bf16[16,768]{1,0:T(8,128)(2,1)S(1)}, u32[]{:S(2)}, u32[]{:S(2)}) collective-permute-start(bf16[16,768]{1,0:T(8,128)(2,1)S(1)} %copy-done), channel_id=1, source_target_pairs={{0,128},{8,136},{16,144},{24,152},{32,160},{40,168},{48,176},{56,1... | collective-permute-start | bytes 73736 | tf_op jit(solution)/shard_map/ppermute | solution.py:308
  18.1 14.4 %collective-permute-start.2 = (bf16[32,768]{1,0:T(8,128)(2,1)S(1)}, bf16[32,768]{1,0:T(8,128)(2,1)S(1)}, u32[]{:S(2)}, u32[]{:S(2)}) collective-permute-start(bf16[32,768]{1,0:T(8,128)(2,1)S(1)} %constant_dynamic-update-slice_fusion.refs_0_), channel_id=1, source_target_pairs={{0,32},{8,40},{16,48},{24,56},{32,0},{40,8},{48,16},{56,24},{64,96... | collective-permute-start | bytes 147464 | tf_op jit(solution)/shard_map/ppermute | solution.py:308
  19.1 13.4 %collective-permute-start.3 = (bf16[32,768]{1,0:T(8,128)(2,1)S(1)}, bf16[32,768]{1,0:T(8,128)(2,1)S(1)}, u32[]{:S(2)}, u32[]{:S(2)}) collective-permute-start(bf16[32,768]{1,0:T(8,128)(2,1)S(1)} %constant_dynamic-update-slice_fusion.refs_0_), channel_id=1, source_target_pairs={{0,64},{8,72},{16,80},{24,88},{32,96},{40,104},{48,112},{56,120},{... | collective-permute-start | bytes 147464 | tf_op jit(solution)/shard_map/ppermute | solution.py:308
  22.0 10.5 %collective-permute-start.4 = (bf16[32,768]{1,0:T(8,128)(2,1)S(1)}, bf16[32,768]{1,0:T(8,128)(2,1)S(1)}, u32[]{:S(2)}, u32[]{:S(2)}) collective-permute-start(bf16[32,768]{1,0:T(8,128)(2,1)S(1)} %constant_dynamic-update-slice_fusion.refs_0_), channel_id=1, source_target_pairs={{0,96},{8,104},{16,112},{24,120},{32,64},{40,72},{48,80},{56,88},{... | collective-permute-start | bytes 147464 | tf_op jit(solution)/shard_map/ppermute | solution.py:308
  26.2 18.3 %copy-start.1 = (s32[4]{0:T(128)S(1)}, s32[4]{0:T(128)}, u32[]{:S(2)}) copy-start(s32[4]{0:T(128)} %param.11) | copy-start | bytes 52
  32.5 11.8 %collective-permute-start.5 = (bf16[128,768]{1,0:T(8,128)(2,1)S(1)}, bf16[128,768]{1,0:T(8,128)(2,1)S(1)}, u32[]{:S(2)}, u32[]{:S(2)}) collective-permute-start(bf16[128,768]{1,0:T(8,128)(2,1)S(1)} %join.2.refs_0_), channel_id=1, source_target_pairs={{0,16},{8,24},{16,0},{24,8},{32,48},{40,56},{48,32},{56,40},{64,80... | collective-permute-start | bytes 589832 | tf_op jit(solution)/shard_map/ppermute | solution.py:308
  44.3 10.7 %collective-permute-start.6 = (bf16[256,768]{1,0:T(8,128)(2,1)S(1)}, bf16[256,768]{1,0:T(8,128)(2,1)S(1)}, u32[]{:S(2)}, u32[]{:S(2)}) collective-permute-start(bf16[256,768]{1,0:T(8,128)(2,1)S(1)} %join.3), channel_id=1, source_target_pairs={{0,8},{8,0},{16,24},{24,16},{32,40},{40,32},{48,56},{56,48},{64,72... | collective-permute-start | bytes 1179656 | tf_op jit(solution)/shard_map/ppermute | solution.py:308
  45.3 20.5 %all-to-all-start.2 = ((f32[16,4,896]{2,1,0:T(4,128)}), f32[16,4,896]{2,1,0:T(4,128)S(1)}, u32[]{:S(2)}, u32[]{:S(2)}) async-start(f32[16,4,896]{2,1,0:T(4,128)} %get-tuple-element.11), calls=%async_computation.2 | async-start | bytes 458752 | tf_op jit(solution)/shard_map/all_to_all | solution.py:330
  56.2 5.2 %collective-permute-start.8 = (f32[4,768]{1,0:T(4,128)S(1)}, f32[4,768]{1,0:T(4,128)S(1)}, u32[]{:S(2)}, u32[]{:S(2)}) collective-permute-start(f32[4,768]{1,0:T(4,128)S(1)} %clip_part.1), channel_id=1, source_target_pairs={{0,2},{1,3},{2,0},{3,1},{4,6},{5,7},{6,4},{7,5},{8,10},{9,11},{10,... | collective-permute-start | bytes 36872 | tf_op jit(solution)/shard_map/ppermute | solution.py:308
  57.4 4.9 %collective-permute-start.9 = (f32[4,768]{1,0:T(4,128)S(1)}, f32[4,768]{1,0:T(4,128)S(1)}, u32[]{:S(2)}, u32[]{:S(2)}) collective-permute-start(f32[4,768]{1,0:T(4,128)S(1)} %clip_part.1), channel_id=1, source_target_pairs={{0,3},{1,2},{2,1},{3,0},{4,7},{5,6},{6,5},{7,4},{8,11},{9,10},{10,... | collective-permute-start | bytes 36872 | tf_op jit(solution)/shard_map/ppermute | solution.py:308
  59.6 3.7 %collective-permute-start.7 = (f32[4,768]{1,0:T(4,128)S(1)}, f32[4,768]{1,0:T(4,128)S(1)}, u32[]{:S(2)}, u32[]{:S(2)}) collective-permute-start(f32[4,768]{1,0:T(4,128)S(1)} %clip_part.1), channel_id=1, source_target_pairs={{0,1},{1,0},{2,3},{3,2},{4,5},{5,4},{6,7},{7,6},{8,9},{9,8},{10,11... | collective-permute-start | bytes 36872 | tf_op jit(solution)/shard_map/ppermute | solution.py:308
  63.3 5.3 %collective-permute-start.10 = (f32[4,768]{1,0:T(4,128)S(1)}, f32[4,768]{1,0:T(4,128)S(1)}, u32[]{:S(2)}, u32[]{:S(2)}) collective-permute-start(f32[4,768]{1,0:T(4,128)S(1)} %add_add_fusion), channel_id=1, source_target_pairs={{0,4},{1,5},{2,6},{3,7},{4,0},{5,1},{6,2},{7,3},{8,12},{9,13},{10,... | collective-permute-start | bytes 36872 | tf_op jit(solution)/shard_map/ppermute | solution.py:308
  65.8 2.9 %collective-permute-start = (f32[16,4,896]{2,1,0:T(4,128)S(1)}, f32[16,4,896]{2,1,0:T(4,128)S(1)}, u32[]{:S(2)}, u32[]{:S(2)}) collective-permute-start(f32[16,4,896]{2,1,0:T(4,128)S(1)} %all-to-all-done.2.units_ref), channel_id=1, source_target_pairs={{0,8},{8,0},{16,24},{24,16},{32,40},{40,32},{48,56},{56,48},{64,72... | collective-permute-start | bytes 688136 | tf_op jit(solution)/shard_map/ppermute | solution.py:308

commit v8 on v7

--- a/solution.py
+++ b/solution.py
@@ -252,7 +252,12 @@
     logits = jnp.concatenate([dot_t(terms, cap) for cap in caps], axis=1)
     logits = (logits[:4] + logits[4:8] + logits[8:12]) * scale + BIAS
     hit = caption_ids(logits.shape, 1, rows, True).astype(F32) == unit_ref[:, E : E + 1]
-    grad = dot(jnp.concatenate(parts_of(slope(logits, hit) * scale, 3), axis=0), jnp.concatenate(caps, axis=0))
+    weight = jnp.concatenate(parts_of(slope(logits, hit) * scale, 3), axis=0)
+    grad = jnp.zeros((12, E), F32)
+    start = 0
+    for cap in caps:
+        grad += dot(weight[:, start : start + cap.shape[0]], cap)
+        start += cap.shape[0]
     grad_ref[...] = grad[:4] + grad[4:8] + grad[8:12]
 
 

time: 70.9 us -> 70.9 us (level)
  no operation moved by 1% of the time
where the time goes in v8:
time: 70.9 us; the launch traced here: 69.9 us
  starting transfers between devices  33.1 us (47%)
  waiting for transfers between devices  11.7 us (17%)
  Pallas kernels  11.4 us (16%)
  blocking collectives  10.3 us (15%)
  local copies, waits for them, and re-layouts  2.49 us (4%)
  between operations  0.74 us (1%)
    ppermute x11, starting transfers between devices, swapped(): lax.ppermute(value, axis, [(i, i ^ bit) for i in range(lax.axis_size(axis...  17.4 us
    all_to_all x1, blocking collectives, per_device(): parts = lax.all_to_all(parts, 'narrow', 0, 0, tiled=True)  10.3 us
    all_to_all x1, starting transfers between devices, per_device(): lax.all_to_all(outgoing, 'wide', 0, 0, axis_index_groups=same_core, tiled...  9.73 us
    pallas_call x1, Pallas kernels, temporal(): pl.pallas_call(temporal_kernel, out_shape=pltpu.VMEM((8, 8, LANES), F32),...  6.28 us
    all_to_all x1, starting transfers between devices, per_device(): tokens = lax.all_to_all(send, 'narrow', 0, 0, tiled=True)  6.03 us
    ppermute x11, waiting for transfers between devices, swapped(): lax.ppermute(value, axis, [(i, i ^ bit) for i in range(lax.axis_size(axis...  6 us
    all_to_all x1, waiting for transfers between devices, per_device(): tokens = lax.all_to_all(send, 'narrow', 0, 0, tiled=True)  3.72 us
    reshape x1, local copies, waits for them, and re-layouts, per_device(): video.reshape(4, 2, 8, 8, D).transpose(0, 2, 1, 3, 4).reshape(8, 64, D)  2.31 us
  transfers between devices with their start and end apart: 13, of which 7 were waited for; matrix products, arithmetic and copies ran while one was open for 0% of the time, Pallas kernels for 15%

profile of v8, /device:TPU:8, one launch (start us, length us, event | category | flops | bytes accessed | tf_op | source)
XLA Modules:
  0.0 69.9 jit_solution(7694012303826252970)
XLA Ops:
  0.6 2.3 %copy.8 = bf16[4,2,8,8,1024]{4,3,1,2,0:T(8,128)(2,1)} copy(bf16[4,2,8,8,1024]{4,3,2,1,0:T(8,128)(2,1)} %bitcast.5) | data formatting | bytes 2097152 | tf_op jit(solution)/shard_map/reshape | solution.py:321
  2.9 6.0 %all-to-all-start = ((bf16[8,64,1024]{2,1,0:T(8,128)(2,1)}), bf16[8,64,1024]{2,1,0:T(8,128)(2,1)S(1)}, u32[]{:S(2)}, u32[]{:S(2)}) async-start(bf16[8,64,1024]{2,1,0:T(8,128)(2,1)} %bitcast.2), calls=%async_computation | async-start | bytes 2097152 | tf_op jit(solution)/shard_map/all_to_all | solution.py:322
  9.0 7.3 %collective-permute-start.1 = (bf16[16,768]{1,0:T(8,128)(2,1)S(1)}, bf16[16,768]{1,0:T(8,128)(2,1)S(1)}, u32[]{:S(2)}, u32[]{:S(2)}) collective-permute-start(bf16[16,768]{1,0:T(8,128)(2,1)S(1)} %copy-done), channel_id=1, source_target_pairs={{0,128},{8,136},{16,144},{24,152},{32,160},{40,168},{48,176},{56,1... | collective-permute-start | bytes 73736 | tf_op jit(solution)/shard_map/ppermute | solution.py:313
  16.3 1.6 %fetch.1 = (bf16[1024,512]{1,0:T(8,128)(2,1)S(1)}, bf16[1024,512]{1,0:T(8,128)(2,1)S(1)}) custom-call(bf16[1024,3072]{1,0:T(8,128)(2,1)} %wqkv_hbm.1), custom_call_target="tpu_custom_call" | custom-call | bytes 4194304 | tf_op jit(solution)/shard_map/fetch/pallas_call | solution.py:140
  17.8 0.2 collective-permute-done.1
  18.1 1.0 %collective-permute-start.2 = (bf16[32,768]{1,0:T(8,128)(2,1)S(1)}, bf16[32,768]{1,0:T(8,128)(2,1)S(1)}, u32[]{:S(2)}, u32[]{:S(2)}) collective-permute-start(bf16[32,768]{1,0:T(8,128)(2,1)S(1)} %constant_dynamic-update-slice_fusion.refs_0_), channel_id=1, source_target_pairs={{0,32},{8,40},{16,48},{24,56},{32,0},{40,8},{48,16},{56,24},{64,96... | collective-permute-start | bytes 147464 | tf_op jit(solution)/shard_map/ppermute | solution.py:313
  19.1 2.9 %collective-permute-start.3 = (bf16[32,768]{1,0:T(8,128)(2,1)S(1)}, bf16[32,768]{1,0:T(8,128)(2,1)S(1)}, u32[]{:S(2)}, u32[]{:S(2)}) collective-permute-start(bf16[32,768]{1,0:T(8,128)(2,1)S(1)} %constant_dynamic-update-slice_fusion.refs_0_), channel_id=1, source_target_pairs={{0,64},{8,72},{16,80},{24,88},{32,96},{40,104},{48,112},{56,120},{... | collective-permute-start | bytes 147464 | tf_op jit(solution)/shard_map/ppermute | solution.py:313
  22.0 0.5 collective-permute-start.4
  22.5 3.7 %all-to-all-done.x_ref = bf16[8,64,1024]{2,1,0:T(8,128)(2,1)S(1)} async-done(((bf16[8,64,1024]{2,1,0:T(8,128)(2,1)}), bf16[8,64,1024]{2,1,0:T(8,128)(2,1)S(1)}, u32[]{:S(2)}, u32[]{:S(2)}) %all-to-all-start) | async-done | bytes 1048608 | tf_op jit(solution)/shard_map/all_to_all | solution.py:322
  26.2 6.3 %temporal.1.after_ref = f32[8,8,128]{2,1,0:T(8,128)S(1)} custom-call(bf16[8,64,1024]{2,1,0:T(8,128)(2,1)S(1)} %all-to-all-done.x_ref, bf16[1024,512]{1,0:T(8,128)(2,1)S(1)} %get-tuple-element.9.query_ref, bf16[1024,512]{1,0:T(8,128)(2,1)S(1)} %get-tuple-element.10.keys_ref, bf16[1024,3072]{1,0:T(8,128)(2,1)} %wqkv_hbm.1, bf16[1024,1024]{1,0:T(8,128)(2,1)} %wout_hbm.1, ...), custom_call_target="tpu_custom_call" | custom-call | flops 3221225472 | bytes 11534336 | tf_op jit(solution)/shard_map/temporal/pallas_call | solution.py:153
  32.5 0.0 collective-permute-done.2.refs_1_
  32.5 0.0 collective-permute-done.3.refs_2_
  32.5 1.4 %collective-permute-start.5 = (bf16[128,768]{1,0:T(8,128)(2,1)S(1)}, bf16[128,768]{1,0:T(8,128)(2,1)S(1)}, u32[]{:S(2)}, u32[]{:S(2)}) collective-permute-start(bf16[128,768]{1,0:T(8,128)(2,1)S(1)} %join.2.refs_0_), channel_id=1, source_target_pairs={{0,16},{8,24},{16,0},{24,8},{32,48},{40,56},{48,32},{56,40},{64,80... | collective-permute-start | bytes 589832 | tf_op jit(solution)/shard_map/ppermute | solution.py:313
  34.0 10.3 %all_to_all.15.parts_ref.after_ref = f32[8,8,128]{2,1,0:T(8,128)S(1)} all-to-all(f32[8,8,128]{2,1,0:T(8,128)S(1)} %temporal.1.after_ref), channel_id=1, replica_groups=mesh['wide'=32,'narrow'=8] {'narrow'}, dimensions={0} | all-to-all | bytes 65536 | tf_op jit(solution)/shard_map/all_to_all | solution.py:330
  44.3 0.1 collective-permute-start.6
  44.5 0.1 broadcast_in_dim.4.positive_ref
  44.5 0.8 %units.1 = (f32[4,896]{1,0:T(4,128)S(1)}, f32[4,128]{1,0:T(4,128)S(1)}, f32[16,4,896]{2,1,0:T(4,128)}) custom-call(f32[4,128]{1,0:T(4,128)S(1)} %broadcast_in_dim.4.positive_ref, f32[8,8,128]{2,1,0:T(8,128)S(1)} %all_to_all.15.parts_ref.after_ref), custom_call_target="tpu_custom_call" | custom-call | tf_op jit(solution)/shard_map/units/pallas_call | solution.py:233
  45.3 9.7 %all-to-all-start.2 = ((f32[16,4,896]{2,1,0:T(4,128)}), f32[16,4,896]{2,1,0:T(4,128)S(1)}, u32[]{:S(2)}, u32[]{:S(2)}) async-start(f32[16,4,896]{2,1,0:T(4,128)} %get-tuple-element.11), calls=%async_computation.2 | async-start | bytes 458752 | tf_op jit(solution)/shard_map/all_to_all | solution.py:335
  55.1 1.0 %clip_part.1 = f32[4,768]{1,0:T(4,128)S(1)} custom-call(f32[4,896]{1,0:T(4,128)S(1)} %get-tuple-element.12.unit_ref, bf16[128,768]{1,0:T(8,128)(2,1)S(1)} %join.2.refs_0_, bf16[128,768]{1,0:T(8,128)(2,1)S(1)} %collective-permute-done.5.refs_1_, bf16[256,768]{1,0:T(8,128)(2,1)S(1)} %collective-permute-done.6.refs_2_), custom_call_target="tpu_custom_call" | custom-call | flops 104857600 | bytes 1048576 | tf_op jit(solution)/shard_map/clip_part/pallas_call | solution.py:265
  56.1 1.2 %collective-permute-start.8 = (f32[4,768]{1,0:T(4,128)S(1)}, f32[4,768]{1,0:T(4,128)S(1)}, u32[]{:S(2)}, u32[]{:S(2)}) collective-permute-start(f32[4,768]{1,0:T(4,128)S(1)} %clip_part.1), channel_id=1, source_target_pairs={{0,2},{1,3},{2,0},{3,1},{4,6},{5,7},{6,4},{7,5},{8,10},{9,11},{10,... | collective-permute-start | bytes 36872 | tf_op jit(solution)/shard_map/ppermute | solution.py:313
  57.4 2.2 %collective-permute-start.9 = (f32[4,768]{1,0:T(4,128)S(1)}, f32[4,768]{1,0:T(4,128)S(1)}, u32[]{:S(2)}, u32[]{:S(2)}) collective-permute-start(f32[4,768]{1,0:T(4,128)S(1)} %clip_part.1), channel_id=1, source_target_pairs={{0,3},{1,2},{2,1},{3,0},{4,7},{5,6},{6,5},{7,4},{8,11},{9,10},{10,... | collective-permute-start | bytes 36872 | tf_op jit(solution)/shard_map/ppermute | solution.py:313
  59.5 0.2 collective-permute-start.7
  59.7 1.7 %collective-permute-done.8 = f32[4,768]{1,0:T(4,128)S(1)} collective-permute-done((f32[4,768]{1,0:T(4,128)S(1)}, f32[4,768]{1,0:T(4,128)S(1)}, u32[]{:S(2)}, u32[]{:S(2)}) %collective-permute-start.8) | collective-permute-done | bytes 12320 | tf_op jit(solution)/shard_map/ppermute | solution.py:313
  61.4 0.9 %collective-permute-done.9 = f32[4,768]{1,0:T(4,128)S(1)} collective-permute-done((f32[4,768]{1,0:T(4,128)S(1)}, f32[4,768]{1,0:T(4,128)S(1)}, u32[]{:S(2)}, u32[]{:S(2)}) %collective-permute-start.9) | collective-permute-done | bytes 12320 | tf_op jit(solution)/shard_map/ppermute | solution.py:313
  62.3 0.9 %collective-permute-done.7 = f32[4,768]{1,0:T(4,128)S(1)} collective-permute-done((f32[4,768]{1,0:T(4,128)S(1)}, f32[4,768]{1,0:T(4,128)S(1)}, u32[]{:S(2)}, u32[]{:S(2)}) %collective-permute-start.7) | collective-permute-done | bytes 12320 | tf_op jit(solution)/shard_map/ppermute | solution.py:313
  63.2 0.6 collective-permute-start.10
  63.9 2.0 %all-to-all-done.2.units_ref = f32[16,4,896]{2,1,0:T(4,128)S(1)} async-done(((f32[16,4,896]{2,1,0:T(4,128)}), f32[16,4,896]{2,1,0:T(4,128)S(1)}, u32[]{:S(2)}, u32[]{:S(2)}) %all-to-all-start.2) | async-done | bytes 229408 | tf_op jit(solution)/shard_map/all_to_all | solution.py:335
  65.8 0.5 caption_near.1.part_ref
  66.3 2.2 %collective-permute-done.10 = f32[4,768]{1,0:T(4,128)S(1)} collective-permute-done((f32[4,768]{1,0:T(4,128)S(1)}, f32[4,768]{1,0:T(4,128)S(1)}, u32[]{:S(2)}, u32[]{:S(2)}) %collective-permute-start.10) | collective-permute-done | bytes 12320 | tf_op jit(solution)/shard_map/ppermute | solution.py:313
  68.5 0.1 multiply_reduce_fusion
  68.6 0.1 copy.9.along_ref
  68.7 1.2 %gradients.1 = (f32[16,768]{1,0:T(8,128)}, f32[4,768]{1,0:T(4,128)}) custom-call(f32[16,4,896]{2,1,0:T(4,128)S(1)} %collective-permute-done.units_ref, f32[16,768]{1,0:T(8,128)S(1)} %caption_near.1.part_ref, bf16[16,768]{1,0:T(8,128)(2,1)S(1)} %copy-done, f32[4,768]{1,0:T(4,128)S(1)} %get-tuple-element.17.own_ref, f32[4,1]{1,0:T(4,128)S(1)} %copy.9.along_ref, ...), custom_call_target="tpu_custom_call" | custom-call | tf_op jit(solution)/shard_map/gradients/pallas_call | solution.py:344
  (15 shorter events, 0.1 us)
Async XLA Ops:
  0.6 8.4 %copy-start = (bf16[16,768]{1,0:T(8,128)(2,1)S(1)}, bf16[16,768]{1,0:T(8,128)(2,1)}, u32[]{:S(2)}) copy-start(bf16[16,768]{1,0:T(8,128)(2,1)} %cap_ref.3) | copy-start | bytes 73732
  2.9 23.2 %all-to-all-start = ((bf16[8,64,1024]{2,1,0:T(8,128)(2,1)}), bf16[8,64,1024]{2,1,0:T(8,128)(2,1)S(1)}, u32[]{:S(2)}, u32[]{:S(2)}) async-start(bf16[8,64,1024]{2,1,0:T(8,128)(2,1)} %bitcast.2), calls=%async_computation | async-start | bytes 2097152 | tf_op jit(solution)/shard_map/all_to_all | solution.py:322
  9.0 9.1 %collective-permute-start.1 = (bf16[16,768]{1,0:T(8,128)(2,1)S(1)}, bf16[16,768]{1,0:T(8,128)(2,1)S(1)}, u32[]{:S(2)}, u32[]{:S(2)}) collective-permute-start(bf16[16,768]{1,0:T(8,128)(2,1)S(1)} %copy-done), channel_id=1, source_target_pairs={{0,128},{8,136},{16,144},{24,152},{32,160},{40,168},{48,176},{56,1... | collective-permute-start | bytes 73736 | tf_op jit(solution)/shard_map/ppermute | solution.py:313
  18.1 14.4 %collective-permute-start.2 = (bf16[32,768]{1,0:T(8,128)(2,1)S(1)}, bf16[32,768]{1,0:T(8,128)(2,1)S(1)}, u32[]{:S(2)}, u32[]{:S(2)}) collective-permute-start(bf16[32,768]{1,0:T(8,128)(2,1)S(1)} %constant_dynamic-update-slice_fusion.refs_0_), channel_id=1, source_target_pairs={{0,32},{8,40},{16,48},{24,56},{32,0},{40,8},{48,16},{56,24},{64,96... | collective-permute-start | bytes 147464 | tf_op jit(solution)/shard_map/ppermute | solution.py:313
  19.1 13.4 %collective-permute-start.3 = (bf16[32,768]{1,0:T(8,128)(2,1)S(1)}, bf16[32,768]{1,0:T(8,128)(2,1)S(1)}, u32[]{:S(2)}, u32[]{:S(2)}) collective-permute-start(bf16[32,768]{1,0:T(8,128)(2,1)S(1)} %constant_dynamic-update-slice_fusion.refs_0_), channel_id=1, source_target_pairs={{0,64},{8,72},{16,80},{24,88},{32,96},{40,104},{48,112},{56,120},{... | collective-permute-start | bytes 147464 | tf_op jit(solution)/shard_map/ppermute | solution.py:313
  22.0 10.5 %collective-permute-start.4 = (bf16[32,768]{1,0:T(8,128)(2,1)S(1)}, bf16[32,768]{1,0:T(8,128)(2,1)S(1)}, u32[]{:S(2)}, u32[]{:S(2)}) collective-permute-start(bf16[32,768]{1,0:T(8,128)(2,1)S(1)} %constant_dynamic-update-slice_fusion.refs_0_), channel_id=1, source_target_pairs={{0,96},{8,104},{16,112},{24,120},{32,64},{40,72},{48,80},{56,88},{... | collective-permute-start | bytes 147464 | tf_op jit(solution)/shard_map/ppermute | solution.py:313
  26.2 18.3 %copy-start.1 = (s32[4]{0:T(128)S(1)}, s32[4]{0:T(128)}, u32[]{:S(2)}) copy-start(s32[4]{0:T(128)} %param.11) | copy-start | bytes 52
  32.5 11.8 %collective-permute-start.5 = (bf16[128,768]{1,0:T(8,128)(2,1)S(1)}, bf16[128,768]{1,0:T(8,128)(2,1)S(1)}, u32[]{:S(2)}, u32[]{:S(2)}) collective-permute-start(bf16[128,768]{1,0:T(8,128)(2,1)S(1)} %join.2.refs_0_), channel_id=1, source_target_pairs={{0,16},{8,24},{16,0},{24,8},{32,48},{40,56},{48,32},{56,40},{64,80... | collective-permute-start | bytes 589832 | tf_op jit(solution)/shard_map/ppermute | solution.py:313
  44.3 10.7 %collective-permute-start.6 = (bf16[256,768]{1,0:T(8,128)(2,1)S(1)}, bf16[256,768]{1,0:T(8,128)(2,1)S(1)}, u32[]{:S(2)}, u32[]{:S(2)}) collective-permute-start(bf16[256,768]{1,0:T(8,128)(2,1)S(1)} %join.3), channel_id=1, source_target_pairs={{0,8},{8,0},{16,24},{24,16},{32,40},{40,32},{48,56},{56,48},{64,72... | collective-permute-start | bytes 1179656 | tf_op jit(solution)/shard_map/ppermute | solution.py:313
  45.3 20.5 %all-to-all-start.2 = ((f32[16,4,896]{2,1,0:T(4,128)}), f32[16,4,896]{2,1,0:T(4,128)S(1)}, u32[]{:S(2)}, u32[]{:S(2)}) async-start(f32[16,4,896]{2,1,0:T(4,128)} %get-tuple-element.11), calls=%async_computation.2 | async-start | bytes 458752 | tf_op jit(solution)/shard_map/all_to_all | solution.py:335
  56.1 5.3 %collective-permute-start.8 = (f32[4,768]{1,0:T(4,128)S(1)}, f32[4,768]{1,0:T(4,128)S(1)}, u32[]{:S(2)}, u32[]{:S(2)}) collective-permute-start(f32[4,768]{1,0:T(4,128)S(1)} %clip_part.1), channel_id=1, source_target_pairs={{0,2},{1,3},{2,0},{3,1},{4,6},{5,7},{6,4},{7,5},{8,10},{9,11},{10,... | collective-permute-start | bytes 36872 | tf_op jit(solution)/shard_map/ppermute | solution.py:313
  57.4 4.9 %collective-permute-start.9 = (f32[4,768]{1,0:T(4,128)S(1)}, f32[4,768]{1,0:T(4,128)S(1)}, u32[]{:S(2)}, u32[]{:S(2)}) collective-permute-start(f32[4,768]{1,0:T(4,128)S(1)} %clip_part.1), channel_id=1, source_target_pairs={{0,3},{1,2},{2,1},{3,0},{4,7},{5,6},{6,5},{7,4},{8,11},{9,10},{10,... | collective-permute-start | bytes 36872 | tf_op jit(solution)/shard_map/ppermute | solution.py:313
  59.5 3.7 %collective-permute-start.7 = (f32[4,768]{1,0:T(4,128)S(1)}, f32[4,768]{1,0:T(4,128)S(1)}, u32[]{:S(2)}, u32[]{:S(2)}) collective-permute-start(f32[4,768]{1,0:T(4,128)S(1)} %clip_part.1), channel_id=1, source_target_pairs={{0,1},{1,0},{2,3},{3,2},{4,5},{5,4},{6,7},{7,6},{8,9},{9,8},{10,11... | collective-permute-start | bytes 36872 | tf_op jit(solution)/shard_map/ppermute | solution.py:313
  63.2 5.3 %collective-permute-start.10 = (f32[4,768]{1,0:T(4,128)S(1)}, f32[4,768]{1,0:T(4,128)S(1)}, u32[]{:S(2)}, u32[]{:S(2)}) collective-permute-start(f32[4,768]{1,0:T(4,128)S(1)} %add_add_fusion), channel_id=1, source_target_pairs={{0,4},{1,5},{2,6},{3,7},{4,0},{5,1},{6,2},{7,3},{8,12},{9,13},{10,... | collective-permute-start | bytes 36872 | tf_op jit(solution)/shard_map/ppermute | solution.py:313
  65.8 2.9 %collective-permute-start = (f32[16,4,896]{2,1,0:T(4,128)S(1)}, f32[16,4,896]{2,1,0:T(4,128)S(1)}, u32[]{:S(2)}, u32[]{:S(2)}) collective-permute-start(f32[16,4,896]{2,1,0:T(4,128)S(1)} %all-to-all-done.2.units_ref), channel_id=1, source_target_pairs={{0,8},{8,0},{16,24},{24,16},{32,40},{40,32},{48,56},{56,48},{64,72... | collective-permute-start | bytes 688136 | tf_op jit(solution)/shard_map/ppermute | solution.py:313
